TPU v7x, 128 devices: a whole 4x4x4 slice. The times are simulated.
128 devices in a mesh: batch: 8 (over y, core), blk: 16 (over x, z).
Axes of the slice: x: 4, y: 4, z: 4, core: 2. Of those that a mesh axis runs over, the one named last changes fastest.
Arguments:
- inputs: bfloat16 [8, 2048, 768], P('batch', 'blk'), may hold values from -6 to 6
- queries: bfloat16 [8, 2048, 768], P('batch', 'blk'), may hold values from -6 to 6
- lengths: int32 [8], P('batch'), may hold values from 1921 to 2048, as said below
- latent_array: bfloat16 [256, 1280], P('blk'), may hold values from -6 to 6
- latent_mats: bfloat16 [10, 1280, 1280], P(None, 'blk'), may hold values from -0.15625 to 0.15625
- out_mats: bfloat16 [2, 1280, 1280], P(None, 'blk'), may hold values from -0.75 to 0.75
- byte_mats: bfloat16 [3, 768, 1280], P(None, 'blk'), may hold values from -0.21875 to 0.21875
- dec_out: bfloat16 [1280, 768], P('blk'), may hold values from -0.75 to 0.75
- latent_gains: float32 [5, 1280], replicated, may hold values from 0.5 to 1.5
- byte_gains: float32 [2, 768], replicated, may hold values from 0.5 to 1.5
- cotangent: bfloat16 [8, 2048, 768], P('batch', 'blk'), may hold values from -6 to 6
Outputs:
- result: bfloat16 [8, 2048, 768], P('batch', 'blk')
- grad_inputs: float32 [8, 2048, 768], P('batch', 'blk')
- grad_queries: float32 [8, 2048, 768], P('batch', 'blk')
- grad_latent_array: float32 [256, 1280], P('batch', 'blk')
- grad_latent_mats: float32 [10, 1280, 1280], P(None, 'batch', 'blk')
- grad_out_mats: float32 [2, 1280, 1280], P(None, 'batch', 'blk')
- grad_byte_mats: float32 [3, 768, 1280], P(None, 'batch', 'blk')
- grad_dec_out: float32 [1280, 768], P('batch', 'blk')
- grad_latent_gains: float32 [5, 1280], replicated
- grad_byte_gains: float32 [2, 768], replicated
Inputs may be any that keep to these rules, and one draw needn't show every extreme that they name: `lengths`: byte positions at or past a sequence's length are padding whose keys are masked; every draw has a sequence of length 2048.
All inputs are finite; a program needn't handle non-finite values.
Results may differ from a plain program's by a relative error of at most 0.025.
Values may be sent and summed in bfloat16 or wider, within the bound.
No kernel may reach another device: no remote copies, remote signals or barrier semaphores. Data moves between devices by JAX's collectives and lax.ppermute only.
A program may use at most 256 MiB of HBM per device.

v0:
```python
import jax
import jax.numpy as jnp
from jax import lax
from jax.experimental import pallas as pl
from jax.experimental.pallas import tpu as pltpu
from jax.sharding import Mesh, PartitionSpec as P

F32, BF = jnp.float32, jnp.bfloat16
D, DI, R, N, H, E = 1280, 768, 256, 128, 8, 160
NX, NZ, NJ, NI = 4, 4, 16, 8
SCALE = E**-0.5
EPS = 1e-5
MIB = 1 << 20
AXES = ("y", "core", "x", "z")
BATCH = ("y", "core")
BLK = ("x", "z")
WIN = [128 * (E * h // 128) for h in range(H)]
OFF = [E * h - WIN[h] for h in range(H)]
SQUARE = [("o", 0), ("l", 1), ("l", 2), ("l", 3), ("l", 4), ("l", 5), ("o", 1), ("l", 6), ("l", 7), ("l", 8), ("l", 9)]
ROWS_I = 128
DEC_ROW, BQ_ROW = 880, 960
PLACE = {9: (0, 0), 10: (0, 80), 8: (0, 160), 3: (1, 0), 4: (1, 80), 5: (1, 160), 7: (2, 0), 6: (2, 80), 2: (2, 160), 1: (3, 0), 0: (3, 80)}


def dot(a, b, ca=1, cb=0):
    return lax.dot_general(a, b, (((ca,), (cb,)), ((), ())), preferred_element_type=F32)


def dot_nt(a, b):
    return dot(a, b, 1, 1)


def dot_tn(a, b):
    return dot(a, b, 0, 0)


def half(v):
    return v.astype(BF)


def norm(v):
    c = v - jnp.mean(v, axis=-1, keepdims=True)
    inv = lax.rsqrt(jnp.mean(c * c, axis=-1, keepdims=True) + EPS)
    return c * inv, inv


def norm_back(g, gain, n, inv):
    gg = jnp.sum(g * n, axis=0, keepdims=True)
    inner = g * gain
    m1 = jnp.mean(inner, axis=-1, keepdims=True)
    m2 = jnp.mean(inner * n, axis=-1, keepdims=True)
    return inv * (inner - m1 - n * m2), gg


C0, C1 = 0.7978845608028654, 0.044715


def gelu(x):
    return 0.5 * x * (1.0 + jnp.tanh(C0 * (x + C1 * x * x * x)))


def gelu_slope(x):
    t = jnp.tanh(C0 * (x + C1 * x * x * x))
    return 0.5 * (1.0 + t) + 0.5 * x * (1.0 - t * t) * (C0 * (1.0 + 3.0 * C1 * x * x))


def lanes(width):
    return lax.broadcasted_iota(jnp.int32, (1, width), 1)


def head_mask(h):
    lane = lanes(256)
    return jnp.where((lane >= OFF[h]) & (lane < OFF[h] + E), 1.0, 0.0).astype(F32)


def pieces(row, count):
    out = []
    done = 0
    while done < count:
        i, r0 = divmod(row + done, ROWS_I)
        n = min(count - done, ROWS_I - r0)
        out.append((i, r0, done, n))
        done += n
    return out


def split3(v):
    hi = half(v).astype(F32)
    mid = half(v - hi).astype(F32)
    lo = half(v - hi - mid).astype(F32)
    return hi, mid, lo


def pack3(v):
    hi, mid, lo = split3(v)
    return half(hi + pltpu.roll(mid, 16, 1) + pltpu.roll(lo, 32, 1))


def unpack3(v, axis):
    return v + pltpu.roll(v, 112, axis) + pltpu.roll(v, 96, axis)


def as_rows(parts, count):
    row = lax.broadcasted_iota(jnp.int32, (count, 128), 0)
    out = jnp.zeros((count, 128), F32)
    for r, part in parts:
        out = jnp.where(row == r, part, out)
    return out


def call(body, outs, args, scratch=(), vmem=48, flops=0, name=None):
    spaces = {"v": pltpu.VMEM, "a": pl.ANY, "s": pltpu.SMEM, "h": pltpu.HBM}
    return pl.pallas_call(
        body,
        out_shape=[jax.ShapeDtypeStruct(s, t) for s, t, _ in outs],
        in_specs=[pl.BlockSpec(memory_space=spaces[m]) for _, m in args],
        out_specs=[pl.BlockSpec(memory_space=spaces[m]) for _, _, m in outs],
        scratch_shapes=list(scratch),
        compiler_params=pltpu.CompilerParams(vmem_limit_bytes=vmem * MIB),
        cost_estimate=pl.CostEstimate(flops=int(flops), bytes_accessed=4 * MIB, transcendentals=0),
        name=name,
    )(*[a for a, _ in args])


DMA = pltpu.SemaphoreType.DMA


def pack_body(sc, lm, om, bm, do, la, g0, wsh, sem):
    i, core = sc[0], sc[4]
    cols = pl.ds(pl.multiple_of(core * 640, 128), 640)
    first = [
        (bm.at[0, :, cols], g0.at[0:48, :]),
        (bm.at[1, :, cols], g0.at[48:96, :]),
        (lm.at[0, :, cols], g0.at[96:176, :]),
        (la.at[:, cols], g0.at[176:192, :]),
    ]
    first = [pltpu.make_async_copy(a, b, sem.at[8 + k]) for k, (a, b) in enumerate(first)]
    for c in first:
        c.start()
    blocks = [(80 * k, 80, (om if s == "o" else lm), n, D) for k, (s, n) in enumerate(SQUARE)]
    blocks += [(DEC_ROW, 80, do, None, DI), (BQ_ROW, 48, bm, 2, D)]
    for k in range(NI):
        lo, hi = ROWS_I * k, ROWS_I * (k + 1)

        @pl.when(i == k)
        def _(lo=lo, hi=hi):
            cs = []
            for row, count, ref, n, width in blocks:
                a, b = max(lo, row), min(hi, row + count)
                if a < b:
                    src = ref.at[a - row : b - row, :] if n is None else ref.at[n, a - row : b - row, :]
                    dst = wsh.at[a - lo : b - lo, :] if width == D else wsh.at[a - lo : b - lo, 0:width]
                    cs.append(pltpu.make_async_copy(src, dst, sem.at[len(cs)]))
            for c in cs:
                c.start()
            for c in cs:
                c.wait()

    for c in first:
        c.wait()


def pieces_from(sc, groups):
    x, z, core = sc[2], sc[3], sc[4]
    out = []
    for side in range(2):
        c = core if side == 0 else 1 - core
        col = pl.ds(pl.multiple_of(c * 640, 128), 640)
        for e in range(4):
            for d in range(4):
                xs = jnp.where(c == 0, (x + 4 - d) & 3, (x + 4 - e) & 3)
                zs = jnp.where(c == 0, (z + 4 - e) & 3, (z + 4 - d) & 3)
                out.append((xs * 4 + zs, col, groups[4 * side + e].at[d]))
    return out


def enc_body(sc, t0, t1, t2, t3, u0, u1, u2, u3, x_in, bg, lg, g_out, nb_o, k_o, v_o, q_o, pay, gs, acc, sem):
    copies = [
        pltpu.make_async_copy(src, gs.at[pos, :, col], sem.at[k])
        for k, (pos, col, src) in enumerate(pieces_from(sc, (t0, t1, t2, t3, u0, u1, u2, u3)))
    ]
    for c in copies:
        c.start()
    n_in, _ = norm(x_in[...].astype(F32))
    nb = half(n_in * bg[0:1, :])
    nb_o[...] = nb
    for c in copies:
        c.wait()
    save = pltpu.make_async_copy(gs, g_out, sem.at[32])
    save.start()
    k_o[...] = half(dot(nb, gs[:, 0:48, :].reshape(DI, D)))
    v_o[...] = half(dot(nb, gs[:, 48:96, :].reshape(DI, D)))
    z0b = gs[:, 176:192, :].reshape(R, D)
    nq, _ = norm(z0b.astype(F32))
    q_o[...] = half(dot(half(nq * lg[0:1, :]), gs[:, 96:176, :].reshape(D, D)))
    acc[...] = jnp.zeros_like(acc)
    valid = lanes(N) + sc[1] * N < sc[5]
    lane = lanes(128)
    stats = jnp.zeros((R, 128), F32)
    for h in range(H):
        w = slice(WIN[h], WIN[h] + 256)
        mk = head_mask(h)
        s = dot_nt(q_o[:, w] * half(mk), k_o[:, w]) * SCALE
        s = jnp.where(valid, s, -1e30)
        m = jnp.max(s, axis=-1, keepdims=True)
        p = jnp.exp(s - m)
        acc[:, w] += dot(half(p), v_o[:, w]) * mk
        stats = jnp.where(lane == h, m, stats)
        stats = jnp.where(lane == 8 + h, jnp.sum(p, axis=-1, keepdims=True), stats)
    pay[:, 0:D] = half(acc[...])
    pay[:, D : D + 128] = pack3(stats)
    save.wait()


def combine_body(rcv, out):
    st = unpack3(rcv[:, :, D : D + 128].astype(F32), 2)
    peak = jnp.max(st, axis=0, keepdims=True)
    w = jnp.exp(st - peak)
    total = jnp.sum(w * pltpu.roll(st, 120, 2), axis=0, keepdims=True)
    coef = w / total
    lane = lax.broadcasted_iota(jnp.int32, (1, 1, 128), 2)
    for t in range(10):
        h0, h1 = 128 * t // E, (128 * t + 127) // E
        c = coef[:, :, h0 : h0 + 1]
        if h1 != h0:
            c = jnp.where(lane >= E * h1 - 128 * t, coef[:, :, h1 : h1 + 1], c)
        o = jnp.sum(rcv[:, :, 128 * t : 128 * t + 128].astype(F32) * c, axis=0)
        out[:, 128 * t : 128 * t + 128] = half(o)
    lse = jnp.where(lanes(128) < 8, (peak + jnp.log(total))[0], 0.0)
    out[:, D : D + 128] = pack3(lse)


class Ring:
    def __init__(self, w, slots, sem, order):
        self.w, self.slots, self.sem, self.order = w, slots, sem, order
        self.n = slots.shape[0]
        self.pos = {m: k for k, m in enumerate(order)}

    def copies(self, m):
        s = self.pos[m] % self.n
        return [
            pltpu.make_async_copy(
                self.w.at[i, :, r0 : r0 + n, :], self.slots.at[s, :, d0 : d0 + n, :], self.sem.at[s, k]
            )
            for k, (i, r0, d0, n) in enumerate(pieces(80 * m, 80))
        ]

    def start(self, m):
        for c in self.copies(m):
            c.start()

    def begin(self):
        for m in self.order[: self.n]:
            self.start(m)

    def get(self, m):
        for c in self.copies(m):
            c.wait()
        return self.slots[self.pos[m] % self.n].reshape(D, D)

    def done(self, m):
        k = self.pos[m] + self.n
        if k < len(self.order):
            self.start(self.order[k])


def forward_body(
    qin, cot, bg, lg, e_h, g_all, w,
    res, gqin, gain_o, pay, mix_o, nd_o, gq_o, z_h, h_h, a_h,
    slots, e, z0b, zs, hs, qs, acc, kd, vd, dec, bq, dacc, gq, gkv, wsem, ssem, lsem,
):
    first = [
        pltpu.make_async_copy(e_h.at[:, 0:D], e, lsem.at[3]),
        pltpu.make_async_copy(g_all.at[:, 176:192, :], z0b, lsem.at[4]),
    ]
    for c in first:
        c.start()
    ring = Ring(w, slots, wsem, list(range(11)))
    ring.begin()
    copies = []
    for i, r0, d0, n in pieces(BQ_ROW, 48):
        copies.append(pltpu.make_async_copy(w.at[i, :, r0 : r0 + n, :], bq.at[:, d0 : d0 + n, :], lsem.at[0]))
    for i, r0, d0, n in pieces(DEC_ROW, 80):
        copies.append(
            pltpu.make_async_copy(w.at[i, :, r0 : r0 + n, 0:DI], dec.at[:, d0 : d0 + n, :], lsem.at[len(copies)])
        )
    for c in copies:
        c.start()
    saves = []

    def save(src, dst):
        c = pltpu.make_async_copy(src, dst, ssem.at[len(saves)])
        c.start()
        saves.append(c)

    def mul(a, m):
        out = dot(a, ring.get(m))
        ring.done(m)
        return out

    for c in first:
        c.wait()
    z1 = z0b[...].reshape(R, D).astype(F32) + mul(e[...], 0)
    zs[0] = z1
    save(zs.at[0], z_h.at[0])
    h1 = mul(half(norm(z1)[0] * lg[1:2, :]), 1)
    hs[0] = h1
    save(hs.at[0], h_h.at[0])
    zs[1] = zs[0] + mul(half(gelu(h1)), 2)
    save(zs.at[1], z_h.at[1])
    s_b = half(norm(zs[1])[0] * lg[2:3, :])
    for k in range(3):
        qs[k] = half(mul(s_b, 3 + k))
        save(qs.at[k], a_h.at[k])
    acc[...] = jnp.zeros_like(acc)
    for h in range(H):
        win = slice(WIN[h], WIN[h] + 256)
        mk = head_mask(h)
        s = dot_nt(qs[0, :, win] * half(mk), qs[1, :, win]) * SCALE
        p = jnp.exp(s - jnp.max(s, axis=-1, keepdims=True))
        p = p / jnp.sum(p, axis=-1, keepdims=True)
        acc[:, win] += dot(half(p), qs[2, :, win]) * mk
    qs[3] = half(acc[...])
    save(qs.at[3], a_h.at[3])
    zs[2] = zs[1] + mul(qs[3], 6)
    save(zs.at[2], z_h.at[2])
    h2 = mul(half(norm(zs[2])[0] * lg[3:4, :]), 7)
    hs[1] = h2
    save(hs.at[1], h_h.at[1])
    zs[3] = zs[2] + mul(half(gelu(h2)), 8)
    save(zs.at[3], z_h.at[3])
    c_b = half(norm(zs[3])[0] * lg[4:5, :])
    kd[...] = half(mul(c_b, 9))
    vd[...] = half(mul(c_b, 10))

    x = qin[...].astype(F32)
    n, inv = norm(x)
    nd = half(n * bg[1:2, :])
    nd_o[...] = nd
    for c in copies:
        c.wait()
    wq = bq[...].reshape(DI, D)
    wd = dec[...].reshape(D, DI)
    gq_o[...] = half(dot(nd, wq))
    mix_o[...] = half(dot_nt(cot[...], wd))
    dacc[...] = jnp.zeros_like(dacc)
    gq[...] = jnp.zeros_like(gq)
    gkv[...] = jnp.zeros_like(gkv)
    for h in range(H):
        win = slice(WIN[h], WIN[h] + 256)
        mk = head_mask(h)
        mkb = half(mk)
        qw, gw, kw, vw = gq_o[:, win], mix_o[:, win], kd[:, win], vd[:, win]
        s = dot_nt(qw * mkb, kw) * SCALE
        p = jnp.exp(s - jnp.max(s, axis=-1, keepdims=True))
        p = p / jnp.sum(p, axis=-1, keepdims=True)
        pb = half(p)
        dacc[:, win] += dot(pb, vw) * mk
        dp = dot_nt(gw * mkb, vw)
        ds = half(p * (dp - jnp.sum(p * dp, axis=-1, keepdims=True)))
        gq[:, win] += dot(ds, kw) * mk
        gkv[0, :, win] += dot_tn(ds, qw) * mk
        gkv[1, :, win] += dot_tn(pb, gw) * mk
    pay[:, 0:D] = half(gkv[0] * SCALE)
    pay[:, D : 2 * D] = half(gkv[1])
    mix = half(dacc[...])
    mix_o[...] = mix
    res[...] = half(x + dot(mix, wd))
    gqb = half(gq[...] * SCALE)
    gq_o[...] = gqb
    gin, gg = norm_back(dot_nt(gqb, wq), bg[1:2, :], n, inv)
    gqin[...] = cot[...].astype(F32) + gin
    gain_o[...] = gg
    for c in saves:
        c.wait()


def prepare_body(lg, z_h, h_h, a_h, n_h, i_h, s_h, act_h, p_h, zs, hs, qs, ns, vs, ss, acts, ps, sem, osem):
    loads = {}
    for k in range(4):
        loads["z", k] = pltpu.make_async_copy(z_h.at[k], zs.at[k], sem.at[k])
    for k in range(2):
        loads["h", k] = pltpu.make_async_copy(h_h.at[k], hs.at[k], sem.at[4 + k])
    loads["q"] = pltpu.make_async_copy(a_h.at[0:2], qs, sem.at[6])
    for c in loads.values():
        c.start()
    saves = []

    def save(src, dst):
        c = pltpu.make_async_copy(src, dst, osem.at[len(saves)])
        c.start()
        saves.append(c)

    for k, a in ((3, 0), (2, 2), (1, 1), (0, 4)):
        loads["z", k].wait()
        n, inv = norm(zs[k])
        ns[k] = n
        save(ns.at[k], n_h.at[k])
        vs[k] = jnp.broadcast_to(inv, (R, 128))
        acts[a] = half(n * lg[k + 1 : k + 2, :])
        save(acts.at[a], act_h.at[a])
    save(vs, i_h)
    for k, a in ((1, 3), (0, 5)):
        loads["h", k].wait()
        x = hs[k]
        t = jnp.tanh(C0 * (x + C1 * x * x * x))
        acts[a] = half(0.5 * x * (1.0 + t))
        save(acts.at[a], act_h.at[a])
        ss[k] = 0.5 * (1.0 + t) + 0.5 * x * (1.0 - t * t) * (C0 * (1.0 + 3.0 * C1 * x * x))
        save(ss.at[k], s_h.at[k])
    loads["q"].wait()
    for h in range(H):
        win = slice(WIN[h], WIN[h] + 256)
        s = dot_nt(qs[0, :, win] * half(head_mask(h)), qs[1, :, win]) * SCALE
        p = jnp.exp(s - jnp.max(s, axis=-1, keepdims=True))
        ps[h] = p / jnp.sum(p, axis=-1, keepdims=True)
    save(ps, p_h)
    for c in saves:
        c.wait()


def lat_backward_body(
    sc, gkv, lg, w, e_h, n_h, i_h, s_h, act_h, a_h, p_h, gmix, pack_o, g1c_o, gains_o,
    slots, ns, vs, ss, acts, qs, ps, acc, acc2, acc3, gh, gw, wsem, lsem,
):
    order = [9, 10, 8, 7, 6, 3, 4, 5, 2, 1, 0]
    ring = Ring(w, slots, wsem, order)
    todo = [
        (n_h.at[3], ns.at[3]),
        (i_h, vs),
        (act_h.at[0], acts.at[0]),
        (s_h.at[1], ss.at[1]),
        (act_h.at[3], acts.at[1]),
        (n_h.at[2], ns.at[2]),
        (act_h.at[2], acts.at[3]),
        (a_h.at[3], acts.at[4]),
        (p_h, ps),
        (a_h.at[0:3], qs.at[0:3]),
        (n_h.at[1], ns.at[1]),
        (act_h.at[1], acts.at[2]),
        (s_h.at[0], ss.at[0]),
        (act_h.at[5], acts.at[5]),
        (n_h.at[0], ns.at[0]),
        (act_h.at[4], acts.at[6]),
        (e_h.at[:, 0:D], acts.at[7]),
    ]
    loads = [pltpu.make_async_copy(a, b, lsem.at[k]) for k, (a, b) in enumerate(todo)]
    for c in loads[:2]:
        c.start()
    ring.start(order[0])
    ring.start(order[1])
    for c in loads[2:6]:
        c.start()
    for m in order[2 : ring.n]:
        ring.start(m)
    for c in loads[6:]:
        c.start()

    def ready(*ks):
        for k in ks:
            loads[k].wait()

    src = sc[1] * 80
    start = pl.multiple_of(jnp.minimum((src >> 7) * 128, 1024), 128)
    offset = src - start
    lane = lanes(256)

    def put(ref, to):
        v = pltpu.roll(ref[:, pl.ds(start, 256)].astype(F32), (to - offset + 256) & 255, 1)
        return jnp.where((lane >= to) & (lane < to + 80), v, 0.0)

    def weight_grad(window, first, count):
        a = acts[first : first + count].reshape(count * R, D)
        pack_o[:, 256 * window : 256 * window + 256] = half(dot_tn(a, gw[first : first + count].reshape(count * R, 256)))

    def mul(g_b, m):
        out = dot_nt(g_b, ring.get(m))
        ring.done(m)
        return out

    gain_rows = []

    def back(g, k):
        out, gg = norm_back(g, lg[k + 1 : k + 2, :], ns[k], vs[k][:, 0:1])
        for t in range(10):
            gain_rows.append((10 * k + t, gg[:, 128 * t : 128 * t + 128]))
        return out

    ready(0, 1)
    gn = mul(gkv[:, 0:D], 9) + mul(gkv[:, D : 2 * D], 10)
    acc[...] = back(gn, 3)
    gw[0] = half(put(gkv.at[:, 0:D], 0) + put(gkv.at[:, D : 2 * D], 80))
    gw[1] = half(put(acc, 160))
    ready(2, 3, 4)
    gh[...] = half(mul(half(acc[...]), 8) * ss[1])
    weight_grad(0, 0, 2)
    ready(5)
    gw[3] = half(put(gh, 0))
    acc[...] += back(mul(gh[...], 7), 2)
    gw[4] = half(put(acc, 80))
    qs[3] = half(mul(half(acc[...]), 6))
    acc2[...] = jnp.zeros_like(acc2)
    acc3[...] = jnp.zeros_like(acc3)
    ready(6, 7, 8, 9)
    for h in range(H):
        win = slice(WIN[h], WIN[h] + 256)
        mk = head_mask(h)
        p = ps[h]
        dp = dot_nt(qs[3, :, win] * half(mk), qs[2, :, win])
        ds = half(p * (dp - jnp.sum(p * dp, axis=-1, keepdims=True)) * SCALE)
        acc2[:, win] += dot(ds, qs[1, :, win]) * mk
        acc3[0, :, win] += dot_tn(ds, qs[0, :, win]) * mk
        acc3[1, :, win] += dot_tn(half(p), qs[3, :, win]) * mk
    gw[2] = half(put(acc2, 0) + put(acc3.at[0], 80) + put(acc3.at[1], 160))
    gn = mul(half(acc2[...]), 3)
    gn = gn + mul(half(acc3[0]), 4)
    gn = gn + mul(half(acc3[1]), 5)
    ready(10, 11)
    weight_grad(1, 2, 1)
    acc[...] += back(gn, 1)
    gw[5] = half(put(acc, 160))
    ready(12, 13)
    gh[...] = half(mul(half(acc[...]), 2) * ss[0])
    weight_grad(2, 3, 3)
    gw[6] = half(put(gh, 0))
    ready(14, 15, 16)
    acc[...] += back(mul(gh[...], 1), 0)
    gw[7] = half(put(acc, 80))
    g1c_o[...] = half(put(acc, 0)[:, 0:128])
    gmix[...] = half(mul(half(acc[...]), 0))
    weight_grad(3, 6, 2)
    gains_o[...] = as_rows(gain_rows, 48)


def sum_rows_body(rcv, out):
    s = half(jnp.sum(rcv[...].astype(F32), axis=0))
    for k in range(NJ):
        out[k] = s


def dec_weights_body(mix, cot, nd, gq, out, buf, sem):
    g = half(dot_tn(mix[...], cot[...]))
    for i in range(NI):
        for t in range(6):
            buf[i, 160 * t : 160 * t + 160, :] = g[160 * i : 160 * i + 160, 128 * t : 128 * t + 128]
    one = pltpu.make_async_copy(buf.at[:, 0:960, :], out.at[:, 0:960, :], sem.at[0])
    one.start()
    g = half(dot_tn(nd[...], gq[...]))
    for i in range(NI):
        for t in range(10):
            r = 960 + 96 * t
            buf[i, r : r + 96, :] = g[96 * i : 96 * i + 96, 128 * t : 128 * t + 128]
    two = pltpu.make_async_copy(buf.at[:, 960:1920, :], out.at[:, 960:1920, :], sem.at[1])
    two.start()
    one.wait()
    two.wait()


def spread(chunk, pay, td, tb):
    fill = jnp.zeros((96, 128), F32)
    for t in range(6):
        v = jnp.concatenate([chunk[160 * t : 160 * t + 160, :].astype(F32), fill], axis=0)
        td[128 * t : 128 * t + 128, :] = v.T
    fill = jnp.zeros((32, 128), F32)
    for t in range(10):
        v = jnp.concatenate([chunk[960 + 96 * t : 960 + 96 * t + 96, :].astype(F32), fill], axis=0)
        tb[128 * t : 128 * t + 128, :] = v.T
    for j in range(NJ):
        pay[j, 512:560, :] = half(td[48 * j : 48 * j + 48, 0:128])
        pay[j, 560:608, :] = half(td[48 * j : 48 * j + 48, 128:256])
        pay[j, 608:688, :] = half(tb[80 * j : 80 * j + 80, :])


def unspread(s, dec_o, bq_o):
    fill = jnp.zeros((80, 128), F32)
    a = jnp.concatenate([s[0:48], fill], axis=0).T
    b = jnp.concatenate([s[48:96], fill], axis=0).T
    dec_o[0:128, :] = a[:, 0:48]
    dec_o[128:160, :] = b[0:32, 0:48]
    c = jnp.concatenate([s[96:176], fill[0:48]], axis=0).T
    bq_o[...] = c[0:96, 0:80]


def enc_back_body(
    sc, x_in, bg, lg, gd, gmix_h, e_h, q_h, k_h, v_h, g_all, dw_h, gin_o, pay,
    gmix, e, q, k, v, wkv, gq, gkt, gvt, dw, td, tb, sem,
):
    pairs = [(gmix_h, gmix), (q_h, q), (k_h, k), (v_h, v), (e_h, e), (g_all, wkv), (dw_h, dw)]
    loads = [pltpu.make_async_copy(a, b, sem.at[n]) for n, (a, b) in enumerate(pairs)]
    for c in loads:
        c.start()
    for c in loads[:5]:
        c.wait()
    lse = unpack3(e[:, D : D + 128].astype(F32), 1)
    valid = lanes(N) + sc[1] * N < sc[5]
    gq[...] = jnp.zeros_like(gq)
    for h in range(H):
        win = slice(WIN[h], WIN[h] + 256)
        mk = head_mask(h)
        mkb = half(mk)
        qw, gw, kw, vw = q[:, win], gmix[:, win], k[:, win], v[:, win]
        rd = jnp.sum(gw.astype(F32) * e[:, win].astype(F32) * mk, axis=-1, keepdims=True)
        s = dot_nt(qw * mkb, kw) * SCALE
        p = jnp.where(valid, jnp.exp(jnp.where(valid, s, -1e30) - lse[:, h : h + 1]), 0.0)
        dp = dot_nt(gw * mkb, vw)
        ds = half(p * (dp - rd))
        gq[:, win] += dot(ds, kw) * mk
        o = OFF[h]
        gkt[E * h : E * h + E, :] = half(dot_tn(qw, ds)[o : o + E, :] * SCALE)
        gvt[E * h : E * h + E, :] = half(dot_tn(gw, half(p))[o : o + E, :])
    pay[:, 320:400, :] = gkt[...].reshape(NJ, 80, 128)
    pay[:, 400:480, :] = gvt[...].reshape(NJ, 80, 128)
    loads[5].wait()
    gqs = gq[...] * SCALE
    gqt = half(gqs.T)
    pay[:, 160:240, :] = gqt[:, 0:128].reshape(NJ, 80, 128)
    pay[:, 240:320, :] = gqt[:, 128:256].reshape(NJ, 80, 128)
    n, inv = norm(wkv[:, 176:192, :].reshape(R, D).astype(F32))
    gz, g0 = norm_back(dot_nt(half(gqs), wkv[:, 96:176, :].reshape(D, D)), lg[0:1, :], n, inv)
    gzt = half(gz.T)
    pay[:, 0:80, :] = gzt[:, 0:128].reshape(NJ, 80, 128)
    pay[:, 80:160, :] = gzt[:, 128:256].reshape(NJ, 80, 128)
    n, inv = norm(x_in[...].astype(F32))
    gnt = dot(wkv[:, 0:48, :].reshape(DI, D), gkt[...]) + dot(wkv[:, 48:96, :].reshape(DI, D), gvt[...])
    gin, gg = norm_back(gnt.T, bg[0:1, :], n, inv)
    gin_o[...] = gin
    rows = [(t, gg[:, 128 * t : 128 * t + 128]) for t in range(6)]
    rows += [(6 + t, gd[:, 128 * t : 128 * t + 128]) for t in range(6)]
    rows += [(16 + t, g0[:, 128 * t : 128 * t + 128]) for t in range(10)]
    g = half(as_rows(rows, 32))
    for j in range(NJ):
        pay[j, 480:512, :] = g
    loads[6].wait()
    spread(dw, pay, td, tb)


def tail_one_body(rcv, nf_h, g_all, lg, lat_gain, g1c, out, dec_o, bq_o, nf, z0b, left, sem):
    loads = [
        pltpu.make_async_copy(nf_h, nf, sem.at[0]),
        pltpu.make_async_copy(g_all.at[:, 176:192, :], z0b, sem.at[1]),
    ]
    for c in loads:
        c.start()
    sums = jnp.sum(rcv[:, 0:320, :].astype(F32), axis=0)
    fill = jnp.zeros((48, 128), F32)
    left[...] = jnp.zeros_like(left)
    for s in range(NJ):
        left[0:80, 128 * s : 128 * s + 128] = rcv[s, 320:400, :]
        left[128:208, 128 * s : 128 * s + 128] = rcv[s, 400:480, :]
    loads[1].wait()
    nq = half(norm(z0b[...].reshape(R, D).astype(F32))[0] * lg[0:1, :])
    a = jnp.concatenate([sums[160:240], fill], axis=0).T
    b = jnp.concatenate([sums[240:320], fill], axis=0).T
    w0 = half(dot_tn(nq, half(jnp.concatenate([a, b], axis=0))))
    a = jnp.concatenate([sums[0:80], fill], axis=0).T
    b = jnp.concatenate([sums[80:160], fill], axis=0).T
    gz = half(jnp.concatenate([a, b], axis=0) + g1c[...].astype(F32))
    gains = jnp.sum(rcv[:, 480:512, :].astype(F32), axis=0)
    gains = half(jnp.concatenate([gains, lat_gain[...]], axis=0))
    loads[0].wait()
    wt = half(dot(left[...], nf[...]).T)
    for i in range(NI):
        out[i, 0:160, :] = w0[160 * i : 160 * i + 160, :]
        out[i, 160:192, :] = gz[32 * i : 32 * i + 32, :]
        out[i, 192:288, :] = wt[96 * i : 96 * i + 96, 0:128]
        out[i, 288:384, :] = wt[96 * i : 96 * i + 96, 128:256]
        out[i, 384:464, :] = gains
    unspread(jnp.sum(rcv[:, 512:688, :].astype(F32), axis=0), dec_o, bq_o)


def tail_two_body(rcv, pack, arr_o, lm_o, om_o, wkv_o, lat_o, byte_o):
    sums = jnp.sum(rcv[...].astype(F32), axis=0)
    lm_o[0] = sums[0:160, 0:80]
    arr_o[...] = sums[160:192, 0:80]
    wkv_o[0] = sums[192:288, 0:80]
    wkv_o[1] = sums[288:384, 0:80]
    g = sums[384:464]
    for t in range(6):
        for b in range(2):
            byte_o[b : b + 1, 128 * t : 128 * t + 128] = g[6 * b + t : 6 * b + t + 1, :]
    for t in range(10):
        for b in range(5):
            r = 16 + t if b == 0 else 32 + 10 * (b - 1) + t
            lat_o[b : b + 1, 128 * t : 128 * t + 128] = g[r : r + 1, :]
    for m, (kind, n) in enumerate(SQUARE):
        window, o = PLACE[m]
        v = pack[:, 256 * window : 256 * window + 256].astype(F32)
        if o:
            v = pltpu.roll(v, 256 - o, 1)
        if kind == "l":
            lm_o[n] = v[:, 0:80]
        else:
            om_o[n] = v[:, 0:80]


def line(y, c, x, z):
    return ((y % 4) * 2 + c) * NJ + (x % 4) * NZ + (z % 4)


EVERY = [(y, c, x, z) for y in range(4) for c in range(2) for x in range(NX) for z in range(NZ)]


def along(stage, d):
    out = []
    for y, c, x, z in EVERY:
        on_x = (c == 0) == (stage == 0)
        out.append((line(y, c, x, z), line(y, c, x + d, z) if on_x else line(y, c, x, z + d)))
    return out


SWAP = [(line(y, c, x, z), line(y, 1 - c, x, z)) for y, c, x, z in EVERY]


def exchange(v, axes):
    flat = v.reshape(v.shape[0] * v.shape[1], v.shape[2])
    return lax.all_to_all(flat, axes, split_axis=0, concat_axis=0, tiled=True).reshape(v.shape)


def shards(inputs, queries, lengths, latent_array, latent_mats, out_mats, byte_mats, dec_out, lg, bg, cotangent):
    y, core, x, z = (lax.axis_index(a) for a in AXES)
    i, j = y * 2 + core, x * NZ + z
    sc = jnp.stack([i, j, x, z, core, lengths[0]]).astype(jnp.int32)
    xin, qin, cot = inputs[0], queries[0], cotangent[0]

    g0, wsh = call(
        pack_body,
        [((192, 640), BF, "h"), ((ROWS_I, D), BF, "h")],
        [(sc, "s"), (latent_mats, "h"), (out_mats, "h"), (byte_mats, "h"), (dec_out, "h"), (latent_array, "h")],
        [DMA((12,))],
        vmem=60,
        name="pack",
    )
    w = lax.all_gather(wsh, AXES, axis=0, tiled=True).reshape(NI, NJ, ROWS_I, D)

    def step(v, stage):
        return [lax.ppermute(v, AXES, along(stage, d)) for d in (1, 2, 3)]

    s0 = jnp.stack([g0] + step(g0, 0))
    own = [s0] + step(s0, 1)
    sib = [lax.ppermute(v, AXES, SWAP) for v in own]
    g_all, nb, k_b, v_b, q_b, pay = call(
        enc_body,
        [
            ((NJ, 192, D), BF, "h"),
            ((N, DI), BF, "v"),
            ((N, D), BF, "v"),
            ((N, D), BF, "v"),
            ((R, D), BF, "v"),
            ((R, D + 128), BF, "v"),
        ],
        [(sc, "s")] + [(v, "h") for v in own + sib] + [(xin, "v"), (bg, "v"), (lg, "v")],
        [pltpu.VMEM((NJ, 192, D), BF), pltpu.VMEM((R, D), F32), DMA((33,))],
        vmem=60,
        flops=3e9,
        name="enc",
    )
    rcv = exchange(pay.reshape(NJ, 16, D + 128), BLK)
    (mine,) = call(combine_body, [((16, D + 128), BF, "v")], [(rcv, "v")], name="combine")
    e = lax.all_gather(mine, BLK, axis=0, tiled=True)
    nf = lax.all_gather(nb, BLK, axis=0, tiled=True)

    big = (NJ, 80, D)
    res, gqin, gd, dpay, mix, nd, gq, z_h, h_h, a_h = call(
        forward_body,
        [
            ((N, DI), BF, "v"),
            ((N, DI), F32, "v"),
            ((1, DI), F32, "v"),
            ((R, 2 * D), BF, "v"),
            ((N, D), BF, "v"),
            ((N, DI), BF, "v"),
            ((N, D), BF, "v"),
            ((4, R, D), F32, "h"),
            ((2, R, D), F32, "h"),
            ((4, R, D), BF, "h"),
        ],
        [(qin, "v"), (cot, "v"), (bg, "v"), (lg, "v"), (e, "h"), (g_all, "h"), (w, "h")],
        [
            pltpu.VMEM((5,) + big, BF),
            pltpu.VMEM((R, D), BF),
            pltpu.VMEM((NJ, 16, D), BF),
            pltpu.VMEM((4, R, D), F32),
            pltpu.VMEM((2, R, D), F32),
            pltpu.VMEM((4, R, D), BF),
            pltpu.VMEM((R, D), F32),
            pltpu.VMEM((R, D), BF),
            pltpu.VMEM((R, D), BF),
            pltpu.VMEM((NJ, 80, DI), BF),
            pltpu.VMEM((NJ, 48, D), BF),
            pltpu.VMEM((N, D), F32),
            pltpu.VMEM((N, D), F32),
            pltpu.VMEM((2, R, D), F32),
            DMA((5, 2)),
            DMA((10,)),
            DMA((5,)),
        ],
        vmem=58,
        flops=1.5e10,
        name="forward",
    )
    rows = exchange(dpay.reshape(NJ, 16, 2 * D), BLK)
    n_h, i_h, s_h, act_h, p_h = call(
        prepare_body,
        [
            ((4, R, D), F32, "h"),
            ((4, R, 128), F32, "h"),
            ((2, R, D), F32, "h"),
            ((6, R, D), BF, "h"),
            ((H, R, R), F32, "h"),
        ],
        [(lg, "v"), (z_h, "h"), (h_h, "h"), (a_h, "h")],
        [
            pltpu.VMEM((4, R, D), F32),
            pltpu.VMEM((2, R, D), F32),
            pltpu.VMEM((2, R, D), BF),
            pltpu.VMEM((4, R, D), F32),
            pltpu.VMEM((4, R, 128), F32),
            pltpu.VMEM((2, R, D), F32),
            pltpu.VMEM((6, R, D), BF),
            pltpu.VMEM((H, R, R), F32),
            DMA((7,)),
            DMA((14,)),
        ],
        vmem=60,
        flops=5e9,
        name="prepare",
    )
    (dup,) = call(sum_rows_body, [((NJ, 16, 2 * D), BF, "v")], [(rows, "v")], name="sum_rows")
    gkv = exchange(dup, BLK).reshape(R, 2 * D)
    mix, _, nf = lax.optimization_barrier((mix, dup, nf))
    (dw,) = call(
        dec_weights_body,
        [((NI, 1920, 128), BF, "h")],
        [(mix, "v"), (cot, "v"), (nd, "v"), (gq, "v")],
        [pltpu.VMEM((NI, 1920, 128), BF), DMA((2,))],
        vmem=60,
        flops=4e9,
        name="dec_weights",
    )
    dw = lax.psum_scatter(dw.reshape(NI * 1920, 128), BATCH, scatter_dimension=0, tiled=True)

    gmix, pack, g1c, lat_gain = call(
        lat_backward_body,
        [((R, D), BF, "v"), ((D, 1024), BF, "v"), ((R, 128), BF, "v"), ((48, 128), F32, "v")],
        [(sc, "s"), (gkv, "v"), (lg, "v")] + [(v, "h") for v in (w, e, n_h, i_h, s_h, act_h, a_h, p_h)],
        [
            pltpu.VMEM((4,) + big, BF),
            pltpu.VMEM((4, R, D), F32),
            pltpu.VMEM((4, R, 128), F32),
            pltpu.VMEM((2, R, D), F32),
            pltpu.VMEM((8, R, D), BF),
            pltpu.VMEM((4, R, D), BF),
            pltpu.VMEM((H, R, R), F32),
            pltpu.VMEM((R, D), F32),
            pltpu.VMEM((R, D), F32),
            pltpu.VMEM((2, R, D), F32),
            pltpu.VMEM((R, D), BF),
            pltpu.VMEM((8, R, 256), BF),
            DMA((4, 2)),
            DMA((17,)),
        ],
        vmem=58,
        flops=1.6e10,
        name="lat_backward",
    )
    pack = lax.psum_scatter(pack, BATCH, scatter_dimension=0, tiled=True)
    gin, epay = call(
        enc_back_body,
        [((N, DI), F32, "v"), ((NJ, 688, 128), BF, "v")],
        [(sc, "s"), (xin, "v"), (bg, "v"), (lg, "v"), (gd, "v")]
        + [(v, "h") for v in (gmix, e, q_b, k_b, v_b, g_all, dw)],
        [
            pltpu.VMEM((R, D), BF),
            pltpu.VMEM((R, D + 128), BF),
            pltpu.VMEM((R, D), BF),
            pltpu.VMEM((N, D), BF),
            pltpu.VMEM((N, D), BF),
            pltpu.VMEM((NJ, 192, D), BF),
            pltpu.VMEM((R, D), F32),
            pltpu.VMEM((D, N), BF),
            pltpu.VMEM((D, N), BF),
            pltpu.VMEM((1920, 128), BF),
            pltpu.VMEM((DI, 256), F32),
            pltpu.VMEM((D, 128), F32),
            DMA((7,)),
        ],
        vmem=56,
        flops=3e9,
        name="enc_back",
    )
    r1 = exchange(epay, BLK)
    p2, dec_grad, bq_grad = call(
        tail_one_body,
        [((NI, 464, 128), BF, "v"), ((160, 48), F32, "v"), ((96, 80), F32, "v")],
        [(r1, "v"), (nf, "h"), (g_all, "h"), (lg, "v"), (lat_gain, "v"), (g1c, "v")],
        [pltpu.VMEM((NJ * N, DI), BF), pltpu.VMEM((NJ, 16, D), BF), pltpu.VMEM((256, 2048), BF), DMA((2,))],
        name="tail_one",
    )
    r2 = exchange(p2, BATCH)
    arr, lm, om, wkv, lat_gains, byte_gain = call(
        tail_two_body,
        [
            ((32, 80), F32, "v"),
            ((10, 160, 80), F32, "v"),
            ((2, 160, 80), F32, "v"),
            ((2, 96, 80), F32, "v"),
            ((5, D), F32, "v"),
            ((2, DI), F32, "v"),
        ],
        [(r2, "v"), (pack, "v")],
        name="tail_two",
    )
    byte_grads = jnp.concatenate([wkv, bq_grad[None]], axis=0)
    return (res[None], gin[None], gqin[None], arr, lm, om, byte_grads, dec_grad, lat_gains, byte_gain)


def solution(mesh):
    grid = Mesh(mesh.devices.reshape(4, 2, NX, NZ), AXES)
    return jax.shard_map(
        shards,
        mesh=grid,
        in_specs=(
            P(BATCH, BLK, None),
            P(BATCH, BLK, None),
            P(BATCH),
            P(BLK, None),
            P(None, BLK, None),
            P(None, BLK, None),
            P(None, BLK, None),
            P(BLK, None),
            P(),
            P(),
            P(BATCH, BLK, None),
        ),
        out_specs=(
            P(BATCH, BLK, None),
            P(BATCH, BLK, None),
            P(BATCH, BLK, None),
            P(BATCH, BLK),
            P(None, BATCH, BLK),
            P(None, BATCH, BLK),
            P(None, BATCH, BLK),
            P(BATCH, BLK),
            P(),
            P(),
        ),
        check_vma=False,
    )
```

profile of v0, /device:TPU:1, one launch (start us, length us, event | category | flops | bytes accessed | tf_op | source)
XLA Modules:
  0.0 386.0 jit_solution(15918921579842064518)
XLA Ops:
  8.5 19.3 %pack.1 = (bf16[192,640]{1,0:T(8,128)(2,1)}, bf16[128,1280]{1,0:T(8,128)(2,1)}) custom-call(s32[6]{0:T(128)} %stack.38.sc, bf16[10,80,1280]{2,1,0:T(8,128)(2,1)} %lm.1, bf16[2,80,1280]{2,1,0:T(8,128)(2,1)} %om.1, bf16[3,48,1280]{2,1,0:T(8,128)(2,1)} %bm.1, bf16[80,768]{1,0:T(8,128)(2,1)} %do.1, bf16[16,1280]{1,0:T(8,128)(2,1)} %la.1), custom_call_target="tpu_custom_call" | custom-call | bytes 4194304 | tf_op jit(solution)/shard_map/pack/pallas_call | solution.py:113
  27.8 4.7 %collective-permute-start.2 = (bf16[192,640]{1,0:T(8,128)(2,1)}, bf16[192,640]{1,0:T(8,128)(2,1)S(1)}, u32[]{:S(2)}, u32[]{:S(2)}) collective-permute-start(bf16[192,640]{1,0:T(8,128)(2,1)} %get-tuple-element.50), channel_id=1, source_target_pairs={{0,12},{1,13},{2,14},{3,15},{4,0},{5,1},{6,2},{7,3},{8,4},{9,5},{1... | collective-permute-start | bytes 737288 | tf_op jit(solution)/shard_map/ppermute | solution.py:736
  33.2 5.4 %collective-permute-done.2 = bf16[192,640]{1,0:T(8,128)(2,1)S(1)} collective-permute-done((bf16[192,640]{1,0:T(8,128)(2,1)}, bf16[192,640]{1,0:T(8,128)(2,1)S(1)}, u32[]{:S(2)}, u32[]{:S(2)}) %collective-permute-start.2) | collective-permute-done | bytes 245792 | tf_op jit(solution)/shard_map/ppermute | solution.py:736
  44.0 2.4 collective-permute-start.4
  47.6 2.8 collective-permute-start.6
  50.4 9.6 %collective-permute-done.3.t1 = bf16[4,192,640]{2,1,0:T(8,128)(2,1)S(1)} collective-permute-done((bf16[4,192,640]{2,1,0:T(8,128)(2,1)S(1)}, bf16[4,192,640]{2,1,0:T(8,128)(2,1)S(1)}, u32[]{:S(2)}, u32[]{:S(2)}) %collective-permute-start.3) | collective-permute-done | bytes 983072 | tf_op jit(solution)/shard_map/ppermute | solution.py:736
  62.3 8.8 %collective-permute-done.4.t2 = bf16[4,192,640]{2,1,0:T(8,128)(2,1)S(1)} collective-permute-done((bf16[4,192,640]{2,1,0:T(8,128)(2,1)S(1)}, bf16[4,192,640]{2,1,0:T(8,128)(2,1)S(1)}, u32[]{:S(2)}, u32[]{:S(2)}) %collective-permute-start.4) | collective-permute-done | bytes 983072 | tf_op jit(solution)/shard_map/ppermute | solution.py:736
  71.1 3.1 collective-permute-start.8
  78.7 9.2 %enc.1 = (bf16[16,192,1280]{2,1,0:T(8,128)(2,1)}, bf16[128,768]{1,0:T(8,128)(2,1)}, bf16[128,1280]{1,0:T(8,128)(2,1)}, bf16[128,1280]{1,0:T(8,128)(2,1)}, bf16[2...) custom-call(s32[6]{0:T(128)} %stack.38.sc, bf16[4,192,640]{2,1,0:T(8,128)(2,1)} %copy-done.5, ...), custom_call_target="tpu_custom_call" | custom-call | flops 3000000000 | bytes 4194304 | tf_op jit(solution)/shard_map/enc/pallas_call | solution.py:113
  88.0 18.5 %all_to_all.38.rcv = bf16[16,16,1408]{2,1,0:T(8,128)(2,1)S(1)} all-to-all(bf16[16,16,1408]{2,1,0:T(8,128)(2,1)} %bitcast.27), channel_id=1, replica_groups=mesh['y'=4,'core'=2,'x'=4,'z'=4] {'x','z'}, dimensions={0} | all-to-all | bytes 1441792 | tf_op jit(solution)/shard_map/all_to_all | solution.py:716
  107.0 23.7 %all_gather.9.e_h = bf16[256,1408]{1,0:T(8,128)(2,1)} all-gather(bf16[16,1408]{1,0:T(8,128)(2,1)S(1)} %combine.1), channel_id=1, replica_groups=mesh['y'=4,'core'=2,'x'=4,'z'=4] {'x','z'}, dimensions={0}, use_global_device_ids=true | all-gather | bytes 765952 | tf_op jit(solution)/shard_map/all_gather | solution.py:759
  130.7 46.1 %all-gather.3.cloned.1.call-done = bf16[16384,1280]{1,0:T(8,128)(2,1)} async-done(((bf16[128,1280]{1,0:T(8,128)(2,1)}), bf16[16384,1280]{1,0:T(8,128)(2,1)}) %all-gather.3.cloned.1.call-update) | async-done | bytes 41943056 | tf_op jit(solution)/shard_map/all_gather | solution.py:733
  176.8 30.3 %forward.1 = (bf16[128,768]{1,0:T(8,128)(2,1)}, f32[128,768]{1,0:T(8,128)}, f32[1,768]{1,0:T(1,128)}, bf16[256,2560]{1,0:T(8,128)(2,1)}, bf16[128,1280]{1,0:T(8,...) custom-call(bf16[128,768]{1,0:T(8,128)(2,1)} %bitcast.35, ...), custom_call_target="tpu_custom_call" | custom-call | flops 15000000512 | bytes 4194304 | tf_op jit(solution)/shard_map/forward/pallas_call | solution.py:113
  207.1 32.6 %all_to_all.39.rcv = bf16[16,16,2560]{2,1,0:T(8,128)(2,1)S(1)} all-to-all(bf16[16,16,2560]{2,1,0:T(8,128)(2,1)} %bitcast.26), channel_id=1, replica_groups=mesh['y'=4,'core'=2,'x'=4,'z'=4] {'x','z'}, dimensions={0} | all-to-all | bytes 2621440 | tf_op jit(solution)/shard_map/all_to_all | solution.py:716
  241.0 4.1 %dec_weights.1 = bf16[8,1920,128]{2,1,0:T(8,128)(2,1)} custom-call(bf16[128,1280]{1,0:T(8,128)(2,1)} %get-tuple-element.71.mix, bf16[128,768]{1,0:T(8,128)(2,1)} %bitcast.37, bf16[128,768]{1,0:T(8,128)(2,1)} %get-tuple-element.72.nd, bf16[128,1280]{1,0:T(8,128)(2,1)} %get-tuple-element.73.gq), custom_call_target="tpu_custom_call" | custom-call | flops 4000000000 | bytes 4194304 | tf_op jit(solution)/shard_map/dec_weights/pallas_call | solution.py:113
  245.1 3.9 %all-to-all-start.2 = ((bf16[16,16,2560]{2,1,0:T(8,128)(2,1)}), bf16[16,16,2560]{2,1,0:T(8,128)(2,1)S(1)}, u32[]{:S(2)}, u32[]{:S(2)}) async-start(bf16[16,16,2560]{2,1,0:T(8,128)(2,1)} %sum_rows.1), calls=%async_computation.2 | async-start | bytes 2621440 | tf_op jit(solution)/shard_map/all_to_all | solution.py:716
  249.2 9.1 %prepare.1 = (f32[4,256,1280]{2,1,0:T(8,128)}, f32[4,256,128]{2,1,0:T(8,128)}, f32[2,256,1280]{2,1,0:T(8,128)}, bf16[6,256,1280]{2,1,0:T(8,128)(2,1)}, f32[8,256,256]{2,1,0:T(8,128)}) custom-call(f32[5,1280]{1,0:T(8,128)} %lg.11, f32[4,256,1280]{2,1,0:T(8,128)} %get-tuple-element.57.z_h, f32[2,256,1280]{2,1,0:T(8,128)} %get-tuple-element.58.h_h, ...), custom_call_target="tpu_custom_call" | custom-call | flops 5000000000 | bytes 4194304 | tf_op jit(solution)/shard_map/prepare/pallas_call | solution.py:113
  258.3 8.6 %all-to-all-done.2 = bf16[16,16,2560]{2,1,0:T(8,128)(2,1)S(1)} async-done(((bf16[16,16,2560]{2,1,0:T(8,128)(2,1)}), bf16[16,16,2560]{2,1,0:T(8,128)(2,1)S(1)}, u32[]{:S(2)}, u32[]{:S(2)}) %all-to-all-start.2) | async-done | bytes 1310752 | tf_op jit(solution)/shard_map/all_to_all | solution.py:716
  268.0 33.2 %lat_backward.1 = (bf16[256,1280]{1,0:T(8,128)(2,1)}, bf16[1280,1024]{1,0:T(8,128)(2,1)}, bf16[256,128]{1,0:T(8,128)(2,1)}, f32[48,128]{1,0:T(8,128)}) custom-call(s32[6]{0:T(128)} %stack.38.sc, bf16[256,2560]{1,0:T(8,128)(2,1)} %bitcast.24, f32[5,1280]{1,0:T(8,128)} %lg.11, bf16[8,16,128,1280]{3,2,1,0:T(8,128)(2,1)} %bitcast.23, ...), custom_call_target="tpu_custom_call" | custom-call | flops 16000000000 | bytes 4194304 | tf_op jit(solution)/shard_map/lat_backward/pallas_call | solution.py:113
  301.3 10.2 %enc_back.1 = (f32[128,768]{1,0:T(8,128)}, bf16[16,688,128]{2,1,0:T(8,128)(2,1)}) custom-call(s32[6]{0:T(128)} %stack.38.sc, bf16[128,768]{1,0:T(8,128)(2,1)} %bitcast.33, f32[2,768]{1,0:T(2,128)} %bg.5, f32[5,1280]{1,0:T(8,128)} %lg.11, f32[1,768]{1,0:T(1,128)} %get-tuple-element.55.gd, bf16[256,1280]{1,0:T(8,128)(2,1)} %get-tuple-element.65.gmix_h, ...), custom_call_target="tpu_custom_call" | custom-call | flops 3000000000 | bytes 4194304 | tf_op jit(solution)/shard_map/enc_back/pallas_call | solution.py:113
  311.5 36.6 %all_to_all.40.rcv = bf16[16,688,128]{2,1,0:T(8,128)(2,1)S(1)} all-to-all(bf16[16,688,128]{2,1,0:T(8,128)(2,1)} %get-tuple-element.76), channel_id=1, replica_groups=mesh['y'=4,'core'=2,'x'=4,'z'=4] {'x','z'}, dimensions={0} | all-to-all | bytes 5636096 | tf_op jit(solution)/shard_map/all_to_all | solution.py:716
  348.1 5.1 %tail_one.1 = (bf16[8,464,128]{2,1,0:T(8,128)(2,1)}, f32[160,48]{1,0:T(8,128)S(1)}, f32[96,80]{1,0:T(8,128)S(1)}) custom-call(bf16[16,688,128]{2,1,0:T(8,128)(2,1)S(1)} %all_to_all.40.rcv, bf16[2048,768]{1,0:T(8,128)(2,1)} %all-gather.5.cloned.1.call-done.nf_h, bf16[16,192,1280]{2,1,0:T(8,128)(2,1)} %get-tuple-element.52.g_all, f32[5,1280]{1,0:T(8,128)S(1)} %copy-done, ...), custom_call_target="tpu_custom_call" | custom-call | bytes 4194304 | tf_op jit(solution)/shard_map/tail_one/pallas_call | solution.py:113
  353.2 8.9 %all-to-all-start.4 = ((bf16[8,464,128]{2,1,0:T(8,128)(2,1)}), bf16[8,464,128]{2,1,0:T(8,128)(2,1)S(1)}, u32[]{:S(2)}, u32[]{:S(2)}) async-start(bf16[8,464,128]{2,1,0:T(8,128)(2,1)} %get-tuple-element.80), calls=%async_computation.5 | async-start | bytes 1900544 | tf_op jit(solution)/shard_map/all_to_all | solution.py:716
  362.8 13.3 %all-to-all-done.4.rcv = bf16[8,464,128]{2,1,0:T(8,128)(2,1)S(1)} async-done(((bf16[8,464,128]{2,1,0:T(8,128)(2,1)}), bf16[8,464,128]{2,1,0:T(8,128)(2,1)S(1)}, u32[]{:S(2)}, u32[]{:S(2)}) %all-to-all-start.4) | async-done | bytes 950304 | tf_op jit(solution)/shard_map/all_to_all | solution.py:716
  (58 shorter events, 21.7 us)
Async XLA Ops:
  7.2 169.6 %all-gather.3.cloned.1.call-start = ((), (), s32[]{:S(2)}) async-start(), calls=%async_computation.7 | async-start | bytes 42270720 | tf_op jit(solution)/shard_map/all_gather | solution.py:733
  27.8 213.2 %all-gather.5.cloned.1.call-start = ((), (), s32[]{:S(2)}) async-start(), calls=%async_computation.8 | async-start | bytes 3342336 | tf_op jit(solution)/shard_map/all_gather | solution.py:760
  27.8 10.7 %collective-permute-start.2 = (bf16[192,640]{1,0:T(8,128)(2,1)}, bf16[192,640]{1,0:T(8,128)(2,1)S(1)}, u32[]{:S(2)}, u32[]{:S(2)}) collective-permute-start(bf16[192,640]{1,0:T(8,128)(2,1)} %get-tuple-element.50), channel_id=1, source_target_pairs={{0,12},{1,13},{2,14},{3,15},{4,0},{5,1},{6,2},{7,3},{8,4},{9,5},{1... | collective-permute-start | bytes 737288 | tf_op jit(solution)/shard_map/ppermute | solution.py:736
  32.5 7.1 %collective-permute-start.1 = (bf16[192,640]{1,0:T(8,128)(2,1)}, bf16[192,640]{1,0:T(8,128)(2,1)S(1)}, u32[]{:S(2)}, u32[]{:S(2)}) collective-permute-start(bf16[192,640]{1,0:T(8,128)(2,1)} %get-tuple-element.50), channel_id=1, source_target_pairs={{0,8},{1,9},{2,10},{3,11},{4,12},{5,13},{6,14},{7,15},{8,0},{9,1},... | collective-permute-start | bytes 737288 | tf_op jit(solution)/shard_map/ppermute | solution.py:736
  32.5 9.4 %collective-permute-start = (bf16[192,640]{1,0:T(8,128)(2,1)}, bf16[192,640]{1,0:T(8,128)(2,1)S(1)}, u32[]{:S(2)}, u32[]{:S(2)}) collective-permute-start(bf16[192,640]{1,0:T(8,128)(2,1)} %get-tuple-element.50), channel_id=1, source_target_pairs={{0,4},{1,5},{2,6},{3,7},{4,8},{5,9},{6,10},{7,11},{8,12},{9,13},{1... | collective-permute-start | bytes 737288 | tf_op jit(solution)/shard_map/ppermute | solution.py:736
  43.0 35.7 %copy-start.5 = (bf16[4,192,640]{2,1,0:T(8,128)(2,1)}, bf16[4,192,640]{2,1,0:T(8,128)(2,1)S(1)}, u32[]{:S(2)}) copy-start(bf16[4,192,640]{2,1,0:T(8,128)(2,1)S(1)} %pad_maximum_fusion.t0) | copy-start | bytes 2949124
  43.0 17.0 %collective-permute-start.3 = (bf16[4,192,640]{2,1,0:T(8,128)(2,1)S(1)}, bf16[4,192,640]{2,1,0:T(8,128)(2,1)S(1)}, u32[]{:S(2)}, u32[]{:S(2)}) collective-permute-start(bf16[4,192,640]{2,1,0:T(8,128)(2,1)S(1)} %pad_maximum_fusion.t0), channel_id=1, source_target_pairs={{0,1},{1,2},{2,3},{3,0},{4,5},{5,6},{6,7},{7,4},{8,9},{9,10},{10,1... | collective-permute-start | bytes 2949128 | tf_op jit(solution)/shard_map/ppermute | solution.py:736
  44.0 27.1 %collective-permute-start.4 = (bf16[4,192,640]{2,1,0:T(8,128)(2,1)S(1)}, bf16[4,192,640]{2,1,0:T(8,128)(2,1)S(1)}, u32[]{:S(2)}, u32[]{:S(2)}) collective-permute-start(bf16[4,192,640]{2,1,0:T(8,128)(2,1)S(1)} %pad_maximum_fusion.t0), channel_id=1, source_target_pairs={{0,2},{1,3},{2,0},{3,1},{4,6},{5,7},{6,4},{7,5},{8,10},{9,11},{10,... | collective-permute-start | bytes 2949128 | tf_op jit(solution)/shard_map/ppermute | solution.py:736
  46.4 27.7 %collective-permute-start.5 = (bf16[4,192,640]{2,1,0:T(8,128)(2,1)S(1)}, bf16[4,192,640]{2,1,0:T(8,128)(2,1)S(1)}, u32[]{:S(2)}, u32[]{:S(2)}) collective-permute-start(bf16[4,192,640]{2,1,0:T(8,128)(2,1)S(1)} %pad_maximum_fusion.t0), channel_id=1, source_target_pairs={{0,3},{1,0},{2,1},{3,2},{4,7},{5,4},{6,5},{7,6},{8,11},{9,8},{10,9... | collective-permute-start | bytes 2949128 | tf_op jit(solution)/shard_map/ppermute | solution.py:736
  47.6 26.7 %collective-permute-start.6 = (bf16[4,192,640]{2,1,0:T(8,128)(2,1)S(1)}, bf16[4,192,640]{2,1,0:T(8,128)(2,1)S(1)}, u32[]{:S(2)}, u32[]{:S(2)}) collective-permute-start(bf16[4,192,640]{2,1,0:T(8,128)(2,1)S(1)} %pad_maximum_fusion.t0), channel_id=1, source_target_pairs={{0,16},{1,17},{2,18},{3,19},{4,20},{5,21},{6,22},{7,23},{8,24},{9,... | collective-permute-start | bytes 2949128 | tf_op jit(solution)/shard_map/ppermute | solution.py:740
  60.0 18.7 %copy-start.6 = (bf16[4,192,640]{2,1,0:T(8,128)(2,1)}, bf16[4,192,640]{2,1,0:T(8,128)(2,1)S(1)}, u32[]{:S(2)}) copy-start(bf16[4,192,640]{2,1,0:T(8,128)(2,1)S(1)} %collective-permute-done.3.t1) | copy-start | bytes 2949124
  60.0 14.3 %collective-permute-start.7 = (bf16[4,192,640]{2,1,0:T(8,128)(2,1)S(1)}, bf16[4,192,640]{2,1,0:T(8,128)(2,1)S(1)}, u32[]{:S(2)}, u32[]{:S(2)}) collective-permute-start(bf16[4,192,640]{2,1,0:T(8,128)(2,1)S(1)} %collective-permute-done.3.t1), channel_id=1, source_target_pairs={{0,16},{1,17},{2,18},{3,19},{4,20},{5,21},{6,22},{7,23},{8,24},{9,... | collective-permute-start | bytes 2949128 | tf_op jit(solution)/shard_map/ppermute | solution.py:740
  71.1 7.6 %copy-start.7 = (bf16[4,192,640]{2,1,0:T(8,128)(2,1)}, bf16[4,192,640]{2,1,0:T(8,128)(2,1)S(1)}, u32[]{:S(2)}) copy-start(bf16[4,192,640]{2,1,0:T(8,128)(2,1)S(1)} %collective-permute-done.4.t2) | copy-start | bytes 2949124
  71.1 5.3 %collective-permute-start.8 = (bf16[4,192,640]{2,1,0:T(8,128)(2,1)S(1)}, bf16[4,192,640]{2,1,0:T(8,128)(2,1)S(1)}, u32[]{:S(2)}, u32[]{:S(2)}) collective-permute-start(bf16[4,192,640]{2,1,0:T(8,128)(2,1)S(1)} %collective-permute-done.4.t2), channel_id=1, source_target_pairs={{0,16},{1,17},{2,18},{3,19},{4,20},{5,21},{6,22},{7,23},{8,24},{9,... | collective-permute-start | bytes 2949128 | tf_op jit(solution)/shard_map/ppermute | solution.py:740
  74.2 4.6 %copy-start.8 = (bf16[4,192,640]{2,1,0:T(8,128)(2,1)}, bf16[4,192,640]{2,1,0:T(8,128)(2,1)S(1)}, u32[]{:S(2)}) copy-start(bf16[4,192,640]{2,1,0:T(8,128)(2,1)S(1)} %collective-permute-done.5.t3) | copy-start | bytes 2949124
  74.2 3.6 collective-permute-start.9
  74.2 3.5 copy-start.9
  87.9 213.4 %reduce-scatter.3.cloned.1.call-start = ((), (), s32[]{:S(2)}) async-start(), calls=%async_computation.9 | async-start | bytes 4423680 | tf_op jit(solution)/shard_map/reduce_scatter | solution.py:840
  245.1 21.9 %all-to-all-start.2 = ((bf16[16,16,2560]{2,1,0:T(8,128)(2,1)}), bf16[16,16,2560]{2,1,0:T(8,128)(2,1)S(1)}, u32[]{:S(2)}, u32[]{:S(2)}) async-start(bf16[16,16,2560]{2,1,0:T(8,128)(2,1)} %sum_rows.1), calls=%async_computation.2 | async-start | bytes 2621440 | tf_op jit(solution)/shard_map/all_to_all | solution.py:716
  249.0 113.8 %reduce-scatter.5.cloned.1.call-start = ((), (), s32[]{:S(2)}) async-start(), calls=%async_computation.10 | async-start | bytes 2949120 | tf_op jit(solution)/shard_map/reduce_scatter | solution.py:866
  311.5 36.6 %copy-start = (f32[5,1280]{1,0:T(8,128)S(1)}, f32[5,1280]{1,0:T(8,128)}, u32[]{:S(2)}) copy-start(f32[5,1280]{1,0:T(8,128)} %lg.11) | copy-start | bytes 76804
  311.5 36.6 %copy-start.2 = (bf16[256,128]{1,0:T(8,128)(2,1)S(1)}, bf16[256,128]{1,0:T(8,128)(2,1)}, u32[]{:S(2)}) copy-start(bf16[256,128]{1,0:T(8,128)(2,1)} %get-tuple-element.79.g1c) | copy-start | bytes 196612
  311.5 36.6 %copy-start.3 = (f32[48,128]{1,0:T(8,128)S(1)}, f32[48,128]{1,0:T(8,128)}, u32[]{:S(2)}) copy-start(f32[48,128]{1,0:T(8,128)} %get-tuple-element.78.lat_gain) | copy-start | bytes 73732
  353.2 22.9 %all-to-all-start.4 = ((bf16[8,464,128]{2,1,0:T(8,128)(2,1)}), bf16[8,464,128]{2,1,0:T(8,128)(2,1)S(1)}, u32[]{:S(2)}, u32[]{:S(2)}) async-start(bf16[8,464,128]{2,1,0:T(8,128)(2,1)} %get-tuple-element.80), calls=%async_computation.5 | async-start | bytes 1900544 | tf_op jit(solution)/shard_map/all_to_all | solution.py:716
  (5 other events, 7.9 us)
Sparse Core Ops, SparseCore 0:
  27.9 148.8 all-gather.2
  179.0 58.6 all-gather.4
  245.2 33.4 reduce-scatter.2
  301.4 32.4 reduce-scatter.4
where the time goes:
time: 392 us; the launch traced here: 386 us
  Pallas kernels  123 us (31%)
  blocking collectives  111 us (28%)
  waiting for transfers between devices  98.8 us (25%)
  starting transfers between devices  31.3 us (8%)
  between operations  15 us (4%)
  local copies, waits for them, and re-layouts  5.09 us (1%)
    pallas_call x11, Pallas kernels, call(): pl.pallas_call(body, out_shape=[jax.ShapeDtypeStruct(s, t) for s, t, _ in...  123 us
    all_to_all x3, blocking collectives, exchange(): lax.all_to_all(flat, axes, split_axis=0, concat_axis=0, tiled=True)  87.6 us
    all_gather x1, waiting for transfers between devices, shards(): w = lax.all_gather(wsh, AXES, axis=0, tiled=True).reshape(NI, NJ, ROWS_I, D)  46.1 us
    ppermute x6, waiting for transfers between devices, step(): return [lax.ppermute(v, AXES, along(stage, d)) for d in (1, 2, 3)]  27.1 us
    all_gather x1, blocking collectives, shards(): e = lax.all_gather(mine, BLK, axis=0, tiled=True)  23.7 us
    all_to_all x2, waiting for transfers between devices, exchange(): lax.all_to_all(flat, axes, split_axis=0, concat_axis=0, tiled=True)  21.9 us
    all_to_all x2, starting transfers between devices, exchange(): lax.all_to_all(flat, axes, split_axis=0, concat_axis=0, tiled=True)  12.8 us
    ppermute x6, starting transfers between devices, step(): return [lax.ppermute(v, AXES, along(stage, d)) for d in (1, 2, 3)]  9.96 us
  transfers between devices with their start and end apart: 16, of which 10 were waited for; matrix products, arithmetic and copies ran while one was open for 0% of the time, Pallas kernels for 26%

commit v1 on v0

--- a/solution.py
+++ b/solution.py
@@ -125,7 +125,7 @@
 DMA = pltpu.SemaphoreType.DMA
 
 
-def pack_body(sc, lm, om, bm, do, la, g0, wsh, sem):
+def pack_body(sc, lm, om, bm, do, la, g0, wsh, buf, sem):
     i, core = sc[0], sc[4]
     cols = pl.ds(pl.multiple_of(core * 640, 128), 640)
     first = [
@@ -149,15 +149,18 @@
                 a, b = max(lo, row), min(hi, row + count)
                 if a < b:
                     src = ref.at[a - row : b - row, :] if n is None else ref.at[n, a - row : b - row, :]
-                    dst = wsh.at[a - lo : b - lo, :] if width == D else wsh.at[a - lo : b - lo, 0:width]
+                    dst = buf.at[a - lo : b - lo, :] if width == D else buf.at[a - lo : b - lo, 0:width]
                     cs.append(pltpu.make_async_copy(src, dst, sem.at[len(cs)]))
             for c in cs:
                 c.start()
             for c in cs:
                 c.wait()
 
+    out = pltpu.make_async_copy(buf, wsh, sem.at[12])
+    out.start()
     for c in first:
         c.wait()
+    out.wait()
 
 
 def pieces_from(sc, groups):
@@ -375,7 +378,7 @@
         c.wait()
 
 
-def prepare_body(lg, z_h, h_h, a_h, n_h, i_h, s_h, act_h, p_h, zs, hs, qs, ns, vs, ss, acts, ps, sem, osem):
+def prepare_body(lg, z_h, h_h, a_h, n_h, i_h, s_h, act_h, p_h, mark, zs, hs, qs, ns, vs, ss, acts, ps, sem, osem):
     loads = {}
     for k in range(4):
         loads["z", k] = pltpu.make_async_copy(z_h.at[k], zs.at[k], sem.at[k])
@@ -394,7 +397,7 @@
     for k, a in ((3, 0), (2, 2), (1, 1), (0, 4)):
         loads["z", k].wait()
         n, inv = norm(zs[k])
-        ns[k] = n
+        ns[k] = half(n)
         save(ns.at[k], n_h.at[k])
         vs[k] = jnp.broadcast_to(inv, (R, 128))
         acts[a] = half(n * lg[k + 1 : k + 2, :])
@@ -413,8 +416,9 @@
         win = slice(WIN[h], WIN[h] + 256)
         s = dot_nt(qs[0, :, win] * half(head_mask(h)), qs[1, :, win]) * SCALE
         p = jnp.exp(s - jnp.max(s, axis=-1, keepdims=True))
-        ps[h] = p / jnp.sum(p, axis=-1, keepdims=True)
+        ps[h] = half(p / jnp.sum(p, axis=-1, keepdims=True))
     save(ps, p_h)
+    mark[...] = vs[0, 0:8, :]
     for c in saves:
         c.wait()
 
@@ -445,16 +449,16 @@
         (e_h.at[:, 0:D], acts.at[7]),
     ]
     loads = [pltpu.make_async_copy(a, b, lsem.at[k]) for k, (a, b) in enumerate(todo)]
+    after = {9: (5, 6, 7), 10: (8,), 8: (9,), 7: (10, 11), 6: (12, 13), 3: (14, 15, 16)}
+    ring.start(9)
+    ring.start(10)
     for c in loads[:2]:
         c.start()
-    ring.start(order[0])
-    ring.start(order[1])
-    for c in loads[2:6]:
-        c.start()
-    for m in order[2 : ring.n]:
+    ring.start(8)
+    for c in loads[2:5]:
+        c.start()
+    for m in order[3 : ring.n]:
         ring.start(m)
-    for c in loads[6:]:
-        c.start()
 
     def ready(*ks):
         for k in ks:
@@ -476,12 +480,14 @@
     def mul(g_b, m):
         out = dot_nt(g_b, ring.get(m))
         ring.done(m)
+        for k in after.get(m, ()):
+            loads[k].start()
         return out
 
     gain_rows = []
 
     def back(g, k):
-        out, gg = norm_back(g, lg[k + 1 : k + 2, :], ns[k], vs[k][:, 0:1])
+        out, gg = norm_back(g, lg[k + 1 : k + 2, :], ns[k].astype(F32), vs[k][:, 0:1])
         for t in range(10):
             gain_rows.append((10 * k + t, gg[:, 128 * t : 128 * t + 128]))
         return out
@@ -505,12 +511,13 @@
     for h in range(H):
         win = slice(WIN[h], WIN[h] + 256)
         mk = head_mask(h)
-        p = ps[h]
+        pb = ps[h]
+        p = pb.astype(F32)
         dp = dot_nt(qs[3, :, win] * half(mk), qs[2, :, win])
         ds = half(p * (dp - jnp.sum(p * dp, axis=-1, keepdims=True)) * SCALE)
         acc2[:, win] += dot(ds, qs[1, :, win]) * mk
         acc3[0, :, win] += dot_tn(ds, qs[0, :, win]) * mk
-        acc3[1, :, win] += dot_tn(half(p), qs[3, :, win]) * mk
+        acc3[1, :, win] += dot_tn(pb, qs[3, :, win]) * mk
     gw[2] = half(put(acc2, 0) + put(acc3.at[0], 80) + put(acc3.at[1], 160))
     gn = mul(half(acc2[...]), 3)
     gn = gn + mul(half(acc3[0]), 4)
@@ -532,13 +539,13 @@
     gains_o[...] = as_rows(gain_rows, 48)
 
 
-def sum_rows_body(rcv, out):
+def sum_rows_body(rcv, dw, out):
     s = half(jnp.sum(rcv[...].astype(F32), axis=0))
     for k in range(NJ):
         out[k] = s
 
 
-def dec_weights_body(mix, cot, nd, gq, out, buf, sem):
+def dec_weights_body(mix, cot, nd, gq, mark, out, buf, sem):
     g = half(dot_tn(mix[...], cot[...]))
     for i in range(NI):
         for t in range(6):
@@ -724,9 +731,9 @@
 
     g0, wsh = call(
         pack_body,
-        [((192, 640), BF, "h"), ((ROWS_I, D), BF, "h")],
+        [((192, 640), BF, "v"), ((ROWS_I, D), BF, "h")],
         [(sc, "s"), (latent_mats, "h"), (out_mats, "h"), (byte_mats, "h"), (dec_out, "h"), (latent_array, "h")],
-        [DMA((12,))],
+        [pltpu.VMEM((ROWS_I, D), BF), DMA((13,))],
         vmem=60,
         name="pack",
     )
@@ -748,7 +755,7 @@
             ((R, D), BF, "v"),
             ((R, D + 128), BF, "v"),
         ],
-        [(sc, "s")] + [(v, "h") for v in own + sib] + [(xin, "v"), (bg, "v"), (lg, "v")],
+        [(sc, "s")] + [(v, "a") for v in own + sib] + [(xin, "v"), (bg, "v"), (lg, "v")],
         [pltpu.VMEM((NJ, 192, D), BF), pltpu.VMEM((R, D), F32), DMA((33,))],
         vmem=60,
         flops=3e9,
@@ -757,7 +764,6 @@
     rcv = exchange(pay.reshape(NJ, 16, D + 128), BLK)
     (mine,) = call(combine_body, [((16, D + 128), BF, "v")], [(rcv, "v")], name="combine")
     e = lax.all_gather(mine, BLK, axis=0, tiled=True)
-    nf = lax.all_gather(nb, BLK, axis=0, tiled=True)
 
     big = (NJ, 80, D)
     res, gqin, gd, dpay, mix, nd, gq, z_h, h_h, a_h = call(
@@ -799,25 +805,26 @@
         name="forward",
     )
     rows = exchange(dpay.reshape(NJ, 16, 2 * D), BLK)
-    n_h, i_h, s_h, act_h, p_h = call(
+    n_h, i_h, s_h, act_h, p_h, mark = call(
         prepare_body,
         [
-            ((4, R, D), F32, "h"),
+            ((4, R, D), BF, "h"),
             ((4, R, 128), F32, "h"),
             ((2, R, D), F32, "h"),
             ((6, R, D), BF, "h"),
-            ((H, R, R), F32, "h"),
+            ((H, R, R), BF, "h"),
+            ((8, 128), F32, "v"),
         ],
         [(lg, "v"), (z_h, "h"), (h_h, "h"), (a_h, "h")],
         [
             pltpu.VMEM((4, R, D), F32),
             pltpu.VMEM((2, R, D), F32),
             pltpu.VMEM((2, R, D), BF),
-            pltpu.VMEM((4, R, D), F32),
+            pltpu.VMEM((4, R, D), BF),
             pltpu.VMEM((4, R, 128), F32),
             pltpu.VMEM((2, R, D), F32),
             pltpu.VMEM((6, R, D), BF),
-            pltpu.VMEM((H, R, R), F32),
+            pltpu.VMEM((H, R, R), BF),
             DMA((7,)),
             DMA((14,)),
         ],
@@ -825,18 +832,25 @@
         flops=5e9,
         name="prepare",
     )
-    (dup,) = call(sum_rows_body, [((NJ, 16, 2 * D), BF, "v")], [(rows, "v")], name="sum_rows")
-    gkv = exchange(dup, BLK).reshape(R, 2 * D)
-    mix, _, nf = lax.optimization_barrier((mix, dup, nf))
     (dw,) = call(
         dec_weights_body,
         [((NI, 1920, 128), BF, "h")],
-        [(mix, "v"), (cot, "v"), (nd, "v"), (gq, "v")],
+        [(mix, "v"), (cot, "v"), (nd, "v"), (gq, "v"), (mark, "h")],
         [pltpu.VMEM((NI, 1920, 128), BF), DMA((2,))],
         vmem=60,
         flops=4e9,
         name="dec_weights",
     )
+    (dup,) = call(
+        sum_rows_body,
+        [((NJ, 16, 2 * D), BF, "v")],
+        [(rows, "v"), (dw, "h")],
+        vmem=60,
+        name="sum_rows",
+    )
+    gkv = exchange(dup, BLK).reshape(R, 2 * D)
+    nb, _ = lax.optimization_barrier((nb, dup))
+    nf = lax.all_gather(nb, BLK, axis=0, tiled=True)
     dw = lax.psum_scatter(dw.reshape(NI * 1920, 128), BATCH, scatter_dimension=0, tiled=True)
 
     gmix, pack, g1c, lat_gain = call(
@@ -844,22 +858,22 @@
         [((R, D), BF, "v"), ((D, 1024), BF, "v"), ((R, 128), BF, "v"), ((48, 128), F32, "v")],
         [(sc, "s"), (gkv, "v"), (lg, "v")] + [(v, "h") for v in (w, e, n_h, i_h, s_h, act_h, a_h, p_h)],
         [
-            pltpu.VMEM((4,) + big, BF),
-            pltpu.VMEM((4, R, D), F32),
+            pltpu.VMEM((5,) + big, BF),
+            pltpu.VMEM((4, R, D), BF),
             pltpu.VMEM((4, R, 128), F32),
             pltpu.VMEM((2, R, D), F32),
             pltpu.VMEM((8, R, D), BF),
             pltpu.VMEM((4, R, D), BF),
-            pltpu.VMEM((H, R, R), F32),
+            pltpu.VMEM((H, R, R), BF),
             pltpu.VMEM((R, D), F32),
             pltpu.VMEM((R, D), F32),
             pltpu.VMEM((2, R, D), F32),
             pltpu.VMEM((R, D), BF),
             pltpu.VMEM((8, R, 256), BF),
-            DMA((4, 2)),
+            DMA((5, 2)),
             DMA((17,)),
         ],
-        vmem=58,
+        vmem=60,
         flops=1.6e10,
         name="lat_backward",
     )

time: 392 us -> 372 us (0.949)
  blocking collectives: 111 us -> 87.8 us
  waiting for transfers between devices: 98.8 us -> 120 us
  Pallas kernels: 123 us -> 104 us
    all_to_all x3, blocking collectives: 87.6 us -> 63.3 us  [exchange(): lax.all_to_all(flat, axes, split_axis=0, concat_axis=0, tiled=True)]
    all_to_all x2, waiting for transfers between devices: 21.9 us -> 45.7 us  [exchange(): lax.all_to_all(flat, axes, split_axis=0, concat_axis=0, tiled=True)]
    pallas_call x11, Pallas kernels: 123 us -> 104 us  [call(): pl.pallas_call(body, out_shape=[jax.ShapeDtypeStruct(s, t) for s, t, _ in...]
  transfers between devices with their start and end apart: 16 -> 16, of which waited for: 10 -> 10; matrix products, arithmetic and copies ran while one was open for 0% -> 0% of each run, Pallas kernels for 26% -> 15%
where the time goes in v1:
time: 372 us; the launch traced here: 365 us
  waiting for transfers between devices  120 us (32%)
  Pallas kernels  104 us (28%)
  blocking collectives  87.8 us (24%)
  starting transfers between devices  32 us (9%)
  between operations  14.8 us (4%)
  local copies, waits for them, and re-layouts  6.2 us (2%)
    pallas_call x11, Pallas kernels, call(): pl.pallas_call(body, out_shape=[jax.ShapeDtypeStruct(s, t) for s, t, _ in...  104 us
    all_to_all x3, blocking collectives, exchange(): lax.all_to_all(flat, axes, split_axis=0, concat_axis=0, tiled=True)  63.3 us
    all_to_all x2, waiting for transfers between devices, exchange(): lax.all_to_all(flat, axes, split_axis=0, concat_axis=0, tiled=True)  45.7 us
    all_gather x1, waiting for transfers between devices, shards(): w = lax.all_gather(wsh, AXES, axis=0, tiled=True).reshape(NI, NJ, ROWS_I, D)  42.3 us
    ppermute x6, waiting for transfers between devices, step(): return [lax.ppermute(v, AXES, along(stage, d)) for d in (1, 2, 3)]  29.5 us
    all_gather x1, blocking collectives, shards(): e = lax.all_gather(mine, BLK, axis=0, tiled=True)  24.5 us
    all_to_all x2, starting transfers between devices, exchange(): lax.all_to_all(flat, axes, split_axis=0, concat_axis=0, tiled=True)  15.4 us
    ppermute x6, starting transfers between devices, step(): return [lax.ppermute(v, AXES, along(stage, d)) for d in (1, 2, 3)]  8.75 us
  transfers between devices with their start and end apart: 16, of which 10 were waited for; matrix products, arithmetic and copies ran while one was open for 0% of the time, Pallas kernels for 15%

profile of v1, /device:TPU:1, one launch (start us, length us, event | category | flops | bytes accessed | tf_op | source)
XLA Modules:
  0.0 365.5 jit_solution(5016448046420257755)
XLA Ops:
  8.5 3.3 pack.1
  11.9 4.7 %collective-permute-start.2 = (bf16[192,640]{1,0:T(8,128)(2,1)}, bf16[192,640]{1,0:T(8,128)(2,1)S(1)}, u32[]{:S(2)}, u32[]{:S(2)}) collective-permute-start(bf16[192,640]{1,0:T(8,128)(2,1)} %get-tuple-element.50), channel_id=1, source_target_pairs={{0,12},{1,13},{2,14},{3,15},{4,0},{5,1},{6,2},{7,3},{8,4},{9,5},{1... | collective-permute-start | bytes 737288 | tf_op jit(solution)/shard_map/ppermute | solution.py:743
  17.2 5.4 %collective-permute-done.2 = bf16[192,640]{1,0:T(8,128)(2,1)S(1)} collective-permute-done((bf16[192,640]{1,0:T(8,128)(2,1)}, bf16[192,640]{1,0:T(8,128)(2,1)S(1)}, u32[]{:S(2)}, u32[]{:S(2)}) %collective-permute-start.2) | collective-permute-done | bytes 245792 | tf_op jit(solution)/shard_map/ppermute | solution.py:743
  30.4 2.8 collective-permute-start.6
  33.2 20.0 %collective-permute-done.5.t3 = bf16[4,192,640]{2,1,0:T(8,128)(2,1)S(1)} collective-permute-done((bf16[4,192,640]{2,1,0:T(8,128)(2,1)S(1)}, bf16[4,192,640]{2,1,0:T(8,128)(2,1)S(1)}, u32[]{:S(2)}, u32[]{:S(2)}) %collective-permute-start.5) | collective-permute-done | bytes 983072 | tf_op jit(solution)/shard_map/ppermute | solution.py:743
  53.2 2.4 collective-permute-start.9
  56.6 2.4 collective-permute-start.7
  62.2 9.1 %enc.1 = (bf16[16,192,1280]{2,1,0:T(8,128)(2,1)}, bf16[128,768]{1,0:T(8,128)(2,1)}, bf16[128,1280]{1,0:T(8,128)(2,1)}, bf16[128,1280]{1,0:T(8,128)(2,1)}, bf16[2...) custom-call(s32[6]{0:T(128)} %stack.38.sc, bf16[4,192,640]{2,1,0:T(8,128)(2,1)} %copy-done.6, ...), custom_call_target="tpu_custom_call" | custom-call | flops 3000000000 | bytes 4194304 | tf_op jit(solution)/shard_map/enc/pallas_call | solution.py:113
  71.2 18.0 %all_to_all.38.rcv = bf16[16,16,1408]{2,1,0:T(8,128)(2,1)S(1)} all-to-all(bf16[16,16,1408]{2,1,0:T(8,128)(2,1)} %bitcast.25), channel_id=1, replica_groups=mesh['y'=4,'core'=2,'x'=4,'z'=4] {'x','z'}, dimensions={0} | all-to-all | bytes 1441792 | tf_op jit(solution)/shard_map/all_to_all | solution.py:723
  89.8 24.5 %all_gather.9.e_h = bf16[256,1408]{1,0:T(8,128)(2,1)} all-gather(bf16[16,1408]{1,0:T(8,128)(2,1)S(1)} %combine.1), channel_id=1, replica_groups=mesh['y'=4,'core'=2,'x'=4,'z'=4] {'x','z'}, dimensions={0}, use_global_device_ids=true | all-gather | bytes 765952 | tf_op jit(solution)/shard_map/all_gather | solution.py:766
  114.3 42.3 %all-gather.3.cloned.1.call-done = bf16[16384,1280]{1,0:T(8,128)(2,1)} async-done(((bf16[128,1280]{1,0:T(8,128)(2,1)}), bf16[16384,1280]{1,0:T(8,128)(2,1)}) %all-gather.3.cloned.1.call-update) | async-done | bytes 41943056 | tf_op jit(solution)/shard_map/all_gather | solution.py:740
  156.6 30.0 %forward.1 = (bf16[128,768]{1,0:T(8,128)(2,1)}, f32[128,768]{1,0:T(8,128)}, f32[1,768]{1,0:T(1,128)}, bf16[256,2560]{1,0:T(8,128)(2,1)}, bf16[128,1280]{1,0:T(8,...) custom-call(bf16[128,768]{1,0:T(8,128)(2,1)} %bitcast.35, ...), custom_call_target="tpu_custom_call" | custom-call | flops 15000000512 | bytes 4194304 | tf_op jit(solution)/shard_map/forward/pallas_call | solution.py:113
  186.6 9.3 %prepare.1 = (bf16[4,256,1280]{2,1,0:T(8,128)(2,1)}, f32[4,256,128]{2,1,0:T(8,128)}, f32[2,256,1280]{2,1,0:T(8,128)}, bf16[6,256,1280]{2,1,0:T(8,128)(2,1)}, bf1...) custom-call(f32[5,1280]{1,0:T(8,128)} %lg.11, f32[4,256,1280]{2,1,0:T(8,128)} %get-tuple-element.60.z_h, ...), custom_call_target="tpu_custom_call" | custom-call | flops 5000000000 | bytes 4194304 | tf_op jit(solution)/shard_map/prepare/pallas_call | solution.py:113
  196.0 4.1 %dec_weights.1.dw = bf16[8,1920,128]{2,1,0:T(8,128)(2,1)} custom-call(bf16[128,1280]{1,0:T(8,128)(2,1)} %get-tuple-element.57.mix, bf16[128,768]{1,0:T(8,128)(2,1)} %bitcast.37, bf16[128,768]{1,0:T(8,128)(2,1)} %get-tuple-element.58.nd, bf16[128,1280]{1,0:T(8,128)(2,1)} %get-tuple-element.59.gq, f32[8,128]{1,0:T(8,128)} %get-tuple-element.63.mark), custom_call_target="tpu_custom_call" | custom-call | flops 4000000000 | bytes 4194304 | tf_op jit(solution)/shard_map/dec_weights/pallas_call | solution.py:113
  201.4 23.5 %all_to_all.39.rcv = bf16[16,16,2560]{2,1,0:T(8,128)(2,1)} all-to-all(bf16[16,16,2560]{2,1,0:T(8,128)(2,1)S(1)} %bitcast.23), channel_id=1, replica_groups=mesh['y'=4,'core'=2,'x'=4,'z'=4] {'x','z'}, dimensions={0} | all-to-all | bytes 2621440 | tf_op jit(solution)/shard_map/all_to_all | solution.py:723
  224.9 2.6 sum_rows.1
  227.6 21.7 %all_to_all.40 = bf16[16,16,2560]{2,1,0:T(8,128)(2,1)} all-to-all(bf16[16,16,2560]{2,1,0:T(8,128)(2,1)} %sum_rows.1), channel_id=1, replica_groups=mesh['y'=4,'core'=2,'x'=4,'z'=4] {'x','z'}, dimensions={0} | all-to-all | bytes 2621440 | tf_op jit(solution)/shard_map/all_to_all | solution.py:723
  249.3 29.4 %lat_backward.1 = (bf16[256,1280]{1,0:T(8,128)(2,1)}, bf16[1280,1024]{1,0:T(8,128)(2,1)}, bf16[256,128]{1,0:T(8,128)(2,1)}, f32[48,128]{1,0:T(8,128)}) custom-call(s32[6]{0:T(128)} %stack.38.sc, bf16[256,2560]{1,0:T(8,128)(2,1)} %bitcast.24, f32[5,1280]{1,0:T(8,128)} %lg.11, bf16[8,16,128,1280]{3,2,1,0:T(8,128)(2,1)} %bitcast.33, ...), custom_call_target="tpu_custom_call" | custom-call | flops 16000000000 | bytes 4194304 | tf_op jit(solution)/shard_map/lat_backward/pallas_call | solution.py:113
  278.8 10.0 %enc_back.1 = (f32[128,768]{1,0:T(8,128)}, bf16[16,688,128]{2,1,0:T(8,128)(2,1)}) custom-call(s32[6]{0:T(128)} %stack.38.sc, bf16[128,768]{1,0:T(8,128)(2,1)} %bitcast.31, f32[2,768]{1,0:T(2,128)} %bg.5, f32[5,1280]{1,0:T(8,128)} %lg.11, f32[1,768]{1,0:T(1,128)} %get-tuple-element.55.gd, bf16[256,1280]{1,0:T(8,128)(2,1)} %get-tuple-element.69.gmix_h, ...), custom_call_target="tpu_custom_call" | custom-call | flops 3000000000 | bytes 4194304 | tf_op jit(solution)/shard_map/enc_back/pallas_call | solution.py:113
  288.8 4.6 %all-to-all-start.3 = ((bf16[16,688,128]{2,1,0:T(8,128)(2,1)}), bf16[16,688,128]{2,1,0:T(8,128)(2,1)S(1)}, u32[]{:S(2)}, u32[]{:S(2)}) async-start(bf16[16,688,128]{2,1,0:T(8,128)(2,1)} %get-tuple-element.75), calls=%async_computation.4 | async-start | bytes 5636096 | tf_op jit(solution)/shard_map/all_to_all | solution.py:723
  293.4 32.3 %all-to-all-done.3.rcv = bf16[16,688,128]{2,1,0:T(8,128)(2,1)S(1)} async-done(((bf16[16,688,128]{2,1,0:T(8,128)(2,1)}), bf16[16,688,128]{2,1,0:T(8,128)(2,1)S(1)}, u32[]{:S(2)}, u32[]{:S(2)}) %all-to-all-start.3) | async-done | bytes 2818080 | tf_op jit(solution)/shard_map/all_to_all | solution.py:723
  325.8 4.2 %tail_one.1 = (bf16[8,464,128]{2,1,0:T(8,128)(2,1)S(1)}, f32[160,48]{1,0:T(8,128)S(1)}, f32[96,80]{1,0:T(8,128)S(1)}) custom-call(bf16[16,688,128]{2,1,0:T(8,128)(2,1)S(1)} %all-to-all-done.3.rcv, bf16[2048,768]{1,0:T(8,128)(2,1)} %all-gather.5.cloned.1.call-done.nf_h, bf16[16,192,1280]{2,1,0:T(8,128)(2,1)} %get-tuple-element.52.g_all, ...), custom_call_target="tpu_custom_call" | custom-call | bytes 4194304 | tf_op jit(solution)/shard_map/tail_one/pallas_call | solution.py:113
  331.0 10.8 %all-to-all-start.4 = ((bf16[8,464,128]{2,1,0:T(8,128)(2,1)}), bf16[8,464,128]{2,1,0:T(8,128)(2,1)S(1)}, u32[]{:S(2)}, u32[]{:S(2)}) async-start(bf16[8,464,128]{2,1,0:T(8,128)(2,1)} %copy-done), calls=%async_computation.5 | async-start | bytes 1900544 | tf_op jit(solution)/shard_map/all_to_all | solution.py:723
  342.4 13.3 %all-to-all-done.4.rcv = bf16[8,464,128]{2,1,0:T(8,128)(2,1)S(1)} async-done(((bf16[8,464,128]{2,1,0:T(8,128)(2,1)}), bf16[8,464,128]{2,1,0:T(8,128)(2,1)S(1)}, u32[]{:S(2)}, u32[]{:S(2)}) %all-to-all-start.4) | async-done | bytes 950304 | tf_op jit(solution)/shard_map/all_to_all | solution.py:723
  (60 shorter events, 19.9 us)
Async XLA Ops:
  7.2 149.4 %all-gather.3.cloned.1.call-start = ((), (), s32[]{:S(2)}) async-start(), calls=%async_computation.7 | async-start | bytes 42270720 | tf_op jit(solution)/shard_map/all_gather | solution.py:740
  11.8 267.0 %reduce-scatter.3.cloned.1.call-start = ((), (), s32[]{:S(2)}) async-start(), calls=%async_computation.8 | async-start | bytes 4423680 | tf_op jit(solution)/shard_map/reduce_scatter | solution.py:854
  11.9 10.7 %collective-permute-start.2 = (bf16[192,640]{1,0:T(8,128)(2,1)}, bf16[192,640]{1,0:T(8,128)(2,1)S(1)}, u32[]{:S(2)}, u32[]{:S(2)}) collective-permute-start(bf16[192,640]{1,0:T(8,128)(2,1)} %get-tuple-element.50), channel_id=1, source_target_pairs={{0,12},{1,13},{2,14},{3,15},{4,0},{5,1},{6,2},{7,3},{8,4},{9,5},{1... | collective-permute-start | bytes 737288 | tf_op jit(solution)/shard_map/ppermute | solution.py:743
  16.5 7.1 %collective-permute-start.1 = (bf16[192,640]{1,0:T(8,128)(2,1)}, bf16[192,640]{1,0:T(8,128)(2,1)S(1)}, u32[]{:S(2)}, u32[]{:S(2)}) collective-permute-start(bf16[192,640]{1,0:T(8,128)(2,1)} %get-tuple-element.50), channel_id=1, source_target_pairs={{0,8},{1,9},{2,10},{3,11},{4,12},{5,13},{6,14},{7,15},{8,0},{9,1},... | collective-permute-start | bytes 737288 | tf_op jit(solution)/shard_map/ppermute | solution.py:743
  16.5 9.4 %collective-permute-start = (bf16[192,640]{1,0:T(8,128)(2,1)}, bf16[192,640]{1,0:T(8,128)(2,1)S(1)}, u32[]{:S(2)}, u32[]{:S(2)}) collective-permute-start(bf16[192,640]{1,0:T(8,128)(2,1)} %get-tuple-element.50), channel_id=1, source_target_pairs={{0,4},{1,5},{2,6},{3,7},{4,8},{5,9},{6,10},{7,11},{8,12},{9,13},{1... | collective-permute-start | bytes 737288 | tf_op jit(solution)/shard_map/ppermute | solution.py:743
  27.0 35.1 %copy-start.6 = (bf16[4,192,640]{2,1,0:T(8,128)(2,1)}, bf16[4,192,640]{2,1,0:T(8,128)(2,1)S(1)}, u32[]{:S(2)}) copy-start(bf16[4,192,640]{2,1,0:T(8,128)(2,1)S(1)} %pad_maximum_fusion.t0) | copy-start | bytes 2949124
  27.0 26.2 %collective-permute-start.5 = (bf16[4,192,640]{2,1,0:T(8,128)(2,1)S(1)}, bf16[4,192,640]{2,1,0:T(8,128)(2,1)S(1)}, u32[]{:S(2)}, u32[]{:S(2)}) collective-permute-start(bf16[4,192,640]{2,1,0:T(8,128)(2,1)S(1)} %pad_maximum_fusion.t0), channel_id=1, source_target_pairs={{0,3},{1,0},{2,1},{3,2},{4,7},{5,4},{6,5},{7,6},{8,11},{9,8},{10,9... | collective-permute-start | bytes 2949128 | tf_op jit(solution)/shard_map/ppermute | solution.py:743
  29.3 26.4 %collective-permute-start.4 = (bf16[4,192,640]{2,1,0:T(8,128)(2,1)S(1)}, bf16[4,192,640]{2,1,0:T(8,128)(2,1)S(1)}, u32[]{:S(2)}, u32[]{:S(2)}) collective-permute-start(bf16[4,192,640]{2,1,0:T(8,128)(2,1)S(1)} %pad_maximum_fusion.t0), channel_id=1, source_target_pairs={{0,2},{1,3},{2,0},{3,1},{4,6},{5,7},{6,4},{7,5},{8,10},{9,11},{10,... | collective-permute-start | bytes 2949128 | tf_op jit(solution)/shard_map/ppermute | solution.py:743
  29.8 26.8 %collective-permute-start.3 = (bf16[4,192,640]{2,1,0:T(8,128)(2,1)S(1)}, bf16[4,192,640]{2,1,0:T(8,128)(2,1)S(1)}, u32[]{:S(2)}, u32[]{:S(2)}) collective-permute-start(bf16[4,192,640]{2,1,0:T(8,128)(2,1)S(1)} %pad_maximum_fusion.t0), channel_id=1, source_target_pairs={{0,1},{1,2},{2,3},{3,0},{4,5},{5,6},{6,7},{7,4},{8,9},{9,10},{10,1... | collective-permute-start | bytes 2949128 | tf_op jit(solution)/shard_map/ppermute | solution.py:743
  30.4 28.6 %collective-permute-start.6 = (bf16[4,192,640]{2,1,0:T(8,128)(2,1)S(1)}, bf16[4,192,640]{2,1,0:T(8,128)(2,1)S(1)}, u32[]{:S(2)}, u32[]{:S(2)}) collective-permute-start(bf16[4,192,640]{2,1,0:T(8,128)(2,1)S(1)} %pad_maximum_fusion.t0), channel_id=1, source_target_pairs={{0,16},{1,17},{2,18},{3,19},{4,20},{5,21},{6,22},{7,23},{8,24},{9,... | collective-permute-start | bytes 2949128 | tf_op jit(solution)/shard_map/ppermute | solution.py:747
  53.2 8.9 %copy-start.7 = (bf16[4,192,640]{2,1,0:T(8,128)(2,1)}, bf16[4,192,640]{2,1,0:T(8,128)(2,1)S(1)}, u32[]{:S(2)}) copy-start(bf16[4,192,640]{2,1,0:T(8,128)(2,1)S(1)} %collective-permute-done.5.t3) | copy-start | bytes 2949124
  53.2 5.8 %collective-permute-start.9 = (bf16[4,192,640]{2,1,0:T(8,128)(2,1)S(1)}, bf16[4,192,640]{2,1,0:T(8,128)(2,1)S(1)}, u32[]{:S(2)}, u32[]{:S(2)}) collective-permute-start(bf16[4,192,640]{2,1,0:T(8,128)(2,1)S(1)} %collective-permute-done.5.t3), channel_id=1, source_target_pairs={{0,16},{1,17},{2,18},{3,19},{4,20},{5,21},{6,22},{7,23},{8,24},{9,... | collective-permute-start | bytes 2949128 | tf_op jit(solution)/shard_map/ppermute | solution.py:747
  55.7 6.5 %copy-start.8 = (bf16[4,192,640]{2,1,0:T(8,128)(2,1)}, bf16[4,192,640]{2,1,0:T(8,128)(2,1)S(1)}, u32[]{:S(2)}) copy-start(bf16[4,192,640]{2,1,0:T(8,128)(2,1)S(1)} %collective-permute-done.4.t2) | copy-start | bytes 2949124
  55.7 3.6 collective-permute-start.8
  56.6 5.5 %copy-start.9 = (bf16[4,192,640]{2,1,0:T(8,128)(2,1)}, bf16[4,192,640]{2,1,0:T(8,128)(2,1)S(1)}, u32[]{:S(2)}) copy-start(bf16[4,192,640]{2,1,0:T(8,128)(2,1)S(1)} %collective-permute-done.3.t1) | copy-start | bytes 2949124
  56.6 4.6 %collective-permute-start.7 = (bf16[4,192,640]{2,1,0:T(8,128)(2,1)S(1)}, bf16[4,192,640]{2,1,0:T(8,128)(2,1)S(1)}, u32[]{:S(2)}, u32[]{:S(2)}) collective-permute-start(bf16[4,192,640]{2,1,0:T(8,128)(2,1)S(1)} %collective-permute-done.3.t1), channel_id=1, source_target_pairs={{0,16},{1,17},{2,18},{3,19},{4,20},{5,21},{6,22},{7,23},{8,24},{9,... | collective-permute-start | bytes 2949128 | tf_op jit(solution)/shard_map/ppermute | solution.py:747
  59.0 2.2 copy-start.10
  200.1 93.4 %all-gather.5.cloned.1.call-start = ((), (), s32[]{:S(2)}) async-start(), calls=%async_computation.9 | async-start | bytes 3342336 | tf_op jit(solution)/shard_map/all_gather | solution.py:853
  227.5 114.9 %reduce-scatter.5.cloned.1.call-start = ((), (), s32[]{:S(2)}) async-start(), calls=%async_computation.10 | async-start | bytes 2949120 | tf_op jit(solution)/shard_map/reduce_scatter | solution.py:880
  288.8 37.0 %copy-start.2 = (f32[5,1280]{1,0:T(8,128)S(1)}, f32[5,1280]{1,0:T(8,128)}, u32[]{:S(2)}) copy-start(f32[5,1280]{1,0:T(8,128)} %lg.11) | copy-start | bytes 76804
  288.8 37.0 %copy-start.3 = (bf16[256,128]{1,0:T(8,128)(2,1)S(1)}, bf16[256,128]{1,0:T(8,128)(2,1)}, u32[]{:S(2)}) copy-start(bf16[256,128]{1,0:T(8,128)(2,1)} %get-tuple-element.79.g1c) | copy-start | bytes 196612
  288.8 37.0 %copy-start.4 = (f32[48,128]{1,0:T(8,128)S(1)}, f32[48,128]{1,0:T(8,128)}, u32[]{:S(2)}) copy-start(f32[48,128]{1,0:T(8,128)} %get-tuple-element.78.lat_gain) | copy-start | bytes 73732
  288.8 37.0 %all-to-all-start.3 = ((bf16[16,688,128]{2,1,0:T(8,128)(2,1)}), bf16[16,688,128]{2,1,0:T(8,128)(2,1)S(1)}, u32[]{:S(2)}, u32[]{:S(2)}) async-start(bf16[16,688,128]{2,1,0:T(8,128)(2,1)} %get-tuple-element.75), calls=%async_computation.4 | async-start | bytes 5636096 | tf_op jit(solution)/shard_map/all_to_all | solution.py:723
  331.0 24.8 %all-to-all-start.4 = ((bf16[8,464,128]{2,1,0:T(8,128)(2,1)}), bf16[8,464,128]{2,1,0:T(8,128)(2,1)S(1)}, u32[]{:S(2)}, u32[]{:S(2)}) async-start(bf16[8,464,128]{2,1,0:T(8,128)(2,1)} %copy-done), calls=%async_computation.5 | async-start | bytes 1900544 | tf_op jit(solution)/shard_map/all_to_all | solution.py:723
  (6 other events, 8.3 us)
Sparse Core Ops, SparseCore 0:
  11.9 144.5 all-gather.2
  200.2 33.8 reduce-scatter.2
  236.3 49.4 all-gather.4
  288.1 31.3 reduce-scatter.4

commit v2 on v1

--- a/solution.py
+++ b/solution.py
@@ -539,13 +539,13 @@
     gains_o[...] = as_rows(gain_rows, 48)
 
 
-def sum_rows_body(rcv, dw, out):
+def sum_rows_body(rcv, mark, out):
     s = half(jnp.sum(rcv[...].astype(F32), axis=0))
     for k in range(NJ):
         out[k] = s
 
 
-def dec_weights_body(mix, cot, nd, gq, mark, out, buf, sem):
+def dec_weights_body(mix, cot, nd, gq, out, buf, sem):
     g = half(dot_tn(mix[...], cot[...]))
     for i in range(NI):
         for t in range(6):
@@ -573,19 +573,10 @@
         v = jnp.concatenate([chunk[960 + 96 * t : 960 + 96 * t + 96, :].astype(F32), fill], axis=0)
         tb[128 * t : 128 * t + 128, :] = v.T
     for j in range(NJ):
-        pay[j, 512:560, :] = half(td[48 * j : 48 * j + 48, 0:128])
-        pay[j, 560:608, :] = half(td[48 * j : 48 * j + 48, 128:256])
-        pay[j, 608:688, :] = half(tb[80 * j : 80 * j + 80, :])
-
-
-def unspread(s, dec_o, bq_o):
-    fill = jnp.zeros((80, 128), F32)
-    a = jnp.concatenate([s[0:48], fill], axis=0).T
-    b = jnp.concatenate([s[48:96], fill], axis=0).T
-    dec_o[0:128, :] = a[:, 0:48]
-    dec_o[128:160, :] = b[0:32, 0:48]
-    c = jnp.concatenate([s[96:176], fill[0:48]], axis=0).T
-    bq_o[...] = c[0:96, 0:80]
+        tail = pltpu.roll(td[48 * j : 48 * j + 48, 128:256], 96, 1)
+        pay[j, 512:560, :] = half(tb[80 * j : 80 * j + 48, :] + tail)
+        pay[j, 560:592, :] = half(tb[80 * j + 48 : 80 * j + 80, :])
+        pay[j, 592:640, :] = half(td[48 * j : 48 * j + 48, 0:128])
 
 
 def enc_back_body(
@@ -658,30 +649,42 @@
     nq = half(norm(z0b[...].reshape(R, D).astype(F32))[0] * lg[0:1, :])
     a = jnp.concatenate([sums[160:240], fill], axis=0).T
     b = jnp.concatenate([sums[240:320], fill], axis=0).T
-    w0 = half(dot_tn(nq, half(jnp.concatenate([a, b], axis=0))))
+    w0 = dot_tn(nq, half(jnp.concatenate([a, b], axis=0)))
     a = jnp.concatenate([sums[0:80], fill], axis=0).T
     b = jnp.concatenate([sums[80:160], fill], axis=0).T
     gz = half(jnp.concatenate([a, b], axis=0) + g1c[...].astype(F32))
     gains = jnp.sum(rcv[:, 480:512, :].astype(F32), axis=0)
     gains = half(jnp.concatenate([gains, lat_gain[...]], axis=0))
     loads[0].wait()
-    wt = half(dot(left[...], nf[...]).T)
+    wt = dot(left[...], nf[...]).T
+    lane = lanes(128)
+    key, value = wt[:, 0:128], wt[:, 128:256]
+    one = half(jnp.where(lane < 80, key, pltpu.roll(value, 80, 1)))
+    other = pltpu.roll(value, 32, 1)
     for i in range(NI):
-        out[i, 0:160, :] = w0[160 * i : 160 * i + 160, :]
+        r = 96 * i
+        beside = jnp.concatenate([other[r : r + 96, :], jnp.zeros((64, 128), F32)], axis=0)
+        out[i, 0:160, :] = half(jnp.where(lane < 80, w0[160 * i : 160 * i + 160, :], beside))
         out[i, 160:192, :] = gz[32 * i : 32 * i + 32, :]
-        out[i, 192:288, :] = wt[96 * i : 96 * i + 96, 0:128]
-        out[i, 288:384, :] = wt[96 * i : 96 * i + 96, 128:256]
-        out[i, 384:464, :] = gains
-    unspread(jnp.sum(rcv[:, 512:688, :].astype(F32), axis=0), dec_o, bq_o)
-
-
-def tail_two_body(rcv, pack, arr_o, lm_o, om_o, wkv_o, lat_o, byte_o):
+        out[i, 192:288, :] = one[r : r + 96, :]
+        out[i, 288:368, :] = gains
+    s = jnp.sum(rcv[:, 512:640, :].astype(F32), axis=0)
+    bq_o[...] = s[0:80, 0:96]
+    dec_o[:, 0:128] = s[80:128]
+    dec_o[:, 128:160] = pltpu.roll(s[0:48], 32, 1)[:, 0:32]
+
+
+def tail_two_body(rcv, pack, bq, arr_o, lm_o, om_o, bm_o, lat_o, byte_o):
     sums = jnp.sum(rcv[...].astype(F32), axis=0)
     lm_o[0] = sums[0:160, 0:80]
     arr_o[...] = sums[160:192, 0:80]
-    wkv_o[0] = sums[192:288, 0:80]
-    wkv_o[1] = sums[288:384, 0:80]
-    g = sums[384:464]
+    lane = lanes(128)
+    value = jnp.where(lane < 48, pltpu.roll(sums[192:288], 48, 1), pltpu.roll(sums[0:96], 96, 1))
+    fill = jnp.zeros((32, 128), F32)
+    bm_o[0] = jnp.concatenate([sums[192:288], fill], axis=0).T[0:80, 0:96]
+    bm_o[1] = jnp.concatenate([value, fill], axis=0).T[0:80, 0:96]
+    bm_o[2] = bq[...]
+    g = sums[288:368]
     for t in range(6):
         for b in range(2):
             byte_o[b : b + 1, 128 * t : 128 * t + 128] = g[6 * b + t : 6 * b + t + 1, :]
@@ -782,7 +785,7 @@
         ],
         [(qin, "v"), (cot, "v"), (bg, "v"), (lg, "v"), (e, "h"), (g_all, "h"), (w, "h")],
         [
-            pltpu.VMEM((5,) + big, BF),
+            pltpu.VMEM((4,) + big, BF),
             pltpu.VMEM((R, D), BF),
             pltpu.VMEM((NJ, 16, D), BF),
             pltpu.VMEM((4, R, D), F32),
@@ -796,11 +799,11 @@
             pltpu.VMEM((N, D), F32),
             pltpu.VMEM((N, D), F32),
             pltpu.VMEM((2, R, D), F32),
-            DMA((5, 2)),
+            DMA((4, 2)),
             DMA((10,)),
             DMA((5,)),
         ],
-        vmem=58,
+        vmem=54,
         flops=1.5e10,
         name="forward",
     )
@@ -828,25 +831,21 @@
             DMA((7,)),
             DMA((14,)),
         ],
-        vmem=60,
+        vmem=36,
         flops=5e9,
         name="prepare",
     )
     (dw,) = call(
         dec_weights_body,
         [((NI, 1920, 128), BF, "h")],
-        [(mix, "v"), (cot, "v"), (nd, "v"), (gq, "v"), (mark, "h")],
+        [(mix, "v"), (cot, "v"), (nd, "v"), (gq, "v")],
         [pltpu.VMEM((NI, 1920, 128), BF), DMA((2,))],
         vmem=60,
         flops=4e9,
         name="dec_weights",
     )
     (dup,) = call(
-        sum_rows_body,
-        [((NJ, 16, 2 * D), BF, "v")],
-        [(rows, "v"), (dw, "h")],
-        vmem=60,
-        name="sum_rows",
+        sum_rows_body, [((NJ, 16, 2 * D), BF, "v")], [(rows, "v"), (mark, "h")], vmem=12, name="sum_rows"
     )
     gkv = exchange(dup, BLK).reshape(R, 2 * D)
     nb, _ = lax.optimization_barrier((nb, dup))
@@ -874,13 +873,13 @@
             DMA((17,)),
         ],
         vmem=60,
-        flops=1.6e10,
+        flops=8e10,
         name="lat_backward",
     )
     pack = lax.psum_scatter(pack, BATCH, scatter_dimension=0, tiled=True)
     gin, epay = call(
         enc_back_body,
-        [((N, DI), F32, "v"), ((NJ, 688, 128), BF, "v")],
+        [((N, DI), F32, "v"), ((NJ, 640, 128), BF, "v")],
         [(sc, "s"), (xin, "v"), (bg, "v"), (lg, "v"), (gd, "v")]
         + [(v, "h") for v in (gmix, e, q_b, k_b, v_b, g_all, dw)],
         [
@@ -898,34 +897,34 @@
             pltpu.VMEM((D, 128), F32),
             DMA((7,)),
         ],
-        vmem=56,
+        vmem=58,
         flops=3e9,
         name="enc_back",
     )
     r1 = exchange(epay, BLK)
     p2, dec_grad, bq_grad = call(
         tail_one_body,
-        [((NI, 464, 128), BF, "v"), ((160, 48), F32, "v"), ((96, 80), F32, "v")],
+        [((NI, 368, 128), BF, "v"), ((48, 160), F32, "v"), ((80, 96), F32, "v")],
         [(r1, "v"), (nf, "h"), (g_all, "h"), (lg, "v"), (lat_gain, "v"), (g1c, "v")],
         [pltpu.VMEM((NJ * N, DI), BF), pltpu.VMEM((NJ, 16, D), BF), pltpu.VMEM((256, 2048), BF), DMA((2,))],
         name="tail_one",
     )
     r2 = exchange(p2, BATCH)
-    arr, lm, om, wkv, lat_gains, byte_gain = call(
+    arr, lm, om, byte_grads, lat_gains, byte_gain = call(
         tail_two_body,
         [
             ((32, 80), F32, "v"),
             ((10, 160, 80), F32, "v"),
             ((2, 160, 80), F32, "v"),
-            ((2, 96, 80), F32, "v"),
+            ((3, 80, 96), F32, "v"),
             ((5, D), F32, "v"),
             ((2, DI), F32, "v"),
         ],
-        [(r2, "v"), (pack, "v")],
+        [(r2, "v"), (pack, "v"), (bq_grad, "v")],
         name="tail_two",
     )
-    byte_grads = jnp.concatenate([wkv, bq_grad[None]], axis=0)
-    return (res[None], gin[None], gqin[None], arr, lm, om, byte_grads, dec_grad, lat_gains, byte_gain)
+    byte_grads = jnp.swapaxes(byte_grads, 1, 2)
+    return (res[None], gin[None], gqin[None], arr, lm, om, byte_grads, dec_grad.T, lat_gains, byte_gain)
 
 
 def solution(mesh):

time: 372 us -> 358 us (0.962)
  blocking collectives: 87.8 us -> 42.2 us
  waiting for transfers between devices: 120 us -> 134 us
  starting transfers between devices: 32 us -> 43.1 us
  local copies, waits for them, and re-layouts: 6.2 us -> 13.2 us
    all_to_all x3 -> x1, blocking collectives: 63.3 us -> 18 us  [exchange(): lax.all_to_all(flat, axes, split_axis=0, concat_axis=0, tiled=True)]
    all_to_all x2 -> x4, waiting for transfers between devices: 45.7 us -> 59.1 us  [exchange(): lax.all_to_all(flat, axes, split_axis=0, concat_axis=0, tiled=True)]
    all_to_all x2 -> x4, starting transfers between devices: 15.4 us -> 26.3 us  [exchange(): lax.all_to_all(flat, axes, split_axis=0, concat_axis=0, tiled=True)]
    unnamed x30 -> x42, local copies, waits for them, and re-layouts: 5.6 us -> 12.6 us
  transfers between devices with their start and end apart: 16 -> 18, of which waited for: 10 -> 11; matrix products, arithmetic and copies ran while one was open for 0% -> 0% of each run, Pallas kernels for 15% -> 19%
where the time goes in v2:
time: 358 us; the launch traced here: 352 us
  waiting for transfers between devices  134 us (37%)
  Pallas kernels  103 us (29%)
  starting transfers between devices  43.1 us (12%)
  blocking collectives  42.2 us (12%)
  between operations  14.9 us (4%)
  local copies, waits for them, and re-layouts  13.2 us (4%)
    pallas_call x11, Pallas kernels, call(): pl.pallas_call(body, out_shape=[jax.ShapeDtypeStruct(s, t) for s, t, _ in...  103 us
    all_to_all x4, waiting for transfers between devices, exchange(): lax.all_to_all(flat, axes, split_axis=0, concat_axis=0, tiled=True)  59.1 us
    all_gather x1, waiting for transfers between devices, shards(): w = lax.all_gather(wsh, AXES, axis=0, tiled=True).reshape(NI, NJ, ROWS_I, D)  42.6 us
    ppermute x6, waiting for transfers between devices, step(): return [lax.ppermute(v, AXES, along(stage, d)) for d in (1, 2, 3)]  29.5 us
    all_to_all x4, starting transfers between devices, exchange(): lax.all_to_all(flat, axes, split_axis=0, concat_axis=0, tiled=True)  26.3 us
    all_gather x1, blocking collectives, shards(): e = lax.all_gather(mine, BLK, axis=0, tiled=True)  24.2 us
    all_to_all x1, blocking collectives, exchange(): lax.all_to_all(flat, axes, split_axis=0, concat_axis=0, tiled=True)  18 us
    unnamed x42, local copies, waits for them, and re-layouts  12.6 us
  transfers between devices with their start and end apart: 18, of which 11 were waited for; matrix products, arithmetic and copies ran while one was open for 0% of the time, Pallas kernels for 19%

profile of v2, /device:TPU:1, one launch (start us, length us, event | category | flops | bytes accessed | tf_op | source)
XLA Modules:
  0.0 351.7 jit_solution(2318606736500713356)
XLA Ops:
  8.5 3.3 pack.1
  11.9 4.7 %collective-permute-start.2 = (bf16[192,640]{1,0:T(8,128)(2,1)}, bf16[192,640]{1,0:T(8,128)(2,1)S(1)}, u32[]{:S(2)}, u32[]{:S(2)}) collective-permute-start(bf16[192,640]{1,0:T(8,128)(2,1)} %get-tuple-element.50), channel_id=1, source_target_pairs={{0,12},{1,13},{2,14},{3,15},{4,0},{5,1},{6,2},{7,3},{8,4},{9,5},{1... | collective-permute-start | bytes 737288 | tf_op jit(solution)/shard_map/ppermute | solution.py:746
  17.2 5.4 %collective-permute-done.2 = bf16[192,640]{1,0:T(8,128)(2,1)S(1)} collective-permute-done((bf16[192,640]{1,0:T(8,128)(2,1)}, bf16[192,640]{1,0:T(8,128)(2,1)S(1)}, u32[]{:S(2)}, u32[]{:S(2)}) %collective-permute-start.2) | collective-permute-done | bytes 245792 | tf_op jit(solution)/shard_map/ppermute | solution.py:746
  30.4 2.8 collective-permute-start.6
  33.2 20.0 %collective-permute-done.5.t3 = bf16[4,192,640]{2,1,0:T(8,128)(2,1)S(1)} collective-permute-done((bf16[4,192,640]{2,1,0:T(8,128)(2,1)S(1)}, bf16[4,192,640]{2,1,0:T(8,128)(2,1)S(1)}, u32[]{:S(2)}, u32[]{:S(2)}) %collective-permute-start.5) | collective-permute-done | bytes 983072 | tf_op jit(solution)/shard_map/ppermute | solution.py:746
  53.2 2.4 collective-permute-start.9
  56.6 2.4 collective-permute-start.7
  62.1 9.1 %enc.1 = (bf16[16,192,1280]{2,1,0:T(8,128)(2,1)}, bf16[128,768]{1,0:T(8,128)(2,1)}, bf16[128,1280]{1,0:T(8,128)(2,1)}, bf16[128,1280]{1,0:T(8,128)(2,1)}, bf16[2...) custom-call(s32[6]{0:T(128)} %stack.38.sc, bf16[4,192,640]{2,1,0:T(8,128)(2,1)} %copy-done.13, ...), custom_call_target="tpu_custom_call" | custom-call | flops 3000000000 | bytes 4194304 | tf_op jit(solution)/shard_map/enc/pallas_call | solution.py:113
  71.2 18.0 %all_to_all.38.rcv = bf16[16,16,1408]{2,1,0:T(8,128)(2,1)S(1)} all-to-all(bf16[16,16,1408]{2,1,0:T(8,128)(2,1)} %bitcast.24), channel_id=1, replica_groups=mesh['y'=4,'core'=2,'x'=4,'z'=4] {'x','z'}, dimensions={0} | all-to-all | bytes 1441792 | tf_op jit(solution)/shard_map/all_to_all | solution.py:726
  89.8 24.2 %all_gather.9.e_h = bf16[256,1408]{1,0:T(8,128)(2,1)} all-gather(bf16[16,1408]{1,0:T(8,128)(2,1)S(1)} %combine.1), channel_id=1, replica_groups=mesh['y'=4,'core'=2,'x'=4,'z'=4] {'x','z'}, dimensions={0}, use_global_device_ids=true | all-gather | bytes 765952 | tf_op jit(solution)/shard_map/all_gather | solution.py:769
  114.0 42.6 %all-gather.3.cloned.1.call-done = bf16[16384,1280]{1,0:T(8,128)(2,1)} async-done(((bf16[128,1280]{1,0:T(8,128)(2,1)}), bf16[16384,1280]{1,0:T(8,128)(2,1)}) %all-gather.3.cloned.1.call-update) | async-done | bytes 41943056 | tf_op jit(solution)/shard_map/all_gather | solution.py:743
  156.6 29.4 %forward.1 = (bf16[128,768]{1,0:T(8,128)(2,1)}, f32[128,768]{1,0:T(8,128)}, f32[1,768]{1,0:T(1,128)}, bf16[256,2560]{1,0:T(8,128)(2,1)}, bf16[128,1280]{1,0:T(8,...) custom-call(bf16[128,768]{1,0:T(8,128)(2,1)} %bitcast.34, ...), custom_call_target="tpu_custom_call" | custom-call | flops 15000000512 | bytes 4194304 | tf_op jit(solution)/shard_map/forward/pallas_call | solution.py:113
  186.0 3.9 %dec_weights.1 = bf16[8,1920,128]{2,1,0:T(8,128)(2,1)} custom-call(bf16[128,1280]{1,0:T(8,128)(2,1)} %get-tuple-element.70.mix, bf16[128,768]{1,0:T(8,128)(2,1)} %bitcast.36, bf16[128,768]{1,0:T(8,128)(2,1)} %get-tuple-element.71.nd, bf16[128,1280]{1,0:T(8,128)(2,1)} %get-tuple-element.72.gq), custom_call_target="tpu_custom_call" | custom-call | flops 4000000000 | bytes 4194304 | tf_op jit(solution)/shard_map/dec_weights/pallas_call | solution.py:113
  189.9 4.6 %all-to-all-start.1 = ((bf16[16,16,2560]{2,1,0:T(8,128)(2,1)}), bf16[16,16,2560]{2,1,0:T(8,128)(2,1)S(1)}, u32[]{:S(2)}, u32[]{:S(2)}) async-start(bf16[16,16,2560]{2,1,0:T(8,128)(2,1)} %bitcast.15), calls=%async_computation.1 | async-start | bytes 2621440 | tf_op jit(solution)/shard_map/all_to_all | solution.py:726
  198.3 9.7 %prepare.1 = (bf16[4,256,1280]{2,1,0:T(8,128)(2,1)S(1)}, f32[4,256,128]{2,1,0:T(8,128)S(1)}, f32[2,256,1280]{2,1,0:T(8,128)S(1)}, bf16[6,256,1280]{2,1,0:T(8,128...) custom-call(f32[5,1280]{1,0:T(8,128)S(1)} %copy-done.1, f32[4,256,1280]{2,1,0:T(8,128)} %get-tuple-element.57.z_h, ...), custom_call_target="tpu_custom_call" | custom-call | flops 5000000000 | bytes 4194304 | tf_op jit(solution)/shard_map/prepare/pallas_call | solution.py:113
  215.3 6.5 %all-to-all-start.2 = ((bf16[16,16,2560]{2,1,0:T(8,128)(2,1)}), bf16[16,16,2560]{2,1,0:T(8,128)(2,1)S(1)}, u32[]{:S(2)}, u32[]{:S(2)}) async-start(bf16[16,16,2560]{2,1,0:T(8,128)(2,1)} %sum_rows.1), calls=%async_computation.2 | async-start | bytes 2621440 | tf_op jit(solution)/shard_map/all_to_all | solution.py:726
  222.7 17.0 %all-to-all-done.2 = bf16[16,16,2560]{2,1,0:T(8,128)(2,1)S(1)} async-done(((bf16[16,16,2560]{2,1,0:T(8,128)(2,1)}), bf16[16,16,2560]{2,1,0:T(8,128)(2,1)S(1)}, u32[]{:S(2)}, u32[]{:S(2)}) %all-to-all-start.2) | async-done | bytes 1310752 | tf_op jit(solution)/shard_map/all_to_all | solution.py:726
  240.8 29.3 %lat_backward.1 = (bf16[256,1280]{1,0:T(8,128)(2,1)}, bf16[1280,1024]{1,0:T(8,128)(2,1)}, bf16[256,128]{1,0:T(8,128)(2,1)}, f32[48,128]{1,0:T(8,128)}) custom-call(s32[6]{0:T(128)} %stack.38.sc, bf16[256,2560]{1,0:T(8,128)(2,1)} %bitcast.23, f32[5,1280]{1,0:T(8,128)} %lg.11, bf16[8,16,128,1280]{3,2,1,0:T(8,128)(2,1)} %bitcast.32, ...), custom_call_target="tpu_custom_call" | custom-call | flops 80000000000 | bytes 4194304 | tf_op jit(solution)/shard_map/lat_backward/pallas_call | solution.py:113
  270.1 10.0 %enc_back.1 = (f32[128,768]{1,0:T(8,128)}, bf16[16,640,128]{2,1,0:T(8,128)(2,1)}) custom-call(s32[6]{0:T(128)} %stack.38.sc, bf16[128,768]{1,0:T(8,128)(2,1)} %bitcast.30, f32[2,768]{1,0:T(2,128)} %bg.5, f32[5,1280]{1,0:T(8,128)} %lg.11, f32[1,768]{1,0:T(1,128)} %get-tuple-element.55.gd, bf16[256,1280]{1,0:T(8,128)(2,1)} %get-tuple-element.66.gmix_h, ...), custom_call_target="tpu_custom_call" | custom-call | flops 3000000000 | bytes 4194304 | tf_op jit(solution)/shard_map/enc_back/pallas_call | solution.py:113
  280.1 4.5 %all-to-all-start.3 = ((bf16[16,640,128]{2,1,0:T(8,128)(2,1)}), bf16[16,640,128]{2,1,0:T(8,128)(2,1)S(1)}, u32[]{:S(2)}, u32[]{:S(2)}) async-start(bf16[16,640,128]{2,1,0:T(8,128)(2,1)} %get-tuple-element.75), calls=%async_computation.4 | async-start | bytes 5242880 | tf_op jit(solution)/shard_map/all_to_all | solution.py:726
  284.7 30.1 %all-to-all-done.3.rcv = bf16[16,640,128]{2,1,0:T(8,128)(2,1)S(1)} async-done(((bf16[16,640,128]{2,1,0:T(8,128)(2,1)}), bf16[16,640,128]{2,1,0:T(8,128)(2,1)S(1)}, u32[]{:S(2)}, u32[]{:S(2)}) %all-to-all-start.3) | async-done | bytes 2621472 | tf_op jit(solution)/shard_map/all_to_all | solution.py:726
  314.8 5.1 %tail_one.1 = (bf16[8,368,128]{2,1,0:T(8,128)(2,1)}, f32[48,160]{1,0:T(8,128)}, f32[80,96]{1,0:T(8,128)S(1)}) custom-call(bf16[16,640,128]{2,1,0:T(8,128)(2,1)S(1)} %all-to-all-done.3.rcv, bf16[2048,768]{1,0:T(8,128)(2,1)} %all-gather.5.cloned.1.call-done.nf_h, bf16[16,192,1280]{2,1,0:T(8,128)(2,1)} %get-tuple-element.52.g_all, f32[5,1280]{1,0:T(8,128)S(1)} %copy-done.2, ...), custom_call_target="tpu_custom_call" | custom-call | bytes 4194304 | tf_op jit(solution)/shard_map/tail_one/pallas_call | solution.py:113
  319.9 10.7 %all-to-all-start.4 = ((bf16[8,368,128]{2,1,0:T(8,128)(2,1)}), bf16[8,368,128]{2,1,0:T(8,128)(2,1)S(1)}, u32[]{:S(2)}, u32[]{:S(2)}) async-start(bf16[8,368,128]{2,1,0:T(8,128)(2,1)} %get-tuple-element.80), calls=%async_computation.5 | async-start | bytes 1507328 | tf_op jit(solution)/shard_map/all_to_all | solution.py:726
  330.6 11.9 %all-to-all-done.4.rcv = bf16[8,368,128]{2,1,0:T(8,128)(2,1)S(1)} async-done(((bf16[8,368,128]{2,1,0:T(8,128)(2,1)}), bf16[8,368,128]{2,1,0:T(8,128)(2,1)S(1)}, u32[]{:S(2)}, u32[]{:S(2)}) %all-to-all-start.4) | async-done | bytes 753696 | tf_op jit(solution)/shard_map/all_to_all | solution.py:726
  (73 shorter events, 29.2 us)
Async XLA Ops:
  7.2 149.4 %all-gather.3.cloned.1.call-start = ((), (), s32[]{:S(2)}) async-start(), calls=%async_computation.7 | async-start | bytes 42270720 | tf_op jit(solution)/shard_map/all_gather | solution.py:743
  11.8 258.3 %reduce-scatter.3.cloned.1.call-start = ((), (), s32[]{:S(2)}) async-start(), calls=%async_computation.8 | async-start | bytes 4423680 | tf_op jit(solution)/shard_map/reduce_scatter | solution.py:853
  11.9 10.7 %collective-permute-start.2 = (bf16[192,640]{1,0:T(8,128)(2,1)}, bf16[192,640]{1,0:T(8,128)(2,1)S(1)}, u32[]{:S(2)}, u32[]{:S(2)}) collective-permute-start(bf16[192,640]{1,0:T(8,128)(2,1)} %get-tuple-element.50), channel_id=1, source_target_pairs={{0,12},{1,13},{2,14},{3,15},{4,0},{5,1},{6,2},{7,3},{8,4},{9,5},{1... | collective-permute-start | bytes 737288 | tf_op jit(solution)/shard_map/ppermute | solution.py:746
  16.5 7.1 %collective-permute-start.1 = (bf16[192,640]{1,0:T(8,128)(2,1)}, bf16[192,640]{1,0:T(8,128)(2,1)S(1)}, u32[]{:S(2)}, u32[]{:S(2)}) collective-permute-start(bf16[192,640]{1,0:T(8,128)(2,1)} %get-tuple-element.50), channel_id=1, source_target_pairs={{0,8},{1,9},{2,10},{3,11},{4,12},{5,13},{6,14},{7,15},{8,0},{9,1},... | collective-permute-start | bytes 737288 | tf_op jit(solution)/shard_map/ppermute | solution.py:746
  16.5 9.4 %collective-permute-start = (bf16[192,640]{1,0:T(8,128)(2,1)}, bf16[192,640]{1,0:T(8,128)(2,1)S(1)}, u32[]{:S(2)}, u32[]{:S(2)}) collective-permute-start(bf16[192,640]{1,0:T(8,128)(2,1)} %get-tuple-element.50), channel_id=1, source_target_pairs={{0,4},{1,5},{2,6},{3,7},{4,8},{5,9},{6,10},{7,11},{8,12},{9,13},{1... | collective-permute-start | bytes 737288 | tf_op jit(solution)/shard_map/ppermute | solution.py:746
  27.0 35.1 %copy-start.13 = (bf16[4,192,640]{2,1,0:T(8,128)(2,1)}, bf16[4,192,640]{2,1,0:T(8,128)(2,1)S(1)}, u32[]{:S(2)}) copy-start(bf16[4,192,640]{2,1,0:T(8,128)(2,1)S(1)} %pad_maximum_fusion.t0) | copy-start | bytes 2949124
  27.0 26.2 %collective-permute-start.5 = (bf16[4,192,640]{2,1,0:T(8,128)(2,1)S(1)}, bf16[4,192,640]{2,1,0:T(8,128)(2,1)S(1)}, u32[]{:S(2)}, u32[]{:S(2)}) collective-permute-start(bf16[4,192,640]{2,1,0:T(8,128)(2,1)S(1)} %pad_maximum_fusion.t0), channel_id=1, source_target_pairs={{0,3},{1,0},{2,1},{3,2},{4,7},{5,4},{6,5},{7,6},{8,11},{9,8},{10,9... | collective-permute-start | bytes 2949128 | tf_op jit(solution)/shard_map/ppermute | solution.py:746
  29.3 26.4 %collective-permute-start.4 = (bf16[4,192,640]{2,1,0:T(8,128)(2,1)S(1)}, bf16[4,192,640]{2,1,0:T(8,128)(2,1)S(1)}, u32[]{:S(2)}, u32[]{:S(2)}) collective-permute-start(bf16[4,192,640]{2,1,0:T(8,128)(2,1)S(1)} %pad_maximum_fusion.t0), channel_id=1, source_target_pairs={{0,2},{1,3},{2,0},{3,1},{4,6},{5,7},{6,4},{7,5},{8,10},{9,11},{10,... | collective-permute-start | bytes 2949128 | tf_op jit(solution)/shard_map/ppermute | solution.py:746
  29.8 26.8 %collective-permute-start.3 = (bf16[4,192,640]{2,1,0:T(8,128)(2,1)S(1)}, bf16[4,192,640]{2,1,0:T(8,128)(2,1)S(1)}, u32[]{:S(2)}, u32[]{:S(2)}) collective-permute-start(bf16[4,192,640]{2,1,0:T(8,128)(2,1)S(1)} %pad_maximum_fusion.t0), channel_id=1, source_target_pairs={{0,1},{1,2},{2,3},{3,0},{4,5},{5,6},{6,7},{7,4},{8,9},{9,10},{10,1... | collective-permute-start | bytes 2949128 | tf_op jit(solution)/shard_map/ppermute | solution.py:746
  30.4 28.6 %collective-permute-start.6 = (bf16[4,192,640]{2,1,0:T(8,128)(2,1)S(1)}, bf16[4,192,640]{2,1,0:T(8,128)(2,1)S(1)}, u32[]{:S(2)}, u32[]{:S(2)}) collective-permute-start(bf16[4,192,640]{2,1,0:T(8,128)(2,1)S(1)} %pad_maximum_fusion.t0), channel_id=1, source_target_pairs={{0,16},{1,17},{2,18},{3,19},{4,20},{5,21},{6,22},{7,23},{8,24},{9,... | collective-permute-start | bytes 2949128 | tf_op jit(solution)/shard_map/ppermute | solution.py:750
  53.2 8.9 %copy-start.14 = (bf16[4,192,640]{2,1,0:T(8,128)(2,1)}, bf16[4,192,640]{2,1,0:T(8,128)(2,1)S(1)}, u32[]{:S(2)}) copy-start(bf16[4,192,640]{2,1,0:T(8,128)(2,1)S(1)} %collective-permute-done.5.t3) | copy-start | bytes 2949124
  53.2 5.8 %collective-permute-start.9 = (bf16[4,192,640]{2,1,0:T(8,128)(2,1)S(1)}, bf16[4,192,640]{2,1,0:T(8,128)(2,1)S(1)}, u32[]{:S(2)}, u32[]{:S(2)}) collective-permute-start(bf16[4,192,640]{2,1,0:T(8,128)(2,1)S(1)} %collective-permute-done.5.t3), channel_id=1, source_target_pairs={{0,16},{1,17},{2,18},{3,19},{4,20},{5,21},{6,22},{7,23},{8,24},{9,... | collective-permute-start | bytes 2949128 | tf_op jit(solution)/shard_map/ppermute | solution.py:750
  55.7 6.5 %copy-start.15 = (bf16[4,192,640]{2,1,0:T(8,128)(2,1)}, bf16[4,192,640]{2,1,0:T(8,128)(2,1)S(1)}, u32[]{:S(2)}) copy-start(bf16[4,192,640]{2,1,0:T(8,128)(2,1)S(1)} %collective-permute-done.4.t2) | copy-start | bytes 2949124
  55.7 3.6 %collective-permute-start.8 = (bf16[4,192,640]{2,1,0:T(8,128)(2,1)S(1)}, bf16[4,192,640]{2,1,0:T(8,128)(2,1)S(1)}, u32[]{:S(2)}, u32[]{:S(2)}) collective-permute-start(bf16[4,192,640]{2,1,0:T(8,128)(2,1)S(1)} %collective-permute-done.4.t2), channel_id=1, source_target_pairs={{0,16},{1,17},{2,18},{3,19},{4,20},{5,21},{6,22},{7,23},{8,24},{9,... | collective-permute-start | bytes 2949128 | tf_op jit(solution)/shard_map/ppermute | solution.py:750
  56.6 4.6 %collective-permute-start.7 = (bf16[4,192,640]{2,1,0:T(8,128)(2,1)S(1)}, bf16[4,192,640]{2,1,0:T(8,128)(2,1)S(1)}, u32[]{:S(2)}, u32[]{:S(2)}) collective-permute-start(bf16[4,192,640]{2,1,0:T(8,128)(2,1)S(1)} %collective-permute-done.3.t1), channel_id=1, source_target_pairs={{0,16},{1,17},{2,18},{3,19},{4,20},{5,21},{6,22},{7,23},{8,24},{9,... | collective-permute-start | bytes 2949128 | tf_op jit(solution)/shard_map/ppermute | solution.py:750
  189.9 23.9 %all-to-all-start.1 = ((bf16[16,16,2560]{2,1,0:T(8,128)(2,1)}), bf16[16,16,2560]{2,1,0:T(8,128)(2,1)S(1)}, u32[]{:S(2)}, u32[]{:S(2)}) async-start(bf16[16,16,2560]{2,1,0:T(8,128)(2,1)} %bitcast.15), calls=%async_computation.1 | async-start | bytes 2621440 | tf_op jit(solution)/shard_map/all_to_all | solution.py:726
  215.3 24.4 %all-to-all-start.2 = ((bf16[16,16,2560]{2,1,0:T(8,128)(2,1)}), bf16[16,16,2560]{2,1,0:T(8,128)(2,1)S(1)}, u32[]{:S(2)}, u32[]{:S(2)}) async-start(bf16[16,16,2560]{2,1,0:T(8,128)(2,1)} %sum_rows.1), calls=%async_computation.2 | async-start | bytes 2621440 | tf_op jit(solution)/shard_map/all_to_all | solution.py:726
  221.8 62.9 %all-gather.5.cloned.1.call-start = ((), (), s32[]{:S(2)}) async-start(), calls=%async_computation.9 | async-start | bytes 3342336 | tf_op jit(solution)/shard_map/all_gather | solution.py:852
  222.5 108.1 %reduce-scatter.5.cloned.1.call-start = ((), (), s32[]{:S(2)}) async-start(), calls=%async_computation.10 | async-start | bytes 2949120 | tf_op jit(solution)/shard_map/reduce_scatter | solution.py:879
  280.1 34.7 %copy-start.2 = (f32[5,1280]{1,0:T(8,128)S(1)}, f32[5,1280]{1,0:T(8,128)}, u32[]{:S(2)}) copy-start(f32[5,1280]{1,0:T(8,128)} %lg.11) | copy-start | bytes 76804
  280.1 34.7 %copy-start.3 = (bf16[256,128]{1,0:T(8,128)(2,1)S(1)}, bf16[256,128]{1,0:T(8,128)(2,1)}, u32[]{:S(2)}) copy-start(bf16[256,128]{1,0:T(8,128)(2,1)} %get-tuple-element.79.g1c) | copy-start | bytes 196612
  280.1 34.7 %copy-start.4 = (f32[48,128]{1,0:T(8,128)S(1)}, f32[48,128]{1,0:T(8,128)}, u32[]{:S(2)}) copy-start(f32[48,128]{1,0:T(8,128)} %get-tuple-element.78.lat_gain) | copy-start | bytes 73732
  280.1 34.7 %all-to-all-start.3 = ((bf16[16,640,128]{2,1,0:T(8,128)(2,1)}), bf16[16,640,128]{2,1,0:T(8,128)(2,1)S(1)}, u32[]{:S(2)}, u32[]{:S(2)}) async-start(bf16[16,640,128]{2,1,0:T(8,128)(2,1)} %get-tuple-element.75), calls=%async_computation.4 | async-start | bytes 5242880 | tf_op jit(solution)/shard_map/all_to_all | solution.py:726
  319.9 22.6 %all-to-all-start.4 = ((bf16[8,368,128]{2,1,0:T(8,128)(2,1)}), bf16[8,368,128]{2,1,0:T(8,128)(2,1)S(1)}, u32[]{:S(2)}, u32[]{:S(2)}) async-start(bf16[8,368,128]{2,1,0:T(8,128)(2,1)} %get-tuple-element.80), calls=%async_computation.5 | async-start | bytes 1507328 | tf_op jit(solution)/shard_map/all_to_all | solution.py:726
  (15 other events, 30.5 us)
Sparse Core Ops, SparseCore 0:
  11.9 144.5 all-gather.2
  190.0 33.4 reduce-scatter.2
  225.7 49.5 all-gather.4
  277.5 31.2 reduce-scatter.4

commit v3 on v2

--- a/solution.py
+++ b/solution.py
@@ -270,7 +270,7 @@
 def forward_body(
     qin, cot, bg, lg, e_h, g_all, w,
     res, gqin, gain_o, pay, mix_o, nd_o, gq_o, z_h, h_h, a_h,
-    slots, e, z0b, zs, hs, qs, acc, kd, vd, dec, bq, dacc, gq, gkv, wsem, ssem, lsem,
+    slots, e, z0b, zs, zb, hs, qs, acc, kd, vd, dec, bq, dacc, gq, gkv, wsem, ssem, lsem,
 ):
     first = [
         pltpu.make_async_copy(e_h.at[:, 0:D], e, lsem.at[3]),
@@ -296,6 +296,10 @@
         c.start()
         saves.append(c)
 
+    def keep(k):
+        zb[k] = half(zs[k])
+        save(zb.at[k], z_h.at[k])
+
     def mul(a, m):
         out = dot(a, ring.get(m))
         ring.done(m)
@@ -305,12 +309,12 @@
         c.wait()
     z1 = z0b[...].reshape(R, D).astype(F32) + mul(e[...], 0)
     zs[0] = z1
-    save(zs.at[0], z_h.at[0])
+    keep(0)
     h1 = mul(half(norm(z1)[0] * lg[1:2, :]), 1)
-    hs[0] = h1
+    hs[0] = half(h1)
     save(hs.at[0], h_h.at[0])
     zs[1] = zs[0] + mul(half(gelu(h1)), 2)
-    save(zs.at[1], z_h.at[1])
+    keep(1)
     s_b = half(norm(zs[1])[0] * lg[2:3, :])
     for k in range(3):
         qs[k] = half(mul(s_b, 3 + k))
@@ -326,12 +330,12 @@
     qs[3] = half(acc[...])
     save(qs.at[3], a_h.at[3])
     zs[2] = zs[1] + mul(qs[3], 6)
-    save(zs.at[2], z_h.at[2])
+    keep(2)
     h2 = mul(half(norm(zs[2])[0] * lg[3:4, :]), 7)
-    hs[1] = h2
+    hs[1] = half(h2)
     save(hs.at[1], h_h.at[1])
     zs[3] = zs[2] + mul(half(gelu(h2)), 8)
-    save(zs.at[3], z_h.at[3])
+    keep(3)
     c_b = half(norm(zs[3])[0] * lg[4:5, :])
     kd[...] = half(mul(c_b, 9))
     vd[...] = half(mul(c_b, 10))
@@ -378,7 +382,7 @@
         c.wait()
 
 
-def prepare_body(lg, z_h, h_h, a_h, n_h, i_h, s_h, act_h, p_h, mark, zs, hs, qs, ns, vs, ss, acts, ps, sem, osem):
+def prepare_body(lg, z_h, h_h, a_h, n_h, i_h, s_h, act_h, p_h, zs, hs, qs, ns, vs, ss, acts, ps, sem, osem):
     loads = {}
     for k in range(4):
         loads["z", k] = pltpu.make_async_copy(z_h.at[k], zs.at[k], sem.at[k])
@@ -396,7 +400,7 @@
 
     for k, a in ((3, 0), (2, 2), (1, 1), (0, 4)):
         loads["z", k].wait()
-        n, inv = norm(zs[k])
+        n, inv = norm(zs[k].astype(F32))
         ns[k] = half(n)
         save(ns.at[k], n_h.at[k])
         vs[k] = jnp.broadcast_to(inv, (R, 128))
@@ -405,7 +409,7 @@
     save(vs, i_h)
     for k, a in ((1, 3), (0, 5)):
         loads["h", k].wait()
-        x = hs[k]
+        x = hs[k].astype(F32)
         t = jnp.tanh(C0 * (x + C1 * x * x * x))
         acts[a] = half(0.5 * x * (1.0 + t))
         save(acts.at[a], act_h.at[a])
@@ -418,19 +422,17 @@
         p = jnp.exp(s - jnp.max(s, axis=-1, keepdims=True))
         ps[h] = half(p / jnp.sum(p, axis=-1, keepdims=True))
     save(ps, p_h)
-    mark[...] = vs[0, 0:8, :]
     for c in saves:
         c.wait()
 
 
 def lat_backward_body(
-    sc, gkv, lg, w, e_h, n_h, i_h, s_h, act_h, a_h, p_h, gmix, pack_o, g1c_o, gains_o,
+    sc, gin, lg, w, e_h, n_h, i_h, s_h, act_h, a_h, p_h, gmix, pack_o, g1c_o, gains_o,
     slots, ns, vs, ss, acts, qs, ps, acc, acc2, acc3, gh, gw, wsem, lsem,
 ):
-    order = [9, 10, 8, 7, 6, 3, 4, 5, 2, 1, 0]
+    order = [8, 7, 6, 3, 4, 5, 2, 1, 0]
     ring = Ring(w, slots, wsem, order)
     todo = [
-        (n_h.at[3], ns.at[3]),
         (i_h, vs),
         (act_h.at[0], acts.at[0]),
         (s_h.at[1], ss.at[1]),
@@ -449,15 +451,11 @@
         (e_h.at[:, 0:D], acts.at[7]),
     ]
     loads = [pltpu.make_async_copy(a, b, lsem.at[k]) for k, (a, b) in enumerate(todo)]
-    after = {9: (5, 6, 7), 10: (8,), 8: (9,), 7: (10, 11), 6: (12, 13), 3: (14, 15, 16)}
-    ring.start(9)
-    ring.start(10)
-    for c in loads[:2]:
-        c.start()
+    after = {8: (4, 5, 6), 7: (7, 8), 6: (9, 10, 11, 12), 3: (13, 14, 15)}
     ring.start(8)
-    for c in loads[2:5]:
-        c.start()
-    for m in order[3 : ring.n]:
+    for c in loads[:4]:
+        c.start()
+    for m in order[1 : ring.n]:
         ring.start(m)
 
     def ready(*ks):
@@ -492,22 +490,24 @@
             gain_rows.append((10 * k + t, gg[:, 128 * t : 128 * t + 128]))
         return out
 
-    ready(0, 1)
-    gn = mul(gkv[:, 0:D], 9) + mul(gkv[:, D : 2 * D], 10)
-    acc[...] = back(gn, 3)
-    gw[0] = half(put(gkv.at[:, 0:D], 0) + put(gkv.at[:, D : 2 * D], 80))
+    for t in range(10):
+        acc[:, 128 * t : 128 * t + 128] = gin[:, 16 * t : 16 * t + 16, :].reshape(R, 128).astype(F32)
+    tile = lanes(128)
+    values = pltpu.roll(gin[:, 176:192, :].reshape(R, 128).astype(F32), 80, 1)
+    gw[0, :, 0:128] = half(jnp.where(tile < 80, gin[:, 160:176, :].reshape(R, 128).astype(F32), values))
+    gw[0, :, 128:256] = half(jnp.where(tile < 32, values, 0.0))
     gw[1] = half(put(acc, 160))
-    ready(2, 3, 4)
+    ready(0, 1, 2, 3)
     gh[...] = half(mul(half(acc[...]), 8) * ss[1])
     weight_grad(0, 0, 2)
-    ready(5)
+    ready(4)
     gw[3] = half(put(gh, 0))
     acc[...] += back(mul(gh[...], 7), 2)
     gw[4] = half(put(acc, 80))
     qs[3] = half(mul(half(acc[...]), 6))
     acc2[...] = jnp.zeros_like(acc2)
     acc3[...] = jnp.zeros_like(acc3)
-    ready(6, 7, 8, 9)
+    ready(5, 6, 7, 8)
     for h in range(H):
         win = slice(WIN[h], WIN[h] + 256)
         mk = head_mask(h)
@@ -522,27 +522,49 @@
     gn = mul(half(acc2[...]), 3)
     gn = gn + mul(half(acc3[0]), 4)
     gn = gn + mul(half(acc3[1]), 5)
-    ready(10, 11)
+    ready(9, 10)
     weight_grad(1, 2, 1)
     acc[...] += back(gn, 1)
     gw[5] = half(put(acc, 160))
-    ready(12, 13)
+    ready(11, 12)
     gh[...] = half(mul(half(acc[...]), 2) * ss[0])
     weight_grad(2, 3, 3)
     gw[6] = half(put(gh, 0))
-    ready(14, 15, 16)
+    ready(13, 14, 15)
     acc[...] += back(mul(gh[...], 1), 0)
     gw[7] = half(put(acc, 80))
     g1c_o[...] = half(put(acc, 0)[:, 0:128])
     gmix[...] = half(mul(half(acc[...]), 0))
     weight_grad(3, 6, 2)
-    gains_o[...] = as_rows(gain_rows, 48)
-
-
-def sum_rows_body(rcv, mark, out):
+    gains_o[...] = as_rows(gain_rows, 32)
+
+
+def key_value_back_body(sc, rcv, lg, n_h, i_h, w, out, gain_o, wbuf, nbuf, ibuf, sem):
+    rows = pl.ds(pl.multiple_of(sc[1] * 16, 16), 16)
+    copies = []
+    for k, m in enumerate((9, 10)):
+        for i, r0, d0, n in pieces(80 * m, 80):
+            copies.append((w.at[i, :, r0 : r0 + n, :], wbuf.at[k, :, d0 : d0 + n, :]))
+    copies += [(n_h.at[3, rows, :], nbuf), (i_h.at[3, rows, :], ibuf)]
+    copies = [pltpu.make_async_copy(a, b, sem.at[k]) for k, (a, b) in enumerate(copies)]
+    for c in copies:
+        c.start()
     s = half(jnp.sum(rcv[...].astype(F32), axis=0))
-    for k in range(NJ):
-        out[k] = s
+    for j in range(NJ):
+        base = min(128 * (80 * j // 128), 1024)
+        for k in range(2):
+            v = s[:, D * k + base : D * k + base + 256].astype(F32)
+            if 80 * j > base:
+                v = pltpu.roll(v, 256 - (80 * j - base), 1)
+            out[j, 160 + 16 * k : 176 + 16 * k, :] = half(v[:, 0:128])
+    for c in copies:
+        c.wait()
+    gn = dot_nt(s[:, 0:D], wbuf[0].reshape(D, D)) + dot_nt(s[:, D : 2 * D], wbuf[1].reshape(D, D))
+    g, gg = norm_back(gn, lg[4:5, :], nbuf[...].astype(F32), ibuf[:, 0:1])
+    gain_o[...] = gg
+    g = jnp.concatenate([half(g[:, 128 * t : 128 * t + 128]) for t in range(10)], axis=0)
+    for j in range(NJ):
+        out[j, 0:160, :] = g
 
 
 def dec_weights_body(mix, cot, nd, gq, out, buf, sem):
@@ -580,7 +602,7 @@
 
 
 def enc_back_body(
-    sc, x_in, bg, lg, gd, gmix_h, e_h, q_h, k_h, v_h, g_all, dw_h, gin_o, pay,
+    sc, x_in, bg, lg, gd, gc, gmix_h, e_h, q_h, k_h, v_h, g_all, dw_h, gin_o, pay,
     gmix, e, q, k, v, wkv, gq, gkt, gvt, dw, td, tb, sem,
 ):
     pairs = [(gmix_h, gmix), (q_h, q), (k_h, k), (v_h, v), (e_h, e), (g_all, wkv), (dw_h, dw)]
@@ -624,7 +646,8 @@
     gin_o[...] = gin
     rows = [(t, gg[:, 128 * t : 128 * t + 128]) for t in range(6)]
     rows += [(6 + t, gd[:, 128 * t : 128 * t + 128]) for t in range(6)]
-    rows += [(16 + t, g0[:, 128 * t : 128 * t + 128]) for t in range(10)]
+    rows += [(12 + t, g0[:, 128 * t : 128 * t + 128]) for t in range(10)]
+    rows += [(22 + t, gc[:, 128 * t : 128 * t + 128]) for t in range(10)]
     g = half(as_rows(rows, 32))
     for j in range(NJ):
         pay[j, 480:512, :] = g
@@ -667,7 +690,7 @@
         out[i, 0:160, :] = half(jnp.where(lane < 80, w0[160 * i : 160 * i + 160, :], beside))
         out[i, 160:192, :] = gz[32 * i : 32 * i + 32, :]
         out[i, 192:288, :] = one[r : r + 96, :]
-        out[i, 288:368, :] = gains
+        out[i, 288:352, :] = gains
     s = jnp.sum(rcv[:, 512:640, :].astype(F32), axis=0)
     bq_o[...] = s[0:80, 0:96]
     dec_o[:, 0:128] = s[80:128]
@@ -684,13 +707,13 @@
     bm_o[0] = jnp.concatenate([sums[192:288], fill], axis=0).T[0:80, 0:96]
     bm_o[1] = jnp.concatenate([value, fill], axis=0).T[0:80, 0:96]
     bm_o[2] = bq[...]
-    g = sums[288:368]
+    g = sums[288:352]
     for t in range(6):
         for b in range(2):
             byte_o[b : b + 1, 128 * t : 128 * t + 128] = g[6 * b + t : 6 * b + t + 1, :]
     for t in range(10):
         for b in range(5):
-            r = 16 + t if b == 0 else 32 + 10 * (b - 1) + t
+            r = {0: 12, 1: 32, 2: 42, 3: 52, 4: 22}[b] + t
             lat_o[b : b + 1, 128 * t : 128 * t + 128] = g[r : r + 1, :]
     for m, (kind, n) in enumerate(SQUARE):
         window, o = PLACE[m]
@@ -779,8 +802,8 @@
             ((N, D), BF, "v"),
             ((N, DI), BF, "v"),
             ((N, D), BF, "v"),
-            ((4, R, D), F32, "h"),
-            ((2, R, D), F32, "h"),
+            ((4, R, D), BF, "h"),
+            ((2, R, D), BF, "h"),
             ((4, R, D), BF, "h"),
         ],
         [(qin, "v"), (cot, "v"), (bg, "v"), (lg, "v"), (e, "h"), (g_all, "h"), (w, "h")],
@@ -789,7 +812,8 @@
             pltpu.VMEM((R, D), BF),
             pltpu.VMEM((NJ, 16, D), BF),
             pltpu.VMEM((4, R, D), F32),
-            pltpu.VMEM((2, R, D), F32),
+            pltpu.VMEM((4, R, D), BF),
+            pltpu.VMEM((2, R, D), BF),
             pltpu.VMEM((4, R, D), BF),
             pltpu.VMEM((R, D), F32),
             pltpu.VMEM((R, D), BF),
@@ -808,7 +832,7 @@
         name="forward",
     )
     rows = exchange(dpay.reshape(NJ, 16, 2 * D), BLK)
-    n_h, i_h, s_h, act_h, p_h, mark = call(
+    n_h, i_h, s_h, act_h, p_h = call(
         prepare_body,
         [
             ((4, R, D), BF, "h"),
@@ -816,12 +840,11 @@
             ((2, R, D), F32, "h"),
             ((6, R, D), BF, "h"),
             ((H, R, R), BF, "h"),
-            ((8, 128), F32, "v"),
         ],
         [(lg, "v"), (z_h, "h"), (h_h, "h"), (a_h, "h")],
         [
-            pltpu.VMEM((4, R, D), F32),
-            pltpu.VMEM((2, R, D), F32),
+            pltpu.VMEM((4, R, D), BF),
+            pltpu.VMEM((2, R, D), BF),
             pltpu.VMEM((2, R, D), BF),
             pltpu.VMEM((4, R, D), BF),
             pltpu.VMEM((4, R, 128), F32),
@@ -831,7 +854,7 @@
             DMA((7,)),
             DMA((14,)),
         ],
-        vmem=36,
+        vmem=58,
         flops=5e9,
         name="prepare",
     )
@@ -844,18 +867,24 @@
         flops=4e9,
         name="dec_weights",
     )
-    (dup,) = call(
-        sum_rows_body, [((NJ, 16, 2 * D), BF, "v")], [(rows, "v"), (mark, "h")], vmem=12, name="sum_rows"
-    )
-    gkv = exchange(dup, BLK).reshape(R, 2 * D)
-    nb, _ = lax.optimization_barrier((nb, dup))
+    kv, gc = call(
+        key_value_back_body,
+        [((NJ, 192, 128), BF, "v"), ((1, D), F32, "v")],
+        [(sc, "s"), (rows, "v"), (lg, "v"), (n_h, "h"), (i_h, "h"), (w, "h")],
+        [pltpu.VMEM((2,) + big, BF), pltpu.VMEM((16, D), BF), pltpu.VMEM((16, 128), F32), DMA((6,))],
+        vmem=58,
+        flops=1e8,
+        name="key_value_back",
+    )
+    gin4 = exchange(kv, BLK)
+    nb, _ = lax.optimization_barrier((nb, gin4))
     nf = lax.all_gather(nb, BLK, axis=0, tiled=True)
     dw = lax.psum_scatter(dw.reshape(NI * 1920, 128), BATCH, scatter_dimension=0, tiled=True)
 
     gmix, pack, g1c, lat_gain = call(
         lat_backward_body,
-        [((R, D), BF, "v"), ((D, 1024), BF, "v"), ((R, 128), BF, "v"), ((48, 128), F32, "v")],
-        [(sc, "s"), (gkv, "v"), (lg, "v")] + [(v, "h") for v in (w, e, n_h, i_h, s_h, act_h, a_h, p_h)],
+        [((R, D), BF, "v"), ((D, 1024), BF, "v"), ((R, 128), BF, "v"), ((32, 128), F32, "v")],
+        [(sc, "s"), (gin4, "v"), (lg, "v")] + [(v, "h") for v in (w, e, n_h, i_h, s_h, act_h, a_h, p_h)],
         [
             pltpu.VMEM((5,) + big, BF),
             pltpu.VMEM((4, R, D), BF),
@@ -870,7 +899,7 @@
             pltpu.VMEM((R, D), BF),
             pltpu.VMEM((8, R, 256), BF),
             DMA((5, 2)),
-            DMA((17,)),
+            DMA((16,)),
         ],
         vmem=60,
         flops=8e10,
@@ -880,7 +909,7 @@
     gin, epay = call(
         enc_back_body,
         [((N, DI), F32, "v"), ((NJ, 640, 128), BF, "v")],
-        [(sc, "s"), (xin, "v"), (bg, "v"), (lg, "v"), (gd, "v")]
+        [(sc, "s"), (xin, "v"), (bg, "v"), (lg, "v"), (gd, "v"), (gc, "v")]
         + [(v, "h") for v in (gmix, e, q_b, k_b, v_b, g_all, dw)],
         [
             pltpu.VMEM((R, D), BF),
@@ -904,7 +933,7 @@
     r1 = exchange(epay, BLK)
     p2, dec_grad, bq_grad = call(
         tail_one_body,
-        [((NI, 368, 128), BF, "v"), ((48, 160), F32, "v"), ((80, 96), F32, "v")],
+        [((NI, 352, 128), BF, "v"), ((48, 160), F32, "v"), ((80, 96), F32, "v")],
         [(r1, "v"), (nf, "h"), (g_all, "h"), (lg, "v"), (lat_gain, "v"), (g1c, "v")],
         [pltpu.VMEM((NJ * N, DI), BF), pltpu.VMEM((NJ, 16, D), BF), pltpu.VMEM((256, 2048), BF), DMA((2,))],
         name="tail_one",

time: 358 us -> 354 us (0.989)
  blocking collectives: 42.2 us -> 57.6 us
  local copies, waits for them, and re-layouts: 13.2 us -> 3.63 us
  starting transfers between devices: 43.1 us -> 35.5 us
  waiting for transfers between devices: 134 us -> 128 us
  Pallas kernels: 103 us -> 107 us
    all_to_all x1 -> x2, blocking collectives: 18 us -> 33.4 us  [exchange(): lax.all_to_all(flat, axes, split_axis=0, concat_axis=0, tiled=True)]
    all_to_all x4 -> x3, waiting for transfers between devices: 59.1 us -> 47.5 us  [exchange(): lax.all_to_all(flat, axes, split_axis=0, concat_axis=0, tiled=True)]
    unnamed x42 -> x26, local copies, waits for them, and re-layouts: 12.6 us -> 3.02 us
    all_to_all x4 -> x3, starting transfers between devices: 26.3 us -> 18.7 us  [exchange(): lax.all_to_all(flat, axes, split_axis=0, concat_axis=0, tiled=True)]
    all_gather x1, waiting for transfers between devices: 0.02 us -> 6.2 us  [shards(): nf = lax.all_gather(nb, BLK, axis=0, tiled=True)]
    pallas_call x11, Pallas kernels: 103 us -> 107 us  [call(): pl.pallas_call(body, out_shape=[jax.ShapeDtypeStruct(s, t) for s, t, _ in...]
  transfers between devices with their start and end apart: 18 -> 17, of which waited for: 11 -> 13; matrix products, arithmetic and copies ran while one was open for 0% -> 0% of each run, Pallas kernels for 19% -> 20%
where the time goes in v3:
time: 354 us; the launch traced here: 348 us
  waiting for transfers between devices  128 us (36%)
  Pallas kernels  107 us (30%)
  blocking collectives  57.6 us (16%)
  starting transfers between devices  35.5 us (10%)
  between operations  14.8 us (4%)
  local copies, waits for them, and re-layouts  3.63 us (1%)
    pallas_call x11, Pallas kernels, call(): pl.pallas_call(body, out_shape=[jax.ShapeDtypeStruct(s, t) for s, t, _ in...  107 us
    all_to_all x3, waiting for transfers between devices, exchange(): lax.all_to_all(flat, axes, split_axis=0, concat_axis=0, tiled=True)  47.5 us
    all_gather x1, waiting for transfers between devices, shards(): w = lax.all_gather(wsh, AXES, axis=0, tiled=True).reshape(NI, NJ, ROWS_I, D)  42.6 us
    all_to_all x2, blocking collectives, exchange(): lax.all_to_all(flat, axes, split_axis=0, concat_axis=0, tiled=True)  33.4 us
    ppermute x6, waiting for transfers between devices, step(): return [lax.ppermute(v, AXES, along(stage, d)) for d in (1, 2, 3)]  29.5 us
    all_gather x1, blocking collectives, shards(): e = lax.all_gather(mine, BLK, axis=0, tiled=True)  24.1 us
    all_to_all x3, starting transfers between devices, exchange(): lax.all_to_all(flat, axes, split_axis=0, concat_axis=0, tiled=True)  18.7 us
    ppermute x6, starting transfers between devices, step(): return [lax.ppermute(v, AXES, along(stage, d)) for d in (1, 2, 3)]  8.75 us
  transfers between devices with their start and end apart: 17, of which 13 were waited for; matrix products, arithmetic and copies ran while one was open for 0% of the time, Pallas kernels for 20%

profile of v3, /device:TPU:1, one launch (start us, length us, event | category | flops | bytes accessed | tf_op | source)
XLA Modules:
  0.0 348.0 jit_solution(11304875274265731311)
XLA Ops:
  8.5 3.3 pack.1
  11.9 4.7 %collective-permute-start.2 = (bf16[192,640]{1,0:T(8,128)(2,1)}, bf16[192,640]{1,0:T(8,128)(2,1)S(1)}, u32[]{:S(2)}, u32[]{:S(2)}) collective-permute-start(bf16[192,640]{1,0:T(8,128)(2,1)} %get-tuple-element.51), channel_id=1, source_target_pairs={{0,12},{1,13},{2,14},{3,15},{4,0},{5,1},{6,2},{7,3},{8,4},{9,5},{1... | collective-permute-start | bytes 737288 | tf_op jit(solution)/shard_map/ppermute | solution.py:769
  17.2 5.4 %collective-permute-done.2 = bf16[192,640]{1,0:T(8,128)(2,1)S(1)} collective-permute-done((bf16[192,640]{1,0:T(8,128)(2,1)}, bf16[192,640]{1,0:T(8,128)(2,1)S(1)}, u32[]{:S(2)}, u32[]{:S(2)}) %collective-permute-start.2) | collective-permute-done | bytes 245792 | tf_op jit(solution)/shard_map/ppermute | solution.py:769
  30.4 2.8 collective-permute-start.6
  33.2 20.0 %collective-permute-done.5.t3 = bf16[4,192,640]{2,1,0:T(8,128)(2,1)S(1)} collective-permute-done((bf16[4,192,640]{2,1,0:T(8,128)(2,1)S(1)}, bf16[4,192,640]{2,1,0:T(8,128)(2,1)S(1)}, u32[]{:S(2)}, u32[]{:S(2)}) %collective-permute-start.5) | collective-permute-done | bytes 983072 | tf_op jit(solution)/shard_map/ppermute | solution.py:769
  62.2 9.1 %enc.1 = (bf16[16,192,1280]{2,1,0:T(8,128)(2,1)}, bf16[128,768]{1,0:T(8,128)(2,1)}, bf16[128,1280]{1,0:T(8,128)(2,1)}, bf16[128,1280]{1,0:T(8,128)(2,1)}, bf16[2...) custom-call(s32[6]{0:T(128)} %stack.38.sc, bf16[4,192,640]{2,1,0:T(8,128)(2,1)} %copy-done.5, ...), custom_call_target="tpu_custom_call" | custom-call | flops 3000000000 | bytes 4194304 | tf_op jit(solution)/shard_map/enc/pallas_call | solution.py:113
  71.2 18.0 %all_to_all.36.rcv = bf16[16,16,1408]{2,1,0:T(8,128)(2,1)S(1)} all-to-all(bf16[16,16,1408]{2,1,0:T(8,128)(2,1)} %bitcast.25), channel_id=1, replica_groups=mesh['y'=4,'core'=2,'x'=4,'z'=4] {'x','z'}, dimensions={0} | all-to-all | bytes 1441792 | tf_op jit(solution)/shard_map/all_to_all | solution.py:749
  89.8 24.1 %all_gather.9.e_h = bf16[256,1408]{1,0:T(8,128)(2,1)} all-gather(bf16[16,1408]{1,0:T(8,128)(2,1)S(1)} %combine.1), channel_id=1, replica_groups=mesh['y'=4,'core'=2,'x'=4,'z'=4] {'x','z'}, dimensions={0}, use_global_device_ids=true | all-gather | bytes 765952 | tf_op jit(solution)/shard_map/all_gather | solution.py:792
  113.9 42.6 %all-gather.3.cloned.1.call-done = bf16[16384,1280]{1,0:T(8,128)(2,1)} async-done(((bf16[128,1280]{1,0:T(8,128)(2,1)}), bf16[16384,1280]{1,0:T(8,128)(2,1)}) %all-gather.3.cloned.1.call-update) | async-done | bytes 41943056 | tf_op jit(solution)/shard_map/all_gather | solution.py:766
  156.6 29.1 %forward.1 = (bf16[128,768]{1,0:T(8,128)(2,1)}, f32[128,768]{1,0:T(8,128)}, f32[1,768]{1,0:T(1,128)}, bf16[256,2560]{1,0:T(8,128)(2,1)}, bf16[128,1280]{1,0:T(8,...) custom-call(bf16[128,768]{1,0:T(8,128)(2,1)} %bitcast.33, ...), custom_call_target="tpu_custom_call" | custom-call | flops 15000000512 | bytes 4194304 | tf_op jit(solution)/shard_map/forward/pallas_call | solution.py:113
  185.7 4.1 %dec_weights.1 = bf16[8,1920,128]{2,1,0:T(8,128)(2,1)} custom-call(bf16[128,1280]{1,0:T(8,128)(2,1)} %get-tuple-element.72.mix, bf16[128,768]{1,0:T(8,128)(2,1)} %bitcast.35, bf16[128,768]{1,0:T(8,128)(2,1)} %get-tuple-element.73.nd, bf16[128,1280]{1,0:T(8,128)(2,1)} %get-tuple-element.74.gq), custom_call_target="tpu_custom_call" | custom-call | flops 4000000000 | bytes 4194304 | tf_op jit(solution)/shard_map/dec_weights/pallas_call | solution.py:113
  189.8 4.6 %all-to-all-start.1 = ((bf16[16,16,2560]{2,1,0:T(8,128)(2,1)}), bf16[16,16,2560]{2,1,0:T(8,128)(2,1)S(1)}, u32[]{:S(2)}, u32[]{:S(2)}) async-start(bf16[16,16,2560]{2,1,0:T(8,128)(2,1)} %bitcast.15), calls=%async_computation.1 | async-start | bytes 2621440 | tf_op jit(solution)/shard_map/all_to_all | solution.py:749
  194.5 8.1 %prepare.1 = (bf16[4,256,1280]{2,1,0:T(8,128)(2,1)}, f32[4,256,128]{2,1,0:T(8,128)}, f32[2,256,1280]{2,1,0:T(8,128)}, bf16[6,256,1280]{2,1,0:T(8,128)(2,1)}, bf16[8,256,256]{2,1,0:T(8,128)(2,1)}) custom-call(f32[5,1280]{1,0:T(8,128)} %lg.13, bf16[4,256,1280]{2,1,0:T(8,128)(2,1)} %get-tuple-element.58.z_h, bf16[2,256,1280]{2,1,0:T(8,128)(2,1)} %get-tuple-element.59.h_h, ...), custom_call_target="tpu_custom_call" | custom-call | flops 5000000000 | bytes 4194304 | tf_op jit(solution)/shard_map/prepare/pallas_call | solution.py:113
  202.6 11.0 %all-to-all-done.1.rcv = bf16[16,16,2560]{2,1,0:T(8,128)(2,1)S(1)} async-done(((bf16[16,16,2560]{2,1,0:T(8,128)(2,1)}), bf16[16,16,2560]{2,1,0:T(8,128)(2,1)S(1)}, u32[]{:S(2)}, u32[]{:S(2)}) %all-to-all-start.1) | async-done | bytes 1310752 | tf_op jit(solution)/shard_map/all_to_all | solution.py:749
  214.6 7.2 %key_value_back.1 = (bf16[16,192,128]{2,1,0:T(8,128)(2,1)}, f32[1,1280]{1,0:T(1,128)}) custom-call(s32[6]{0:T(128)} %stack.38.sc, bf16[16,16,2560]{2,1,0:T(8,128)(2,1)} %copy-done.4, f32[5,1280]{1,0:T(8,128)} %lg.13, bf16[4,256,1280]{2,1,0:T(8,128)(2,1)} %get-tuple-element.61.n_h, f32[4,256,128]{2,1,0:T(8,128)} %get-tuple-element.62.i_h, ...), custom_call_target="tpu_custom_call" | custom-call | flops 100000000 | bytes 4194304 | tf_op jit(solution)/shard_map/key_value_back/pallas_call | solution.py:113
  221.8 15.4 %all_to_all.37.gin = bf16[16,192,128]{2,1,0:T(8,128)(2,1)} all-to-all(bf16[16,192,128]{2,1,0:T(8,128)(2,1)} %get-tuple-element.64), channel_id=1, replica_groups=mesh['y'=4,'core'=2,'x'=4,'z'=4] {'x','z'}, dimensions={0} | all-to-all | bytes 1572864 | tf_op jit(solution)/shard_map/all_to_all | solution.py:749
  237.5 29.2 %lat_backward.1 = (bf16[256,1280]{1,0:T(8,128)(2,1)}, bf16[1280,1024]{1,0:T(8,128)(2,1)}, bf16[256,128]{1,0:T(8,128)(2,1)}, f32[32,128]{1,0:T(8,128)}) custom-call(s32[6]{0:T(128)} %stack.38.sc, bf16[16,192,128]{2,1,0:T(8,128)(2,1)} %all_to_all.37.gin, f32[5,1280]{1,0:T(8,128)} %lg.13, bf16[8,16,128,1280]{3,2,1,0:T(8,128)(2,1)} %bitcast.23, ...), custom_call_target="tpu_custom_call" | custom-call | flops 80000000000 | bytes 4194304 | tf_op jit(solution)/shard_map/lat_backward/pallas_call | solution.py:113
  266.8 10.0 %enc_back.1 = (f32[128,768]{1,0:T(8,128)}, bf16[16,640,128]{2,1,0:T(8,128)(2,1)}) custom-call(s32[6]{0:T(128)} %stack.38.sc, bf16[128,768]{1,0:T(8,128)(2,1)} %bitcast.31, f32[2,768]{1,0:T(2,128)} %bg.5, f32[5,1280]{1,0:T(8,128)} %lg.13, f32[1,768]{1,0:T(1,128)} %get-tuple-element.56.gd, f32[1,1280]{1,0:T(1,128)} %get-tuple-element.63.gc, ...), custom_call_target="tpu_custom_call" | custom-call | flops 3000000000 | bytes 4194304 | tf_op jit(solution)/shard_map/enc_back/pallas_call | solution.py:113
  276.8 4.2 %all-to-all-start.3 = ((bf16[16,640,128]{2,1,0:T(8,128)(2,1)}), bf16[16,640,128]{2,1,0:T(8,128)(2,1)S(1)}, u32[]{:S(2)}, u32[]{:S(2)}) async-start(bf16[16,640,128]{2,1,0:T(8,128)(2,1)} %get-tuple-element.77), calls=%async_computation.4 | async-start | bytes 5242880 | tf_op jit(solution)/shard_map/all_to_all | solution.py:749
  281.0 6.2 %all-gather.5.cloned.1.call-done.nf_h = bf16[2048,768]{1,0:T(8,128)(2,1)} async-done(((bf16[128,768]{1,0:T(8,128)(2,1)}), bf16[2048,768]{1,0:T(8,128)(2,1)}) %all-gather.5.cloned.1.call-update) | async-done | bytes 3145744 | tf_op jit(solution)/shard_map/all_gather | solution.py:881
  287.2 25.2 %all-to-all-done.3.rcv = bf16[16,640,128]{2,1,0:T(8,128)(2,1)S(1)} async-done(((bf16[16,640,128]{2,1,0:T(8,128)(2,1)}), bf16[16,640,128]{2,1,0:T(8,128)(2,1)S(1)}, u32[]{:S(2)}, u32[]{:S(2)}) %all-to-all-start.3) | async-done | bytes 2621472 | tf_op jit(solution)/shard_map/all_to_all | solution.py:749
  312.4 5.1 %tail_one.1 = (bf16[8,352,128]{2,1,0:T(8,128)(2,1)}, f32[48,160]{1,0:T(8,128)}, f32[80,96]{1,0:T(8,128)S(1)}) custom-call(bf16[16,640,128]{2,1,0:T(8,128)(2,1)S(1)} %all-to-all-done.3.rcv, bf16[2048,768]{1,0:T(8,128)(2,1)} %all-gather.5.cloned.1.call-done.nf_h, bf16[16,192,1280]{2,1,0:T(8,128)(2,1)} %get-tuple-element.53.g_all, f32[5,1280]{1,0:T(8,128)S(1)} %copy-done, ...), custom_call_target="tpu_custom_call" | custom-call | bytes 4194304 | tf_op jit(solution)/shard_map/tail_one/pallas_call | solution.py:113
  317.5 9.8 %all-to-all-start.4 = ((bf16[8,352,128]{2,1,0:T(8,128)(2,1)}), bf16[8,352,128]{2,1,0:T(8,128)(2,1)S(1)}, u32[]{:S(2)}, u32[]{:S(2)}) async-start(bf16[8,352,128]{2,1,0:T(8,128)(2,1)} %get-tuple-element.82), calls=%async_computation.5 | async-start | bytes 1441792 | tf_op jit(solution)/shard_map/all_to_all | solution.py:749
  327.6 11.4 %all-to-all-done.4.rcv = bf16[8,352,128]{2,1,0:T(8,128)(2,1)S(1)} async-done(((bf16[8,352,128]{2,1,0:T(8,128)(2,1)}), bf16[8,352,128]{2,1,0:T(8,128)(2,1)S(1)}, u32[]{:S(2)}, u32[]{:S(2)}) %all-to-all-start.4) | async-done | bytes 720928 | tf_op jit(solution)/shard_map/all_to_all | solution.py:749
  (56 shorter events, 22.6 us)
Async XLA Ops:
  7.2 149.4 %all-gather.3.cloned.1.call-start = ((), (), s32[]{:S(2)}) async-start(), calls=%async_computation.7 | async-start | bytes 42270720 | tf_op jit(solution)/shard_map/all_gather | solution.py:766
  11.8 255.0 %reduce-scatter.3.cloned.1.call-start = ((), (), s32[]{:S(2)}) async-start(), calls=%async_computation.8 | async-start | bytes 4423680 | tf_op jit(solution)/shard_map/reduce_scatter | solution.py:882
  11.9 10.7 %collective-permute-start.2 = (bf16[192,640]{1,0:T(8,128)(2,1)}, bf16[192,640]{1,0:T(8,128)(2,1)S(1)}, u32[]{:S(2)}, u32[]{:S(2)}) collective-permute-start(bf16[192,640]{1,0:T(8,128)(2,1)} %get-tuple-element.51), channel_id=1, source_target_pairs={{0,12},{1,13},{2,14},{3,15},{4,0},{5,1},{6,2},{7,3},{8,4},{9,5},{1... | collective-permute-start | bytes 737288 | tf_op jit(solution)/shard_map/ppermute | solution.py:769
  16.5 7.1 %collective-permute-start.1 = (bf16[192,640]{1,0:T(8,128)(2,1)}, bf16[192,640]{1,0:T(8,128)(2,1)S(1)}, u32[]{:S(2)}, u32[]{:S(2)}) collective-permute-start(bf16[192,640]{1,0:T(8,128)(2,1)} %get-tuple-element.51), channel_id=1, source_target_pairs={{0,8},{1,9},{2,10},{3,11},{4,12},{5,13},{6,14},{7,15},{8,0},{9,1},... | collective-permute-start | bytes 737288 | tf_op jit(solution)/shard_map/ppermute | solution.py:769
  16.5 9.4 %collective-permute-start = (bf16[192,640]{1,0:T(8,128)(2,1)}, bf16[192,640]{1,0:T(8,128)(2,1)S(1)}, u32[]{:S(2)}, u32[]{:S(2)}) collective-permute-start(bf16[192,640]{1,0:T(8,128)(2,1)} %get-tuple-element.51), channel_id=1, source_target_pairs={{0,4},{1,5},{2,6},{3,7},{4,8},{5,9},{6,10},{7,11},{8,12},{9,13},{1... | collective-permute-start | bytes 737288 | tf_op jit(solution)/shard_map/ppermute | solution.py:769
  27.0 35.1 %copy-start.5 = (bf16[4,192,640]{2,1,0:T(8,128)(2,1)}, bf16[4,192,640]{2,1,0:T(8,128)(2,1)S(1)}, u32[]{:S(2)}) copy-start(bf16[4,192,640]{2,1,0:T(8,128)(2,1)S(1)} %pad_maximum_fusion.t0) | copy-start | bytes 2949124
  27.0 26.2 %collective-permute-start.5 = (bf16[4,192,640]{2,1,0:T(8,128)(2,1)S(1)}, bf16[4,192,640]{2,1,0:T(8,128)(2,1)S(1)}, u32[]{:S(2)}, u32[]{:S(2)}) collective-permute-start(bf16[4,192,640]{2,1,0:T(8,128)(2,1)S(1)} %pad_maximum_fusion.t0), channel_id=1, source_target_pairs={{0,3},{1,0},{2,1},{3,2},{4,7},{5,4},{6,5},{7,6},{8,11},{9,8},{10,9... | collective-permute-start | bytes 2949128 | tf_op jit(solution)/shard_map/ppermute | solution.py:769
  29.3 26.4 %collective-permute-start.4 = (bf16[4,192,640]{2,1,0:T(8,128)(2,1)S(1)}, bf16[4,192,640]{2,1,0:T(8,128)(2,1)S(1)}, u32[]{:S(2)}, u32[]{:S(2)}) collective-permute-start(bf16[4,192,640]{2,1,0:T(8,128)(2,1)S(1)} %pad_maximum_fusion.t0), channel_id=1, source_target_pairs={{0,2},{1,3},{2,0},{3,1},{4,6},{5,7},{6,4},{7,5},{8,10},{9,11},{10,... | collective-permute-start | bytes 2949128 | tf_op jit(solution)/shard_map/ppermute | solution.py:769
  29.8 26.8 %collective-permute-start.3 = (bf16[4,192,640]{2,1,0:T(8,128)(2,1)S(1)}, bf16[4,192,640]{2,1,0:T(8,128)(2,1)S(1)}, u32[]{:S(2)}, u32[]{:S(2)}) collective-permute-start(bf16[4,192,640]{2,1,0:T(8,128)(2,1)S(1)} %pad_maximum_fusion.t0), channel_id=1, source_target_pairs={{0,1},{1,2},{2,3},{3,0},{4,5},{5,6},{6,7},{7,4},{8,9},{9,10},{10,1... | collective-permute-start | bytes 2949128 | tf_op jit(solution)/shard_map/ppermute | solution.py:769
  30.4 28.6 %collective-permute-start.6 = (bf16[4,192,640]{2,1,0:T(8,128)(2,1)S(1)}, bf16[4,192,640]{2,1,0:T(8,128)(2,1)S(1)}, u32[]{:S(2)}, u32[]{:S(2)}) collective-permute-start(bf16[4,192,640]{2,1,0:T(8,128)(2,1)S(1)} %pad_maximum_fusion.t0), channel_id=1, source_target_pairs={{0,16},{1,17},{2,18},{3,19},{4,20},{5,21},{6,22},{7,23},{8,24},{9,... | collective-permute-start | bytes 2949128 | tf_op jit(solution)/shard_map/ppermute | solution.py:773
  53.2 8.9 %copy-start.6 = (bf16[4,192,640]{2,1,0:T(8,128)(2,1)}, bf16[4,192,640]{2,1,0:T(8,128)(2,1)S(1)}, u32[]{:S(2)}) copy-start(bf16[4,192,640]{2,1,0:T(8,128)(2,1)S(1)} %collective-permute-done.5.t3) | copy-start | bytes 2949124
  53.2 5.8 %collective-permute-start.9 = (bf16[4,192,640]{2,1,0:T(8,128)(2,1)S(1)}, bf16[4,192,640]{2,1,0:T(8,128)(2,1)S(1)}, u32[]{:S(2)}, u32[]{:S(2)}) collective-permute-start(bf16[4,192,640]{2,1,0:T(8,128)(2,1)S(1)} %collective-permute-done.5.t3), channel_id=1, source_target_pairs={{0,16},{1,17},{2,18},{3,19},{4,20},{5,21},{6,22},{7,23},{8,24},{9,... | collective-permute-start | bytes 2949128 | tf_op jit(solution)/shard_map/ppermute | solution.py:773
  55.7 6.5 %copy-start.7 = (bf16[4,192,640]{2,1,0:T(8,128)(2,1)}, bf16[4,192,640]{2,1,0:T(8,128)(2,1)S(1)}, u32[]{:S(2)}) copy-start(bf16[4,192,640]{2,1,0:T(8,128)(2,1)S(1)} %collective-permute-done.4.t2) | copy-start | bytes 2949124
  55.7 3.6 %collective-permute-start.8 = (bf16[4,192,640]{2,1,0:T(8,128)(2,1)S(1)}, bf16[4,192,640]{2,1,0:T(8,128)(2,1)S(1)}, u32[]{:S(2)}, u32[]{:S(2)}) collective-permute-start(bf16[4,192,640]{2,1,0:T(8,128)(2,1)S(1)} %collective-permute-done.4.t2), channel_id=1, source_target_pairs={{0,16},{1,17},{2,18},{3,19},{4,20},{5,21},{6,22},{7,23},{8,24},{9,... | collective-permute-start | bytes 2949128 | tf_op jit(solution)/shard_map/ppermute | solution.py:773
  56.6 5.5 %copy-start.8 = (bf16[4,192,640]{2,1,0:T(8,128)(2,1)}, bf16[4,192,640]{2,1,0:T(8,128)(2,1)S(1)}, u32[]{:S(2)}) copy-start(bf16[4,192,640]{2,1,0:T(8,128)(2,1)S(1)} %collective-permute-done.3.t1) | copy-start | bytes 2949124
  56.6 4.6 %collective-permute-start.7 = (bf16[4,192,640]{2,1,0:T(8,128)(2,1)S(1)}, bf16[4,192,640]{2,1,0:T(8,128)(2,1)S(1)}, u32[]{:S(2)}, u32[]{:S(2)}) collective-permute-start(bf16[4,192,640]{2,1,0:T(8,128)(2,1)S(1)} %collective-permute-done.3.t1), channel_id=1, source_target_pairs={{0,16},{1,17},{2,18},{3,19},{4,20},{5,21},{6,22},{7,23},{8,24},{9,... | collective-permute-start | bytes 2949128 | tf_op jit(solution)/shard_map/ppermute | solution.py:773
  189.8 23.8 %all-to-all-start.1 = ((bf16[16,16,2560]{2,1,0:T(8,128)(2,1)}), bf16[16,16,2560]{2,1,0:T(8,128)(2,1)S(1)}, u32[]{:S(2)}, u32[]{:S(2)}) async-start(bf16[16,16,2560]{2,1,0:T(8,128)(2,1)} %bitcast.15), calls=%async_computation.1 | async-start | bytes 2621440 | tf_op jit(solution)/shard_map/all_to_all | solution.py:749
  194.4 92.8 %all-gather.5.cloned.1.call-start = ((), (), s32[]{:S(2)}) async-start(), calls=%async_computation.9 | async-start | bytes 3342336 | tf_op jit(solution)/shard_map/all_gather | solution.py:881
  237.3 90.3 %reduce-scatter.5.cloned.1.call-start = ((), (), s32[]{:S(2)}) async-start(), calls=%async_computation.10 | async-start | bytes 2949120 | tf_op jit(solution)/shard_map/reduce_scatter | solution.py:908
  276.8 35.6 %copy-start = (f32[5,1280]{1,0:T(8,128)S(1)}, f32[5,1280]{1,0:T(8,128)}, u32[]{:S(2)}) copy-start(f32[5,1280]{1,0:T(8,128)} %lg.13) | copy-start | bytes 76804
  276.8 35.6 %copy-start.2 = (bf16[256,128]{1,0:T(8,128)(2,1)S(1)}, bf16[256,128]{1,0:T(8,128)(2,1)}, u32[]{:S(2)}) copy-start(bf16[256,128]{1,0:T(8,128)(2,1)} %get-tuple-element.81.g1c) | copy-start | bytes 196612
  276.8 35.6 %copy-start.3 = (f32[32,128]{1,0:T(8,128)S(1)}, f32[32,128]{1,0:T(8,128)}, u32[]{:S(2)}) copy-start(f32[32,128]{1,0:T(8,128)} %get-tuple-element.80.lat_gain) | copy-start | bytes 49156
  276.8 35.6 %all-to-all-start.3 = ((bf16[16,640,128]{2,1,0:T(8,128)(2,1)}), bf16[16,640,128]{2,1,0:T(8,128)(2,1)S(1)}, u32[]{:S(2)}, u32[]{:S(2)}) async-start(bf16[16,640,128]{2,1,0:T(8,128)(2,1)} %get-tuple-element.77), calls=%async_computation.4 | async-start | bytes 5242880 | tf_op jit(solution)/shard_map/all_to_all | solution.py:749
  317.5 21.4 %all-to-all-start.4 = ((bf16[8,352,128]{2,1,0:T(8,128)(2,1)}), bf16[8,352,128]{2,1,0:T(8,128)(2,1)S(1)}, u32[]{:S(2)}, u32[]{:S(2)}) async-start(bf16[8,352,128]{2,1,0:T(8,128)(2,1)} %get-tuple-element.82), calls=%async_computation.5 | async-start | bytes 1441792 | tf_op jit(solution)/shard_map/all_to_all | solution.py:749
  (6 other events, 9.3 us)
Sparse Core Ops, SparseCore 0:
  11.9 144.5 all-gather.2
  189.9 33.4 reduce-scatter.2
  237.4 49.7 all-gather.4
  289.5 38.0 reduce-scatter.4

commit v4 on v3

--- a/solution.py
+++ b/solution.py
@@ -427,7 +427,7 @@
 
 
 def lat_backward_body(
-    sc, gin, lg, w, e_h, n_h, i_h, s_h, act_h, a_h, p_h, gmix, pack_o, g1c_o, gains_o,
+    sc, gin, lg, w, e_h, n_h, i_h, s_h, act_h, a_h, p_h, nf, gmix, pack_o, g1c_o, gains_o,
     slots, ns, vs, ss, acts, qs, ps, acc, acc2, acc3, gh, gw, wsem, lsem,
 ):
     order = [8, 7, 6, 3, 4, 5, 2, 1, 0]
@@ -539,7 +539,7 @@
     gains_o[...] = as_rows(gain_rows, 32)
 
 
-def key_value_back_body(sc, rcv, lg, n_h, i_h, w, out, gain_o, wbuf, nbuf, ibuf, sem):
+def key_value_back_body(sc, rcv, lg, n_h, i_h, w, mark, out, gain_o, wbuf, nbuf, ibuf, sem):
     rows = pl.ds(pl.multiple_of(sc[1] * 16, 16), 16)
     copies = []
     for k, m in enumerate((9, 10)):
@@ -567,7 +567,7 @@
         out[j, 0:160, :] = g
 
 
-def dec_weights_body(mix, cot, nd, gq, out, buf, sem):
+def dec_weights_body(mix, cot, nd, gq, after, out, mark, buf, sem):
     g = half(dot_tn(mix[...], cot[...]))
     for i in range(NI):
         for t in range(6):
@@ -581,6 +581,7 @@
             buf[i, r : r + 96, :] = g[96 * i : 96 * i + 96, 128 * t : 128 * t + 128]
     two = pltpu.make_async_copy(buf.at[:, 960:1920, :], out.at[:, 960:1920, :], sem.at[1])
     two.start()
+    mark[...] = jnp.zeros_like(mark)
     one.wait()
     two.wait()
 
@@ -790,6 +791,7 @@
     rcv = exchange(pay.reshape(NJ, 16, D + 128), BLK)
     (mine,) = call(combine_body, [((16, D + 128), BF, "v")], [(rcv, "v")], name="combine")
     e = lax.all_gather(mine, BLK, axis=0, tiled=True)
+    nf = lax.all_gather(nb, BLK, axis=0, tiled=True)
 
     big = (NJ, 80, D)
     res, gqin, gd, dpay, mix, nd, gq, z_h, h_h, a_h = call(
@@ -858,10 +860,10 @@
         flops=5e9,
         name="prepare",
     )
-    (dw,) = call(
+    dw, mark = call(
         dec_weights_body,
-        [((NI, 1920, 128), BF, "h")],
-        [(mix, "v"), (cot, "v"), (nd, "v"), (gq, "v")],
+        [((NI, 1920, 128), BF, "h"), ((8, 128), F32, "v")],
+        [(mix, "v"), (cot, "v"), (nd, "v"), (gq, "v"), (i_h, "h")],
         [pltpu.VMEM((NI, 1920, 128), BF), DMA((2,))],
         vmem=60,
         flops=4e9,
@@ -870,21 +872,19 @@
     kv, gc = call(
         key_value_back_body,
         [((NJ, 192, 128), BF, "v"), ((1, D), F32, "v")],
-        [(sc, "s"), (rows, "v"), (lg, "v"), (n_h, "h"), (i_h, "h"), (w, "h")],
+        [(sc, "s"), (rows, "v"), (lg, "v"), (n_h, "h"), (i_h, "h"), (w, "h"), (mark, "v")],
         [pltpu.VMEM((2,) + big, BF), pltpu.VMEM((16, D), BF), pltpu.VMEM((16, 128), F32), DMA((6,))],
-        vmem=58,
+        vmem=16,
         flops=1e8,
         name="key_value_back",
     )
     gin4 = exchange(kv, BLK)
-    nb, _ = lax.optimization_barrier((nb, gin4))
-    nf = lax.all_gather(nb, BLK, axis=0, tiled=True)
     dw = lax.psum_scatter(dw.reshape(NI * 1920, 128), BATCH, scatter_dimension=0, tiled=True)
 
     gmix, pack, g1c, lat_gain = call(
         lat_backward_body,
         [((R, D), BF, "v"), ((D, 1024), BF, "v"), ((R, 128), BF, "v"), ((32, 128), F32, "v")],
-        [(sc, "s"), (gin4, "v"), (lg, "v")] + [(v, "h") for v in (w, e, n_h, i_h, s_h, act_h, a_h, p_h)],
+        [(sc, "s"), (gin4, "v"), (lg, "v")] + [(v, "h") for v in (w, e, n_h, i_h, s_h, act_h, a_h, p_h, nf)],
         [
             pltpu.VMEM((5,) + big, BF),
             pltpu.VMEM((4, R, D), BF),

time: 354 us -> 362 us (1.023)
  blocking collectives: 57.6 us -> 75.5 us
  waiting for transfers between devices: 128 us -> 113 us
    all_to_all x2, blocking collectives: 33.4 us -> 51.9 us  [exchange(): lax.all_to_all(flat, axes, split_axis=0, concat_axis=0, tiled=True)]
    all_to_all x3, waiting for transfers between devices: 47.5 us -> 38.1 us  [exchange(): lax.all_to_all(flat, axes, split_axis=0, concat_axis=0, tiled=True)]
    all_gather x1, waiting for transfers between devices: 6.2 us -> 0.02 us  [shards(): nf = lax.all_gather(nb, BLK, axis=0, tiled=True)]
  transfers between devices with their start and end apart: 17 -> 17, of which waited for: 13 -> 11; matrix products, arithmetic and copies ran while one was open for 0% -> 0% of each run, Pallas kernels for 20% -> 29%
where the time goes in v4:
time: 362 us; the launch traced here: 355 us
  waiting for transfers between devices  113 us (31%)
  Pallas kernels  107 us (30%)
  blocking collectives  75.5 us (21%)
  starting transfers between devices  37 us (10%)
  between operations  14.9 us (4%)
  local copies, waits for them, and re-layouts  6.53 us (2%)
    pallas_call x11, Pallas kernels, call(): pl.pallas_call(body, out_shape=[jax.ShapeDtypeStruct(s, t) for s, t, _ in...  107 us
    all_to_all x2, blocking collectives, exchange(): lax.all_to_all(flat, axes, split_axis=0, concat_axis=0, tiled=True)  51.9 us
    all_gather x1, waiting for transfers between devices, shards(): w = lax.all_gather(wsh, AXES, axis=0, tiled=True).reshape(NI, NJ, ROWS_I, D)  42.9 us
    all_to_all x3, waiting for transfers between devices, exchange(): lax.all_to_all(flat, axes, split_axis=0, concat_axis=0, tiled=True)  38.1 us
    ppermute x6, waiting for transfers between devices, step(): return [lax.ppermute(v, AXES, along(stage, d)) for d in (1, 2, 3)]  29.5 us
    all_gather x1, blocking collectives, shards(): e = lax.all_gather(mine, BLK, axis=0, tiled=True)  23.6 us
    all_to_all x3, starting transfers between devices, exchange(): lax.all_to_all(flat, axes, split_axis=0, concat_axis=0, tiled=True)  20.2 us
    ppermute x6, starting transfers between devices, step(): return [lax.ppermute(v, AXES, along(stage, d)) for d in (1, 2, 3)]  8.75 us
  transfers between devices with their start and end apart: 17, of which 11 were waited for; matrix products, arithmetic and copies ran while one was open for 0% of the time, Pallas kernels for 29%

profile of v4, /device:TPU:1, one launch (start us, length us, event | category | flops | bytes accessed | tf_op | source)
XLA Modules:
  0.0 355.3 jit_solution(2906063238191036977)
XLA Ops:
  8.5 3.3 pack.1
  11.9 4.7 %collective-permute-start.2 = (bf16[192,640]{1,0:T(8,128)(2,1)}, bf16[192,640]{1,0:T(8,128)(2,1)S(1)}, u32[]{:S(2)}, u32[]{:S(2)}) collective-permute-start(bf16[192,640]{1,0:T(8,128)(2,1)} %get-tuple-element.52), channel_id=1, source_target_pairs={{0,12},{1,13},{2,14},{3,15},{4,0},{5,1},{6,2},{7,3},{8,4},{9,5},{1... | collective-permute-start | bytes 737288 | tf_op jit(solution)/shard_map/ppermute | solution.py:770
  17.2 5.4 %collective-permute-done.2 = bf16[192,640]{1,0:T(8,128)(2,1)S(1)} collective-permute-done((bf16[192,640]{1,0:T(8,128)(2,1)}, bf16[192,640]{1,0:T(8,128)(2,1)S(1)}, u32[]{:S(2)}, u32[]{:S(2)}) %collective-permute-start.2) | collective-permute-done | bytes 245792 | tf_op jit(solution)/shard_map/ppermute | solution.py:770
  30.4 2.8 collective-permute-start.6
  33.2 20.0 %collective-permute-done.5.t3 = bf16[4,192,640]{2,1,0:T(8,128)(2,1)S(1)} collective-permute-done((bf16[4,192,640]{2,1,0:T(8,128)(2,1)S(1)}, bf16[4,192,640]{2,1,0:T(8,128)(2,1)S(1)}, u32[]{:S(2)}, u32[]{:S(2)}) %collective-permute-start.5) | collective-permute-done | bytes 983072 | tf_op jit(solution)/shard_map/ppermute | solution.py:770
  53.2 2.4 collective-permute-start.9
  62.2 9.1 %enc.1 = (bf16[16,192,1280]{2,1,0:T(8,128)(2,1)}, bf16[128,768]{1,0:T(8,128)(2,1)}, bf16[128,1280]{1,0:T(8,128)(2,1)}, bf16[128,1280]{1,0:T(8,128)(2,1)}, bf16[2...) custom-call(s32[6]{0:T(128)} %stack.38.sc, bf16[4,192,640]{2,1,0:T(8,128)(2,1)} %copy-done.10, ...), custom_call_target="tpu_custom_call" | custom-call | flops 3000000000 | bytes 4194304 | tf_op jit(solution)/shard_map/enc/pallas_call | solution.py:113
  71.3 18.0 %all_to_all.36.rcv = bf16[16,16,1408]{2,1,0:T(8,128)(2,1)S(1)} all-to-all(bf16[16,16,1408]{2,1,0:T(8,128)(2,1)} %bitcast.26), channel_id=1, replica_groups=mesh['y'=4,'core'=2,'x'=4,'z'=4] {'x','z'}, dimensions={0} | all-to-all | bytes 1441792 | tf_op jit(solution)/shard_map/all_to_all | solution.py:750
  89.8 23.6 %all_gather.9.e_h = bf16[256,1408]{1,0:T(8,128)(2,1)} all-gather(bf16[16,1408]{1,0:T(8,128)(2,1)S(1)} %combine.1), channel_id=1, replica_groups=mesh['y'=4,'core'=2,'x'=4,'z'=4] {'x','z'}, dimensions={0}, use_global_device_ids=true | all-gather | bytes 765952 | tf_op jit(solution)/shard_map/all_gather | solution.py:793
  113.4 42.9 %all-gather.3.cloned.1.call-done = bf16[16384,1280]{1,0:T(8,128)(2,1)} async-done(((bf16[128,1280]{1,0:T(8,128)(2,1)}), bf16[16384,1280]{1,0:T(8,128)(2,1)}) %all-gather.3.cloned.1.call-update) | async-done | bytes 41943056 | tf_op jit(solution)/shard_map/all_gather | solution.py:767
  156.3 29.1 %forward.1 = (bf16[128,768]{1,0:T(8,128)(2,1)}, f32[128,768]{1,0:T(8,128)}, f32[1,768]{1,0:T(1,128)}, bf16[256,2560]{1,0:T(8,128)(2,1)}, bf16[128,1280]{1,0:T(8,...) custom-call(bf16[128,768]{1,0:T(8,128)(2,1)} %bitcast.34, ...), custom_call_target="tpu_custom_call" | custom-call | flops 15000000512 | bytes 4194304 | tf_op jit(solution)/shard_map/forward/pallas_call | solution.py:113
  185.4 4.7 %all-to-all-start.1 = ((bf16[16,16,2560]{2,1,0:T(8,128)(2,1)}), bf16[16,16,2560]{2,1,0:T(8,128)(2,1)S(1)}, u32[]{:S(2)}, u32[]{:S(2)}) async-start(bf16[16,16,2560]{2,1,0:T(8,128)(2,1)} %bitcast.25), calls=%async_computation.1 | async-start | bytes 2621440 | tf_op jit(solution)/shard_map/all_to_all | solution.py:750
  190.1 8.1 %prepare.1 = (bf16[4,256,1280]{2,1,0:T(8,128)(2,1)}, f32[4,256,128]{2,1,0:T(8,128)}, f32[2,256,1280]{2,1,0:T(8,128)}, bf16[6,256,1280]{2,1,0:T(8,128)(2,1)}, bf16[8,256,256]{2,1,0:T(8,128)(2,1)}) custom-call(f32[5,1280]{1,0:T(8,128)} %lg.13, bf16[4,256,1280]{2,1,0:T(8,128)(2,1)} %get-tuple-element.59.z_h, bf16[2,256,1280]{2,1,0:T(8,128)(2,1)} %get-tuple-element.60.h_h, ...), custom_call_target="tpu_custom_call" | custom-call | flops 5000000000 | bytes 4194304 | tf_op jit(solution)/shard_map/prepare/pallas_call | solution.py:113
  198.2 4.6 %dec_weights.1 = (bf16[8,1920,128]{2,1,0:T(8,128)(2,1)}, f32[8,128]{1,0:T(8,128)}) custom-call(bf16[128,1280]{1,0:T(8,128)(2,1)} %get-tuple-element.64.mix, bf16[128,768]{1,0:T(8,128)(2,1)} %bitcast.36, bf16[128,768]{1,0:T(8,128)(2,1)} %get-tuple-element.65.nd, bf16[128,1280]{1,0:T(8,128)(2,1)} %get-tuple-element.66.gq, ...), custom_call_target="tpu_custom_call" | custom-call | flops 4000000000 | bytes 4194304 | tf_op jit(solution)/shard_map/dec_weights/pallas_call | solution.py:113
  202.9 14.7 %all-to-all-done.1.rcv = bf16[16,16,2560]{2,1,0:T(8,128)(2,1)S(1)} async-done(((bf16[16,16,2560]{2,1,0:T(8,128)(2,1)}), bf16[16,16,2560]{2,1,0:T(8,128)(2,1)S(1)}, u32[]{:S(2)}, u32[]{:S(2)}) %all-to-all-start.1) | async-done | bytes 1310752 | tf_op jit(solution)/shard_map/all_to_all | solution.py:750
  220.0 6.3 %key_value_back.1 = (bf16[16,192,128]{2,1,0:T(8,128)(2,1)}, f32[1,1280]{1,0:T(1,128)S(1)}) custom-call(s32[6]{0:T(128)S(1)} %copy-done.7, bf16[16,16,2560]{2,1,0:T(8,128)(2,1)S(1)} %all-to-all-done.1.rcv, f32[5,1280]{1,0:T(8,128)S(1)} %copy-done.2, bf16[4,256,1280]{2,1,0:T(8,128)(2,1)S(1)} %copy-done, f32[4,256,128]{2,1,0:T(8,128)S(1)} %copy-done.1, ...), custom_call_target="tpu_custom_call" | custom-call | flops 100000000 | bytes 4194304 | tf_op jit(solution)/shard_map/key_value_back/pallas_call | solution.py:113
  227.0 5.9 %all-to-all-start.2 = ((bf16[16,192,128]{2,1,0:T(8,128)(2,1)}), bf16[16,192,128]{2,1,0:T(8,128)(2,1)S(1)}, u32[]{:S(2)}, u32[]{:S(2)}) async-start(bf16[16,192,128]{2,1,0:T(8,128)(2,1)} %get-tuple-element.69), calls=%async_computation.2 | async-start | bytes 1572864 | tf_op jit(solution)/shard_map/all_to_all | solution.py:750
  233.8 11.8 %all-to-all-done.2.gin = bf16[16,192,128]{2,1,0:T(8,128)(2,1)S(1)} async-done(((bf16[16,192,128]{2,1,0:T(8,128)(2,1)}), bf16[16,192,128]{2,1,0:T(8,128)(2,1)S(1)}, u32[]{:S(2)}, u32[]{:S(2)}) %all-to-all-start.2) | async-done | bytes 786464 | tf_op jit(solution)/shard_map/all_to_all | solution.py:750
  246.5 29.4 %lat_backward.1 = (bf16[256,1280]{1,0:T(8,128)(2,1)}, bf16[1280,1024]{1,0:T(8,128)(2,1)}, bf16[256,128]{1,0:T(8,128)(2,1)}, f32[32,128]{1,0:T(8,128)}) custom-call(s32[6]{0:T(128)} %stack.38.sc, bf16[16,192,128]{2,1,0:T(8,128)(2,1)} %copy-done.11, f32[5,1280]{1,0:T(8,128)} %lg.13, bf16[8,16,128,1280]{3,2,1,0:T(8,128)(2,1)} %bitcast.23, ...), custom_call_target="tpu_custom_call" | custom-call | flops 80000000000 | bytes 4194304 | tf_op jit(solution)/shard_map/lat_backward/pallas_call | solution.py:113
  276.0 10.0 %enc_back.1 = (f32[128,768]{1,0:T(8,128)}, bf16[16,640,128]{2,1,0:T(8,128)(2,1)}) custom-call(s32[6]{0:T(128)} %stack.38.sc, bf16[128,768]{1,0:T(8,128)(2,1)} %bitcast.32, f32[2,768]{1,0:T(2,128)} %bg.5, f32[5,1280]{1,0:T(8,128)} %lg.13, f32[1,768]{1,0:T(1,128)} %get-tuple-element.57.gd, f32[1,1280]{1,0:T(1,128)} %copy-done.8, ...), custom_call_target="tpu_custom_call" | custom-call | flops 3000000000 | bytes 4194304 | tf_op jit(solution)/shard_map/enc_back/pallas_call | solution.py:113
  286.0 33.9 %all_to_all.37.rcv = bf16[16,640,128]{2,1,0:T(8,128)(2,1)S(1)} all-to-all(bf16[16,640,128]{2,1,0:T(8,128)(2,1)} %get-tuple-element.81), channel_id=1, replica_groups=mesh['y'=4,'core'=2,'x'=4,'z'=4] {'x','z'}, dimensions={0} | all-to-all | bytes 5242880 | tf_op jit(solution)/shard_map/all_to_all | solution.py:750
  320.0 5.1 %tail_one.1 = (bf16[8,352,128]{2,1,0:T(8,128)(2,1)}, f32[48,160]{1,0:T(8,128)}, f32[80,96]{1,0:T(8,128)S(1)}) custom-call(bf16[16,640,128]{2,1,0:T(8,128)(2,1)S(1)} %all_to_all.37.rcv, bf16[2048,768]{1,0:T(8,128)(2,1)} %all-gather.5.cloned.1.call-done.nf.nf_h, bf16[16,192,1280]{2,1,0:T(8,128)(2,1)} %get-tuple-element.54.g_all, f32[5,1280]{1,0:T(8,128)S(1)} %copy-done.3, ...), custom_call_target="tpu_custom_call" | custom-call | bytes 4194304 | tf_op jit(solution)/shard_map/tail_one/pallas_call | solution.py:113
  325.1 9.6 %all-to-all-start.4 = ((bf16[8,352,128]{2,1,0:T(8,128)(2,1)}), bf16[8,352,128]{2,1,0:T(8,128)(2,1)S(1)}, u32[]{:S(2)}, u32[]{:S(2)}) async-start(bf16[8,352,128]{2,1,0:T(8,128)(2,1)} %get-tuple-element.84), calls=%async_computation.5 | async-start | bytes 1441792 | tf_op jit(solution)/shard_map/all_to_all | solution.py:750
  334.7 11.6 %all-to-all-done.4.rcv = bf16[8,352,128]{2,1,0:T(8,128)(2,1)S(1)} async-done(((bf16[8,352,128]{2,1,0:T(8,128)(2,1)}), bf16[8,352,128]{2,1,0:T(8,128)(2,1)S(1)}, u32[]{:S(2)}, u32[]{:S(2)}) %all-to-all-start.4) | async-done | bytes 720928 | tf_op jit(solution)/shard_map/all_to_all | solution.py:750
  (68 shorter events, 23.5 us)
Async XLA Ops:
  7.2 149.1 %all-gather.3.cloned.1.call-start = ((), (), s32[]{:S(2)}) async-start(), calls=%async_computation.7 | async-start | bytes 42270720 | tf_op jit(solution)/shard_map/all_gather | solution.py:767
  11.8 222.0 %all-gather.5.cloned.1.call-start = ((), (), s32[]{:S(2)}) async-start(), calls=%async_computation.8 | async-start | bytes 3342336 | tf_op jit(solution)/shard_map/all_gather | solution.py:794
  11.9 10.7 %collective-permute-start.2 = (bf16[192,640]{1,0:T(8,128)(2,1)}, bf16[192,640]{1,0:T(8,128)(2,1)S(1)}, u32[]{:S(2)}, u32[]{:S(2)}) collective-permute-start(bf16[192,640]{1,0:T(8,128)(2,1)} %get-tuple-element.52), channel_id=1, source_target_pairs={{0,12},{1,13},{2,14},{3,15},{4,0},{5,1},{6,2},{7,3},{8,4},{9,5},{1... | collective-permute-start | bytes 737288 | tf_op jit(solution)/shard_map/ppermute | solution.py:770
  16.5 7.1 %collective-permute-start.1 = (bf16[192,640]{1,0:T(8,128)(2,1)}, bf16[192,640]{1,0:T(8,128)(2,1)S(1)}, u32[]{:S(2)}, u32[]{:S(2)}) collective-permute-start(bf16[192,640]{1,0:T(8,128)(2,1)} %get-tuple-element.52), channel_id=1, source_target_pairs={{0,8},{1,9},{2,10},{3,11},{4,12},{5,13},{6,14},{7,15},{8,0},{9,1},... | collective-permute-start | bytes 737288 | tf_op jit(solution)/shard_map/ppermute | solution.py:770
  16.5 9.4 %collective-permute-start = (bf16[192,640]{1,0:T(8,128)(2,1)}, bf16[192,640]{1,0:T(8,128)(2,1)S(1)}, u32[]{:S(2)}, u32[]{:S(2)}) collective-permute-start(bf16[192,640]{1,0:T(8,128)(2,1)} %get-tuple-element.52), channel_id=1, source_target_pairs={{0,4},{1,5},{2,6},{3,7},{4,8},{5,9},{6,10},{7,11},{8,12},{9,13},{1... | collective-permute-start | bytes 737288 | tf_op jit(solution)/shard_map/ppermute | solution.py:770
  27.0 35.2 %copy-start.10 = (bf16[4,192,640]{2,1,0:T(8,128)(2,1)}, bf16[4,192,640]{2,1,0:T(8,128)(2,1)S(1)}, u32[]{:S(2)}) copy-start(bf16[4,192,640]{2,1,0:T(8,128)(2,1)S(1)} %pad_maximum_fusion.t0) | copy-start | bytes 2949124
  27.0 26.2 %collective-permute-start.5 = (bf16[4,192,640]{2,1,0:T(8,128)(2,1)S(1)}, bf16[4,192,640]{2,1,0:T(8,128)(2,1)S(1)}, u32[]{:S(2)}, u32[]{:S(2)}) collective-permute-start(bf16[4,192,640]{2,1,0:T(8,128)(2,1)S(1)} %pad_maximum_fusion.t0), channel_id=1, source_target_pairs={{0,3},{1,0},{2,1},{3,2},{4,7},{5,4},{6,5},{7,6},{8,11},{9,8},{10,9... | collective-permute-start | bytes 2949128 | tf_op jit(solution)/shard_map/ppermute | solution.py:770
  29.3 26.4 %collective-permute-start.4 = (bf16[4,192,640]{2,1,0:T(8,128)(2,1)S(1)}, bf16[4,192,640]{2,1,0:T(8,128)(2,1)S(1)}, u32[]{:S(2)}, u32[]{:S(2)}) collective-permute-start(bf16[4,192,640]{2,1,0:T(8,128)(2,1)S(1)} %pad_maximum_fusion.t0), channel_id=1, source_target_pairs={{0,2},{1,3},{2,0},{3,1},{4,6},{5,7},{6,4},{7,5},{8,10},{9,11},{10,... | collective-permute-start | bytes 2949128 | tf_op jit(solution)/shard_map/ppermute | solution.py:770
  29.8 26.8 %collective-permute-start.3 = (bf16[4,192,640]{2,1,0:T(8,128)(2,1)S(1)}, bf16[4,192,640]{2,1,0:T(8,128)(2,1)S(1)}, u32[]{:S(2)}, u32[]{:S(2)}) collective-permute-start(bf16[4,192,640]{2,1,0:T(8,128)(2,1)S(1)} %pad_maximum_fusion.t0), channel_id=1, source_target_pairs={{0,1},{1,2},{2,3},{3,0},{4,5},{5,6},{6,7},{7,4},{8,9},{9,10},{10,1... | collective-permute-start | bytes 2949128 | tf_op jit(solution)/shard_map/ppermute | solution.py:770
  30.4 28.6 %collective-permute-start.6 = (bf16[4,192,640]{2,1,0:T(8,128)(2,1)S(1)}, bf16[4,192,640]{2,1,0:T(8,128)(2,1)S(1)}, u32[]{:S(2)}, u32[]{:S(2)}) collective-permute-start(bf16[4,192,640]{2,1,0:T(8,128)(2,1)S(1)} %pad_maximum_fusion.t0), channel_id=1, source_target_pairs={{0,16},{1,17},{2,18},{3,19},{4,20},{5,21},{6,22},{7,23},{8,24},{9,... | collective-permute-start | bytes 2949128 | tf_op jit(solution)/shard_map/ppermute | solution.py:774
  53.2 5.8 %collective-permute-start.9 = (bf16[4,192,640]{2,1,0:T(8,128)(2,1)S(1)}, bf16[4,192,640]{2,1,0:T(8,128)(2,1)S(1)}, u32[]{:S(2)}, u32[]{:S(2)}) collective-permute-start(bf16[4,192,640]{2,1,0:T(8,128)(2,1)S(1)} %collective-permute-done.5.t3), channel_id=1, source_target_pairs={{0,16},{1,17},{2,18},{3,19},{4,20},{5,21},{6,22},{7,23},{8,24},{9,... | collective-permute-start | bytes 2949128 | tf_op jit(solution)/shard_map/ppermute | solution.py:774
  55.7 3.6 %collective-permute-start.8 = (bf16[4,192,640]{2,1,0:T(8,128)(2,1)S(1)}, bf16[4,192,640]{2,1,0:T(8,128)(2,1)S(1)}, u32[]{:S(2)}, u32[]{:S(2)}) collective-permute-start(bf16[4,192,640]{2,1,0:T(8,128)(2,1)S(1)} %collective-permute-done.4.t2), channel_id=1, source_target_pairs={{0,16},{1,17},{2,18},{3,19},{4,20},{5,21},{6,22},{7,23},{8,24},{9,... | collective-permute-start | bytes 2949128 | tf_op jit(solution)/shard_map/ppermute | solution.py:774
  56.6 4.6 %collective-permute-start.7 = (bf16[4,192,640]{2,1,0:T(8,128)(2,1)S(1)}, bf16[4,192,640]{2,1,0:T(8,128)(2,1)S(1)}, u32[]{:S(2)}, u32[]{:S(2)}) collective-permute-start(bf16[4,192,640]{2,1,0:T(8,128)(2,1)S(1)} %collective-permute-done.3.t1), channel_id=1, source_target_pairs={{0,16},{1,17},{2,18},{3,19},{4,20},{5,21},{6,22},{7,23},{8,24},{9,... | collective-permute-start | bytes 2949128 | tf_op jit(solution)/shard_map/ppermute | solution.py:774
  185.4 32.2 %all-to-all-start.1 = ((bf16[16,16,2560]{2,1,0:T(8,128)(2,1)}), bf16[16,16,2560]{2,1,0:T(8,128)(2,1)S(1)}, u32[]{:S(2)}, u32[]{:S(2)}) async-start(bf16[16,16,2560]{2,1,0:T(8,128)(2,1)} %bitcast.25), calls=%async_computation.1 | async-start | bytes 2621440 | tf_op jit(solution)/shard_map/all_to_all | solution.py:750
  198.2 19.4 %copy-start.1 = (f32[4,256,128]{2,1,0:T(8,128)S(1)}, f32[4,256,128]{2,1,0:T(8,128)}, u32[]{:S(2)}) copy-start(f32[4,256,128]{2,1,0:T(8,128)} %get-tuple-element.63.after.i_h) | copy-start | bytes 1572868
  198.2 19.4 %copy-start.2 = (f32[5,1280]{1,0:T(8,128)S(1)}, f32[5,1280]{1,0:T(8,128)}, u32[]{:S(2)}) copy-start(f32[5,1280]{1,0:T(8,128)} %lg.13) | copy-start | bytes 76804
  198.2 19.4 %copy-start.7 = (s32[6]{0:T(128)S(1)}, s32[6]{0:T(128)}, u32[]{:S(2)}) copy-start(s32[6]{0:T(128)} %stack.38.sc) | copy-start | bytes 76
  227.0 18.7 %all-to-all-start.2 = ((bf16[16,192,128]{2,1,0:T(8,128)(2,1)}), bf16[16,192,128]{2,1,0:T(8,128)(2,1)S(1)}, u32[]{:S(2)}, u32[]{:S(2)}) async-start(bf16[16,192,128]{2,1,0:T(8,128)(2,1)} %get-tuple-element.69), calls=%async_computation.2 | async-start | bytes 1572864 | tf_op jit(solution)/shard_map/all_to_all | solution.py:750
  232.9 43.1 %reduce-scatter.3.cloned.1.call-start = ((), (), s32[]{:S(2)}) async-start(), calls=%async_computation.9 | async-start | bytes 4423680 | tf_op jit(solution)/shard_map/reduce_scatter | solution.py:882
  233.6 101.1 %reduce-scatter.5.cloned.1.call-start = ((), (), s32[]{:S(2)}) async-start(), calls=%async_computation.10 | async-start | bytes 2949120 | tf_op jit(solution)/shard_map/reduce_scatter | solution.py:908
  286.0 34.0 %copy-start.3 = (f32[5,1280]{1,0:T(8,128)S(1)}, f32[5,1280]{1,0:T(8,128)}, u32[]{:S(2)}) copy-start(f32[5,1280]{1,0:T(8,128)} %lg.13) | copy-start | bytes 76804
  286.0 34.0 %copy-start.5 = (bf16[256,128]{1,0:T(8,128)(2,1)S(1)}, bf16[256,128]{1,0:T(8,128)(2,1)}, u32[]{:S(2)}) copy-start(bf16[256,128]{1,0:T(8,128)(2,1)} %get-tuple-element.83.g1c) | copy-start | bytes 196612
  286.0 33.9 %copy-start.6 = (f32[32,128]{1,0:T(8,128)S(1)}, f32[32,128]{1,0:T(8,128)}, u32[]{:S(2)}) copy-start(f32[32,128]{1,0:T(8,128)} %get-tuple-element.82.lat_gain) | copy-start | bytes 49156
  325.1 21.2 %all-to-all-start.4 = ((bf16[8,352,128]{2,1,0:T(8,128)(2,1)}), bf16[8,352,128]{2,1,0:T(8,128)(2,1)S(1)}, u32[]{:S(2)}, u32[]{:S(2)}) async-start(bf16[8,352,128]{2,1,0:T(8,128)(2,1)} %get-tuple-element.84), calls=%async_computation.5 | async-start | bytes 1441792 | tf_op jit(solution)/shard_map/all_to_all | solution.py:750
  (12 other events, 33.3 us)
Sparse Core Ops, SparseCore 0:
  11.9 144.3 all-gather.2
  158.5 60.8 all-gather.4
  236.1 36.1 reduce-scatter.2
  276.1 32.2 reduce-scatter.4

commit v5 on v3

--- a/solution.py
+++ b/solution.py
@@ -125,18 +125,23 @@
 DMA = pltpu.SemaphoreType.DMA
 
 
-def pack_body(sc, lm, om, bm, do, la, g0, wsh, buf, sem):
-    i, core = sc[0], sc[4]
-    cols = pl.ds(pl.multiple_of(core * 640, 128), 640)
-    first = [
+def pack_early_body(sc, lm, bm, la, g0, sem):
+    cols = pl.ds(pl.multiple_of(sc[4] * 640, 128), 640)
+    copies = [
         (bm.at[0, :, cols], g0.at[0:48, :]),
         (bm.at[1, :, cols], g0.at[48:96, :]),
         (lm.at[0, :, cols], g0.at[96:176, :]),
         (la.at[:, cols], g0.at[176:192, :]),
     ]
-    first = [pltpu.make_async_copy(a, b, sem.at[8 + k]) for k, (a, b) in enumerate(first)]
-    for c in first:
+    copies = [pltpu.make_async_copy(a, b, sem.at[k]) for k, (a, b) in enumerate(copies)]
+    for c in copies:
         c.start()
+    for c in copies:
+        c.wait()
+
+
+def pack_body(sc, lm, om, bm, do, wsh, buf, sem):
+    i = sc[0]
     blocks = [(80 * k, 80, (om if s == "o" else lm), n, D) for k, (s, n) in enumerate(SQUARE)]
     blocks += [(DEC_ROW, 80, do, None, DI), (BQ_ROW, 48, bm, 2, D)]
     for k in range(NI):
@@ -156,31 +161,32 @@
             for c in cs:
                 c.wait()
 
-    out = pltpu.make_async_copy(buf, wsh, sem.at[12])
+    out = pltpu.make_async_copy(buf, wsh, sem.at[8])
     out.start()
-    for c in first:
-        c.wait()
     out.wait()
 
 
-def pieces_from(sc, groups):
+def pieces_from(sc, own, sib):
     x, z, core = sc[2], sc[3], sc[4]
     out = []
-    for side in range(2):
+    for side, (t0, t1, t2a, t2b, t3) in enumerate((own, sib)):
         c = core if side == 0 else 1 - core
         col = pl.ds(pl.multiple_of(c * 640, 128), 640)
         for e in range(4):
             for d in range(4):
                 xs = jnp.where(c == 0, (x + 4 - d) & 3, (x + 4 - e) & 3)
                 zs = jnp.where(c == 0, (z + 4 - e) & 3, (z + 4 - d) & 3)
-                out.append((xs * 4 + zs, col, groups[4 * side + e].at[d]))
+                ref = (t0, t1, None, t3)[e] if e != 2 else (t2a, t2b)[d // 2]
+                out.append((xs * 4 + zs, col, ref.at[d % 2 if e == 2 else d]))
     return out
 
 
-def enc_body(sc, t0, t1, t2, t3, u0, u1, u2, u3, x_in, bg, lg, g_out, nb_o, k_o, v_o, q_o, pay, gs, acc, sem):
+def enc_body(
+    sc, a0, a1, a2, a3, a4, b0, b1, b2, b3, b4, x_in, bg, lg, g_out, nb_o, k_o, v_o, q_o, pay, n_o, i_o, gs, acc, sem
+):
     copies = [
         pltpu.make_async_copy(src, gs.at[pos, :, col], sem.at[k])
-        for k, (pos, col, src) in enumerate(pieces_from(sc, (t0, t1, t2, t3, u0, u1, u2, u3)))
+        for k, (pos, col, src) in enumerate(pieces_from(sc, (a0, a1, a2, a3, a4), (b0, b1, b2, b3, b4)))
     ]
     for c in copies:
         c.start()
@@ -194,7 +200,9 @@
     k_o[...] = half(dot(nb, gs[:, 0:48, :].reshape(DI, D)))
     v_o[...] = half(dot(nb, gs[:, 48:96, :].reshape(DI, D)))
     z0b = gs[:, 176:192, :].reshape(R, D)
-    nq, _ = norm(z0b.astype(F32))
+    nq, inv = norm(z0b.astype(F32))
+    n_o[...] = half(nq)
+    i_o[...] = jnp.broadcast_to(inv, (R, 128))
     q_o[...] = half(dot(half(nq * lg[0:1, :]), gs[:, 96:176, :].reshape(D, D)))
     acc[...] = jnp.zeros_like(acc)
     valid = lanes(N) + sc[1] * N < sc[5]
@@ -602,10 +610,10 @@
 
 
 def enc_back_body(
-    sc, x_in, bg, lg, gd, gc, gmix_h, e_h, q_h, k_h, v_h, g_all, dw_h, gin_o, pay,
-    gmix, e, q, k, v, wkv, gq, gkt, gvt, dw, td, tb, sem,
+    sc, x_in, bg, lg, gd, gc, gmix_h, e_h, q_h, k_h, v_h, g_all, dw_h, n0_h, i0_h, gin_o, pay,
+    gmix, e, q, k, v, wkv, n0, i0, gq, gkt, gvt, dw, td, tb, sem,
 ):
-    pairs = [(gmix_h, gmix), (q_h, q), (k_h, k), (v_h, v), (e_h, e), (g_all, wkv), (dw_h, dw)]
+    pairs = [(gmix_h, gmix), (q_h, q), (k_h, k), (v_h, v), (e_h, e), (g_all, wkv), (dw_h, dw), (n0_h, n0), (i0_h, i0)]
     loads = [pltpu.make_async_copy(a, b, sem.at[n]) for n, (a, b) in enumerate(pairs)]
     for c in loads:
         c.start()
@@ -635,8 +643,9 @@
     gqt = half(gqs.T)
     pay[:, 160:240, :] = gqt[:, 0:128].reshape(NJ, 80, 128)
     pay[:, 240:320, :] = gqt[:, 128:256].reshape(NJ, 80, 128)
-    n, inv = norm(wkv[:, 176:192, :].reshape(R, D).astype(F32))
-    gz, g0 = norm_back(dot_nt(half(gqs), wkv[:, 96:176, :].reshape(D, D)), lg[0:1, :], n, inv)
+    loads[7].wait()
+    loads[8].wait()
+    gz, g0 = norm_back(dot_nt(half(gqs), wkv[:, 96:176, :].reshape(D, D)), lg[0:1, :], n0[...].astype(F32), i0[:, 0:1])
     gzt = half(gz.T)
     pay[:, 0:80, :] = gzt[:, 0:128].reshape(NJ, 80, 128)
     pay[:, 80:160, :] = gzt[:, 128:256].reshape(NJ, 80, 128)
@@ -655,10 +664,10 @@
     spread(dw, pay, td, tb)
 
 
-def tail_one_body(rcv, nf_h, g_all, lg, lat_gain, g1c, out, dec_o, bq_o, nf, z0b, left, sem):
+def tail_one_body(rcv, nf_h, n0_h, lg, lat_gain, g1c, out, dec_o, bq_o, nf, n0, left, sem):
     loads = [
         pltpu.make_async_copy(nf_h, nf, sem.at[0]),
-        pltpu.make_async_copy(g_all.at[:, 176:192, :], z0b, sem.at[1]),
+        pltpu.make_async_copy(n0_h, n0, sem.at[1]),
     ]
     for c in loads:
         c.start()
@@ -669,7 +678,7 @@
         left[0:80, 128 * s : 128 * s + 128] = rcv[s, 320:400, :]
         left[128:208, 128 * s : 128 * s + 128] = rcv[s, 400:480, :]
     loads[1].wait()
-    nq = half(norm(z0b[...].reshape(R, D).astype(F32))[0] * lg[0:1, :])
+    nq = half(n0[...].astype(F32) * lg[0:1, :])
     a = jnp.concatenate([sums[160:240], fill], axis=0).T
     b = jnp.concatenate([sums[240:320], fill], axis=0).T
     w0 = dot_tn(nq, half(jnp.concatenate([a, b], axis=0)))
@@ -697,7 +706,9 @@
     dec_o[:, 128:160] = pltpu.roll(s[0:48], 32, 1)[:, 0:32]
 
 
-def tail_two_body(rcv, pack, bq, arr_o, lm_o, om_o, bm_o, lat_o, byte_o):
+def tail_two_body(rcv, pack_h, bq, arr_o, lm_o, om_o, bm_o, lat_o, byte_o, pack, sem):
+    load = pltpu.make_async_copy(pack_h, pack, sem)
+    load.start()
     sums = jnp.sum(rcv[...].astype(F32), axis=0)
     lm_o[0] = sums[0:160, 0:80]
     arr_o[...] = sums[160:192, 0:80]
@@ -715,6 +726,7 @@
         for b in range(5):
             r = {0: 12, 1: 32, 2: 42, 3: 52, 4: 22}[b] + t
             lat_o[b : b + 1, 128 * t : 128 * t + 128] = g[r : r + 1, :]
+    load.wait()
     for m, (kind, n) in enumerate(SQUARE):
         window, o = PLACE[m]
         v = pack[:, 256 * window : 256 * window + 256].astype(F32)
@@ -755,23 +767,30 @@
     sc = jnp.stack([i, j, x, z, core, lengths[0]]).astype(jnp.int32)
     xin, qin, cot = inputs[0], queries[0], cotangent[0]
 
-    g0, wsh = call(
+    (wsh,) = call(
         pack_body,
-        [((192, 640), BF, "v"), ((ROWS_I, D), BF, "h")],
-        [(sc, "s"), (latent_mats, "h"), (out_mats, "h"), (byte_mats, "h"), (dec_out, "h"), (latent_array, "h")],
-        [pltpu.VMEM((ROWS_I, D), BF), DMA((13,))],
+        [((ROWS_I, D), BF, "h")],
+        [(sc, "s"), (latent_mats, "h"), (out_mats, "h"), (byte_mats, "h"), (dec_out, "h")],
+        [pltpu.VMEM((ROWS_I, D), BF), DMA((9,))],
         vmem=60,
         name="pack",
     )
+    (g0,) = call(
+        pack_early_body,
+        [((192, 640), BF, "v")],
+        [(sc, "s"), (latent_mats, "h"), (byte_mats, "h"), (latent_array, "h")],
+        [DMA((4,))],
+        vmem=60,
+        name="pack_early",
+    )
     w = lax.all_gather(wsh, AXES, axis=0, tiled=True).reshape(NI, NJ, ROWS_I, D)
 
-    def step(v, stage):
-        return [lax.ppermute(v, AXES, along(stage, d)) for d in (1, 2, 3)]
-
-    s0 = jnp.stack([g0] + step(g0, 0))
-    own = [s0] + step(s0, 1)
+    s0 = jnp.stack([g0] + [lax.ppermute(g0, AXES, along(0, d)) for d in (1, 2, 3)])
+    t1, t3 = (lax.ppermute(s0, AXES, along(1, d)) for d in (1, 3))
+    t2a, t2b = lax.ppermute(t1[0:2], AXES, along(1, 1)), lax.ppermute(t3[2:4], AXES, along(1, 3))
+    own = [s0, t1, t2a, t2b, t3]
     sib = [lax.ppermute(v, AXES, SWAP) for v in own]
-    g_all, nb, k_b, v_b, q_b, pay = call(
+    g_all, nb, k_b, v_b, q_b, pay, n0, i0 = call(
         enc_body,
         [
             ((NJ, 192, D), BF, "h"),
@@ -780,6 +799,8 @@
             ((N, D), BF, "v"),
             ((R, D), BF, "v"),
             ((R, D + 128), BF, "v"),
+            ((R, D), BF, "v"),
+            ((R, 128), F32, "v"),
         ],
         [(sc, "s")] + [(v, "a") for v in own + sib] + [(xin, "v"), (bg, "v"), (lg, "v")],
         [pltpu.VMEM((NJ, 192, D), BF), pltpu.VMEM((R, D), F32), DMA((33,))],
@@ -808,7 +829,7 @@
         ],
         [(qin, "v"), (cot, "v"), (bg, "v"), (lg, "v"), (e, "h"), (g_all, "h"), (w, "h")],
         [
-            pltpu.VMEM((4,) + big, BF),
+            pltpu.VMEM((3,) + big, BF),
             pltpu.VMEM((R, D), BF),
             pltpu.VMEM((NJ, 16, D), BF),
             pltpu.VMEM((4, R, D), F32),
@@ -823,7 +844,7 @@
             pltpu.VMEM((N, D), F32),
             pltpu.VMEM((N, D), F32),
             pltpu.VMEM((2, R, D), F32),
-            DMA((4, 2)),
+            DMA((3, 2)),
             DMA((10,)),
             DMA((5,)),
         ],
@@ -886,7 +907,7 @@
         [((R, D), BF, "v"), ((D, 1024), BF, "v"), ((R, 128), BF, "v"), ((32, 128), F32, "v")],
         [(sc, "s"), (gin4, "v"), (lg, "v")] + [(v, "h") for v in (w, e, n_h, i_h, s_h, act_h, a_h, p_h)],
         [
-            pltpu.VMEM((5,) + big, BF),
+            pltpu.VMEM((2,) + big, BF),
             pltpu.VMEM((4, R, D), BF),
             pltpu.VMEM((4, R, 128), F32),
             pltpu.VMEM((2, R, D), F32),
@@ -898,7 +919,7 @@
             pltpu.VMEM((2, R, D), F32),
             pltpu.VMEM((R, D), BF),
             pltpu.VMEM((8, R, 256), BF),
-            DMA((5, 2)),
+            DMA((2, 2)),
             DMA((16,)),
         ],
         vmem=60,
@@ -910,7 +931,7 @@
         enc_back_body,
         [((N, DI), F32, "v"), ((NJ, 640, 128), BF, "v")],
         [(sc, "s"), (xin, "v"), (bg, "v"), (lg, "v"), (gd, "v"), (gc, "v")]
-        + [(v, "h") for v in (gmix, e, q_b, k_b, v_b, g_all, dw)],
+        + [(v, "h") for v in (gmix, e, q_b, k_b, v_b, g_all, dw, n0, i0)],
         [
             pltpu.VMEM((R, D), BF),
             pltpu.VMEM((R, D + 128), BF),
@@ -918,13 +939,15 @@
             pltpu.VMEM((N, D), BF),
             pltpu.VMEM((N, D), BF),
             pltpu.VMEM((NJ, 192, D), BF),
+            pltpu.VMEM((R, D), BF),
+            pltpu.VMEM((R, 128), F32),
             pltpu.VMEM((R, D), F32),
             pltpu.VMEM((D, N), BF),
             pltpu.VMEM((D, N), BF),
             pltpu.VMEM((1920, 128), BF),
             pltpu.VMEM((DI, 256), F32),
             pltpu.VMEM((D, 128), F32),
-            DMA((7,)),
+            DMA((9,)),
         ],
         vmem=58,
         flops=3e9,
@@ -934,8 +957,9 @@
     p2, dec_grad, bq_grad = call(
         tail_one_body,
         [((NI, 352, 128), BF, "v"), ((48, 160), F32, "v"), ((80, 96), F32, "v")],
-        [(r1, "v"), (nf, "h"), (g_all, "h"), (lg, "v"), (lat_gain, "v"), (g1c, "v")],
-        [pltpu.VMEM((NJ * N, DI), BF), pltpu.VMEM((NJ, 16, D), BF), pltpu.VMEM((256, 2048), BF), DMA((2,))],
+        [(r1, "v"), (nf, "h"), (n0, "h"), (lg, "v"), (lat_gain, "v"), (g1c, "v")],
+        [pltpu.VMEM((NJ * N, DI), BF), pltpu.VMEM((R, D), BF), pltpu.VMEM((256, 2048), BF), DMA((2,))],
+        vmem=52,
         name="tail_one",
     )
     r2 = exchange(p2, BATCH)
@@ -949,7 +973,8 @@
             ((5, D), F32, "v"),
             ((2, DI), F32, "v"),
         ],
-        [(r2, "v"), (pack, "v"), (bq_grad, "v")],
+        [(r2, "v"), (pack, "h"), (bq_grad, "v")],
+        [pltpu.VMEM((160, 1024), BF), DMA],
         name="tail_two",
     )
     byte_grads = jnp.swapaxes(byte_grads, 1, 2)

time: 354 us -> 359 us (1.014)
  the two profiles are of different devices: /device:TPU:1 before, /device:TPU:2 now
where the time goes in v5:
time: 359 us; the launch traced here: 352 us
  waiting for transfers between devices  121 us (34%)
  Pallas kernels  108 us (30%)
  blocking collectives  69.8 us (19%)
  starting transfers between devices  29.2 us (8%)
  between operations  14.9 us (4%)
  local copies, waits for them, and re-layouts  7.77 us (2%)
    pallas_call x12, Pallas kernels, call(): pl.pallas_call(body, out_shape=[jax.ShapeDtypeStruct(s, t) for s, t, _ in...  108 us
    all_to_all x2, blocking collectives, exchange(): lax.all_to_all(flat, axes, split_axis=0, concat_axis=0, tiled=True)  42.4 us
    all_gather x1, blocking collectives, shards(): e = lax.all_gather(mine, BLK, axis=0, tiled=True)  27.4 us
    all_gather x1, waiting for transfers between devices, shards(): nf = lax.all_gather(nb, BLK, axis=0, tiled=True)  25.4 us
    reduce_scatter x1, waiting for transfers between devices, shards(): pack = lax.psum_scatter(pack, BATCH, scatter_dimension=0, tiled=True)  20.2 us
    all_to_all x3, waiting for transfers between devices, exchange(): lax.all_to_all(flat, axes, split_axis=0, concat_axis=0, tiled=True)  20 us
    ppermute x1, waiting for transfers between devices, shards(): lax.ppermute(t3[2:4], AXES, along(1, 3))  16.2 us
    all_to_all x3, starting transfers between devices, exchange(): lax.all_to_all(flat, axes, split_axis=0, concat_axis=0, tiled=True)  15.6 us
  transfers between devices with their start and end apart: 19, of which 11 were waited for; matrix products, arithmetic and copies ran while one was open for 0% of the time, Pallas kernels for 20%

profile of v5, /device:TPU:2, one launch (start us, length us, event | category | flops | bytes accessed | tf_op | source)
XLA Modules:
  0.0 351.5 jit_solution(16821508515003566246)
XLA Ops:
  25.7 4.1 %collective-permute-start.5 = (bf16[4,192,640]{2,1,0:T(8,128)(2,1)S(1)}, bf16[4,192,640]{2,1,0:T(8,128)(2,1)S(1)}, u32[]{:S(2)}, u32[]{:S(2)}) collective-permute-start(bf16[4,192,640]{2,1,0:T(8,128)(2,1)S(1)} %pad_maximum_fusion.a0), channel_id=1, source_target_pairs={{0,3},{1,0},{2,1},{3,2},{4,7},{5,4},{6,5},{7,6},{8,11},{9,8},{10,9... | collective-permute-start | bytes 2949128 | tf_op jit(solution)/shard_map/ppermute | solution.py:789
  29.9 13.5 %collective-permute-done.5.a4 = bf16[4,192,640]{2,1,0:T(8,128)(2,1)S(1)} collective-permute-done((bf16[4,192,640]{2,1,0:T(8,128)(2,1)S(1)}, bf16[4,192,640]{2,1,0:T(8,128)(2,1)S(1)}, u32[]{:S(2)}, u32[]{:S(2)}) %collective-permute-start.5) | collective-permute-done | bytes 983072 | tf_op jit(solution)/shard_map/ppermute | solution.py:789
  43.4 3.8 %collective-permute-start.6 = (bf16[2,192,640]{2,1,0:T(8,128)(2,1)S(1)}, bf16[2,192,640]{2,1,0:T(8,128)(2,1)S(1)}, u32[]{:S(2)}, u32[]{:S(2)}) collective-permute-start(bf16[2,192,640]{2,1,0:T(8,128)(2,1)S(1)} %slice.9), channel_id=1, source_target_pairs={{0,3},{1,0},{2,1},{3,2},{4,7},{5,4},{6,5},{7,6},{8,11},{9,8},{10,9... | collective-permute-start | bytes 1474568 | tf_op jit(solution)/shard_map/ppermute | solution.py:790
  47.8 16.2 %collective-permute-done.6.a3 = bf16[2,192,640]{2,1,0:T(8,128)(2,1)S(1)} collective-permute-done((bf16[2,192,640]{2,1,0:T(8,128)(2,1)S(1)}, bf16[2,192,640]{2,1,0:T(8,128)(2,1)S(1)}, u32[]{:S(2)}, u32[]{:S(2)}) %collective-permute-start.6) | collective-permute-done | bytes 491552 | tf_op jit(solution)/shard_map/ppermute | solution.py:790
  64.0 4.3 %collective-permute-done.4.a2 = bf16[2,192,640]{2,1,0:T(8,128)(2,1)S(1)} collective-permute-done((bf16[2,192,640]{2,1,0:T(8,128)(2,1)S(1)}, bf16[2,192,640]{2,1,0:T(8,128)(2,1)S(1)}, u32[]{:S(2)}, u32[]{:S(2)}) %collective-permute-start.4) | collective-permute-done | bytes 491552 | tf_op jit(solution)/shard_map/ppermute | solution.py:790
  71.8 11.4 %enc.1 = (bf16[16,192,1280]{2,1,0:T(8,128)(2,1)}, bf16[128,768]{1,0:T(8,128)(2,1)}, bf16[128,1280]{1,0:T(8,128)(2,1)}, bf16[128,1280]{1,0:T(8,128)(2,1)}, bf16[2...) custom-call(s32[6]{0:T(128)} %stack.38.sc, ...), custom_call_target="tpu_custom_call" | custom-call | flops 3000000000 | bytes 4194304 | tf_op jit(solution)/shard_map/enc/pallas_call | solution.py:113
  83.3 24.7 %all_to_all.36.rcv = bf16[16,16,1408]{2,1,0:T(8,128)(2,1)S(1)} all-to-all(bf16[16,16,1408]{2,1,0:T(8,128)(2,1)} %bitcast.26), channel_id=1, replica_groups=mesh['y'=4,'core'=2,'x'=4,'z'=4] {'x','z'}, dimensions={0} | all-to-all | bytes 1441792 | tf_op jit(solution)/shard_map/all_to_all | solution.py:761
  108.6 27.4 %all_gather.9.e_h = bf16[256,1408]{1,0:T(8,128)(2,1)} all-gather(bf16[16,1408]{1,0:T(8,128)(2,1)S(1)} %combine.1), channel_id=1, replica_groups=mesh['y'=4,'core'=2,'x'=4,'z'=4] {'x','z'}, dimensions={0}, use_global_device_ids=true | all-gather | bytes 765952 | tf_op jit(solution)/shard_map/all_gather | solution.py:813
  135.9 15.1 %all-gather.3.cloned.1.call-done = bf16[16384,1280]{1,0:T(8,128)(2,1)} async-done(((bf16[128,1280]{1,0:T(8,128)(2,1)}), bf16[16384,1280]{1,0:T(8,128)(2,1)}) %all-gather.3.cloned.1.call-update) | async-done | bytes 41943056 | tf_op jit(solution)/shard_map/all_gather | solution.py:786
  151.1 27.7 %forward.1 = (bf16[128,768]{1,0:T(8,128)(2,1)}, f32[128,768]{1,0:T(8,128)}, f32[1,768]{1,0:T(1,128)}, bf16[256,2560]{1,0:T(8,128)(2,1)}, bf16[128,1280]{1,0:T(8,...) custom-call(bf16[128,768]{1,0:T(8,128)(2,1)} %bitcast.33, ...), custom_call_target="tpu_custom_call" | custom-call | flops 15000000512 | bytes 4194304 | tf_op jit(solution)/shard_map/forward/pallas_call | solution.py:113
  178.8 4.0 %dec_weights.1 = bf16[8,1920,128]{2,1,0:T(8,128)(2,1)} custom-call(bf16[128,1280]{1,0:T(8,128)(2,1)} %get-tuple-element.70.mix, bf16[128,768]{1,0:T(8,128)(2,1)} %bitcast.35, bf16[128,768]{1,0:T(8,128)(2,1)} %get-tuple-element.71.nd, bf16[128,1280]{1,0:T(8,128)(2,1)} %get-tuple-element.72.gq), custom_call_target="tpu_custom_call" | custom-call | flops 4000000000 | bytes 4194304 | tf_op jit(solution)/shard_map/dec_weights/pallas_call | solution.py:113
  182.8 5.5 %all-to-all-start.1 = ((bf16[16,16,2560]{2,1,0:T(8,128)(2,1)}), bf16[16,16,2560]{2,1,0:T(8,128)(2,1)S(1)}, u32[]{:S(2)}, u32[]{:S(2)}) async-start(bf16[16,16,2560]{2,1,0:T(8,128)(2,1)} %bitcast.15), calls=%async_computation.1 | async-start | bytes 2621440 | tf_op jit(solution)/shard_map/all_to_all | solution.py:761
  188.4 8.1 %prepare.1 = (bf16[4,256,1280]{2,1,0:T(8,128)(2,1)}, f32[4,256,128]{2,1,0:T(8,128)}, f32[2,256,1280]{2,1,0:T(8,128)}, bf16[6,256,1280]{2,1,0:T(8,128)(2,1)}, bf16[8,256,256]{2,1,0:T(8,128)(2,1)}) custom-call(f32[5,1280]{1,0:T(8,128)} %lg.13, bf16[4,256,1280]{2,1,0:T(8,128)(2,1)} %get-tuple-element.56.z_h, bf16[2,256,1280]{2,1,0:T(8,128)(2,1)} %get-tuple-element.57.h_h, ...), custom_call_target="tpu_custom_call" | custom-call | flops 5000000000 | bytes 4194304 | tf_op jit(solution)/shard_map/prepare/pallas_call | solution.py:113
  196.5 10.4 %all-to-all-done.1.rcv = bf16[16,16,2560]{2,1,0:T(8,128)(2,1)S(1)} async-done(((bf16[16,16,2560]{2,1,0:T(8,128)(2,1)}), bf16[16,16,2560]{2,1,0:T(8,128)(2,1)S(1)}, u32[]{:S(2)}, u32[]{:S(2)}) %all-to-all-start.1) | async-done | bytes 1310752 | tf_op jit(solution)/shard_map/all_to_all | solution.py:761
  208.0 7.3 %key_value_back.1 = (bf16[16,192,128]{2,1,0:T(8,128)(2,1)}, f32[1,1280]{1,0:T(1,128)}) custom-call(s32[6]{0:T(128)} %stack.38.sc, bf16[16,16,2560]{2,1,0:T(8,128)(2,1)} %copy-done.6, f32[5,1280]{1,0:T(8,128)} %lg.13, bf16[4,256,1280]{2,1,0:T(8,128)(2,1)} %get-tuple-element.59.n_h, f32[4,256,128]{2,1,0:T(8,128)} %get-tuple-element.60.i_h, ...), custom_call_target="tpu_custom_call" | custom-call | flops 100000000 | bytes 4194304 | tf_op jit(solution)/shard_map/key_value_back/pallas_call | solution.py:113
  215.3 17.7 %all_to_all.37.gin = bf16[16,192,128]{2,1,0:T(8,128)(2,1)} all-to-all(bf16[16,192,128]{2,1,0:T(8,128)(2,1)} %get-tuple-element.62), channel_id=1, replica_groups=mesh['y'=4,'core'=2,'x'=4,'z'=4] {'x','z'}, dimensions={0} | all-to-all | bytes 1572864 | tf_op jit(solution)/shard_map/all_to_all | solution.py:761
  233.3 26.2 %lat_backward.1 = (bf16[256,1280]{1,0:T(8,128)(2,1)}, bf16[1280,1024]{1,0:T(8,128)(2,1)}, bf16[256,128]{1,0:T(8,128)(2,1)}, f32[32,128]{1,0:T(8,128)}) custom-call(s32[6]{0:T(128)} %stack.38.sc, bf16[16,192,128]{2,1,0:T(8,128)(2,1)} %all_to_all.37.gin, f32[5,1280]{1,0:T(8,128)} %lg.13, bf16[8,16,128,1280]{3,2,1,0:T(8,128)(2,1)} %bitcast.23, ...), custom_call_target="tpu_custom_call" | custom-call | flops 80000000000 | bytes 4194304 | tf_op jit(solution)/shard_map/lat_backward/pallas_call | solution.py:113
  259.5 10.1 %enc_back.1 = (f32[128,768]{1,0:T(8,128)}, bf16[16,640,128]{2,1,0:T(8,128)(2,1)}) custom-call(s32[6]{0:T(128)} %stack.38.sc, bf16[128,768]{1,0:T(8,128)(2,1)} %bitcast.31, f32[2,768]{1,0:T(2,128)} %bg.5, f32[5,1280]{1,0:T(8,128)} %lg.13, f32[1,768]{1,0:T(1,128)} %get-tuple-element.54.gd, f32[1,1280]{1,0:T(1,128)} %get-tuple-element.61.gc, ...), custom_call_target="tpu_custom_call" | custom-call | flops 3000000000 | bytes 4194304 | tf_op jit(solution)/shard_map/enc_back/pallas_call | solution.py:113
  269.6 5.8 %all-to-all-start.3 = ((bf16[16,640,128]{2,1,0:T(8,128)(2,1)}), bf16[16,640,128]{2,1,0:T(8,128)(2,1)S(1)}, u32[]{:S(2)}, u32[]{:S(2)}) async-start(bf16[16,640,128]{2,1,0:T(8,128)(2,1)} %get-tuple-element.77), calls=%async_computation.4 | async-start | bytes 5242880 | tf_op jit(solution)/shard_map/all_to_all | solution.py:761
  275.4 25.4 %all-gather.5.cloned.1.call-done.nf_h = bf16[2048,768]{1,0:T(8,128)(2,1)} async-done(((bf16[128,768]{1,0:T(8,128)(2,1)}), bf16[2048,768]{1,0:T(8,128)(2,1)}) %all-gather.5.cloned.1.call-update) | async-done | bytes 3145744 | tf_op jit(solution)/shard_map/all_gather | solution.py:902
  300.9 9.6 %all-to-all-done.3.rcv = bf16[16,640,128]{2,1,0:T(8,128)(2,1)S(1)} async-done(((bf16[16,640,128]{2,1,0:T(8,128)(2,1)}), bf16[16,640,128]{2,1,0:T(8,128)(2,1)S(1)}, u32[]{:S(2)}, u32[]{:S(2)}) %all-to-all-start.3) | async-done | bytes 2621472 | tf_op jit(solution)/shard_map/all_to_all | solution.py:761
  311.9 5.8 %tail_one.1 = (bf16[8,352,128]{2,1,0:T(8,128)(2,1)}, f32[48,160]{1,0:T(8,128)}, f32[80,96]{1,0:T(8,128)S(1)}) custom-call(bf16[16,640,128]{2,1,0:T(8,128)(2,1)} %copy-done.5, bf16[2048,768]{1,0:T(8,128)(2,1)} %all-gather.5.cloned.1.call-done.nf_h, bf16[256,1280]{1,0:T(8,128)(2,1)S(1)} %copy-done, f32[5,1280]{1,0:T(8,128)S(1)} %copy-done.1, ...), custom_call_target="tpu_custom_call" | custom-call | bytes 4194304 | tf_op jit(solution)/shard_map/tail_one/pallas_call | solution.py:113
  317.8 4.3 %all-to-all-start.4 = ((bf16[8,352,128]{2,1,0:T(8,128)(2,1)}), bf16[8,352,128]{2,1,0:T(8,128)(2,1)S(1)}, u32[]{:S(2)}, u32[]{:S(2)}) async-start(bf16[8,352,128]{2,1,0:T(8,128)(2,1)} %get-tuple-element.82), calls=%async_computation.5 | async-start | bytes 1441792 | tf_op jit(solution)/shard_map/all_to_all | solution.py:761
  322.1 20.2 %reduce-scatter.5.cloned.1.call-done.pack_h = bf16[160,1024]{1,0:T(8,128)(2,1)} async-done(((bf16[1280,1024]{1,0:T(8,128)(2,1)}), bf16[160,1024]{1,0:T(8,128)(2,1)}) %reduce-scatter.5.cloned.1.call-update) | async-done | bytes 327696 | tf_op jit(solution)/shard_map/reduce_scatter | solution.py:929
  (71 shorter events, 27.9 us)
Async XLA Ops:
  7.2 143.9 %all-gather.3.cloned.1.call-start = ((), (), s32[]{:S(2)}) async-start(), calls=%async_computation.7 | async-start | bytes 42270720 | tf_op jit(solution)/shard_map/all_gather | solution.py:786
  11.0 248.4 %reduce-scatter.3.cloned.1.call-start = ((), (), s32[]{:S(2)}) async-start(), calls=%async_computation.8 | async-start | bytes 4423680 | tf_op jit(solution)/shard_map/reduce_scatter | solution.py:903
  13.5 6.5 %collective-permute-start.2 = (bf16[192,640]{1,0:T(8,128)(2,1)}, bf16[192,640]{1,0:T(8,128)(2,1)S(1)}, u32[]{:S(2)}, u32[]{:S(2)}) collective-permute-start(bf16[192,640]{1,0:T(8,128)(2,1)} %pack_early.1), channel_id=1, source_target_pairs={{0,12},{1,13},{2,14},{3,15},{4,0},{5,1},{6,2},{7,3},{8,4},{9,5},{1... | collective-permute-start | bytes 737288 | tf_op jit(solution)/shard_map/ppermute | solution.py:788
  14.0 9.5 %collective-permute-start.1 = (bf16[192,640]{1,0:T(8,128)(2,1)}, bf16[192,640]{1,0:T(8,128)(2,1)S(1)}, u32[]{:S(2)}, u32[]{:S(2)}) collective-permute-start(bf16[192,640]{1,0:T(8,128)(2,1)} %pack_early.1), channel_id=1, source_target_pairs={{0,8},{1,9},{2,10},{3,11},{4,12},{5,13},{6,14},{7,15},{8,0},{9,1},... | collective-permute-start | bytes 737288 | tf_op jit(solution)/shard_map/ppermute | solution.py:788
  16.5 8.2 %collective-permute-start = (bf16[192,640]{1,0:T(8,128)(2,1)}, bf16[192,640]{1,0:T(8,128)(2,1)S(1)}, u32[]{:S(2)}, u32[]{:S(2)}) collective-permute-start(bf16[192,640]{1,0:T(8,128)(2,1)} %pack_early.1), channel_id=1, source_target_pairs={{0,4},{1,5},{2,6},{3,7},{4,8},{5,9},{6,10},{7,11},{8,12},{9,13},{1... | collective-permute-start | bytes 737288 | tf_op jit(solution)/shard_map/ppermute | solution.py:788
  25.7 46.1 %copy-start.7 = (bf16[4,192,640]{2,1,0:T(8,128)(2,1)}, bf16[4,192,640]{2,1,0:T(8,128)(2,1)S(1)}, u32[]{:S(2)}) copy-start(bf16[4,192,640]{2,1,0:T(8,128)(2,1)S(1)} %pad_maximum_fusion.a0) | copy-start | bytes 2949124
  25.7 17.6 %collective-permute-start.5 = (bf16[4,192,640]{2,1,0:T(8,128)(2,1)S(1)}, bf16[4,192,640]{2,1,0:T(8,128)(2,1)S(1)}, u32[]{:S(2)}, u32[]{:S(2)}) collective-permute-start(bf16[4,192,640]{2,1,0:T(8,128)(2,1)S(1)} %pad_maximum_fusion.a0), channel_id=1, source_target_pairs={{0,3},{1,0},{2,1},{3,2},{4,7},{5,4},{6,5},{7,6},{8,11},{9,8},{10,9... | collective-permute-start | bytes 2949128 | tf_op jit(solution)/shard_map/ppermute | solution.py:789
  29.8 17.3 %collective-permute-start.3 = (bf16[4,192,640]{2,1,0:T(8,128)(2,1)S(1)}, bf16[4,192,640]{2,1,0:T(8,128)(2,1)S(1)}, u32[]{:S(2)}, u32[]{:S(2)}) collective-permute-start(bf16[4,192,640]{2,1,0:T(8,128)(2,1)S(1)} %pad_maximum_fusion.a0), channel_id=1, source_target_pairs={{0,1},{1,2},{2,3},{3,0},{4,5},{5,6},{6,7},{7,4},{8,9},{9,10},{10,1... | collective-permute-start | bytes 2949128 | tf_op jit(solution)/shard_map/ppermute | solution.py:789
  29.9 38.5 %collective-permute-start.7 = (bf16[4,192,640]{2,1,0:T(8,128)(2,1)S(1)}, bf16[4,192,640]{2,1,0:T(8,128)(2,1)S(1)}, u32[]{:S(2)}, u32[]{:S(2)}) collective-permute-start(bf16[4,192,640]{2,1,0:T(8,128)(2,1)S(1)} %pad_maximum_fusion.a0), channel_id=1, source_target_pairs={{0,16},{1,17},{2,18},{3,19},{4,20},{5,21},{6,22},{7,23},{8,24},{9,... | collective-permute-start | bytes 2949128 | tf_op jit(solution)/shard_map/ppermute | solution.py:792
  43.4 20.6 %collective-permute-start.6 = (bf16[2,192,640]{2,1,0:T(8,128)(2,1)S(1)}, bf16[2,192,640]{2,1,0:T(8,128)(2,1)S(1)}, u32[]{:S(2)}, u32[]{:S(2)}) collective-permute-start(bf16[2,192,640]{2,1,0:T(8,128)(2,1)S(1)} %slice.9), channel_id=1, source_target_pairs={{0,3},{1,0},{2,1},{3,2},{4,7},{5,4},{6,5},{7,6},{8,11},{9,8},{10,9... | collective-permute-start | bytes 1474568 | tf_op jit(solution)/shard_map/ppermute | solution.py:790
  47.2 21.2 %collective-permute-start.11 = (bf16[4,192,640]{2,1,0:T(8,128)(2,1)S(1)}, bf16[4,192,640]{2,1,0:T(8,128)(2,1)S(1)}, u32[]{:S(2)}, u32[]{:S(2)}) collective-permute-start(bf16[4,192,640]{2,1,0:T(8,128)(2,1)S(1)} %collective-permute-done.5.a4), channel_id=1, source_target_pairs={{0,16},{1,17},{2,18},{3,19},{4,20},{5,21},{6,22},{7,23},{8,24},{9,... | collective-permute-start | bytes 2949128 | tf_op jit(solution)/shard_map/ppermute | solution.py:792
  47.2 21.1 %collective-permute-start.8 = (bf16[4,192,640]{2,1,0:T(8,128)(2,1)S(1)}, bf16[4,192,640]{2,1,0:T(8,128)(2,1)S(1)}, u32[]{:S(2)}, u32[]{:S(2)}) collective-permute-start(bf16[4,192,640]{2,1,0:T(8,128)(2,1)S(1)} %collective-permute-done.3.a1), channel_id=1, source_target_pairs={{0,16},{1,17},{2,18},{3,19},{4,20},{5,21},{6,22},{7,23},{8,24},{9,... | collective-permute-start | bytes 2949128 | tf_op jit(solution)/shard_map/ppermute | solution.py:792
  47.8 20.5 %collective-permute-start.4 = (bf16[2,192,640]{2,1,0:T(8,128)(2,1)S(1)}, bf16[2,192,640]{2,1,0:T(8,128)(2,1)S(1)}, u32[]{:S(2)}, u32[]{:S(2)}) collective-permute-start(bf16[2,192,640]{2,1,0:T(8,128)(2,1)S(1)} %slice.8), channel_id=1, source_target_pairs={{0,1},{1,2},{2,3},{3,0},{4,5},{5,6},{6,7},{7,4},{8,9},{9,10},{10,1... | collective-permute-start | bytes 1474568 | tf_op jit(solution)/shard_map/ppermute | solution.py:790
  64.0 5.4 %collective-permute-start.10 = (bf16[2,192,640]{2,1,0:T(8,128)(2,1)S(1)}, bf16[2,192,640]{2,1,0:T(8,128)(2,1)S(1)}, u32[]{:S(2)}, u32[]{:S(2)}) collective-permute-start(bf16[2,192,640]{2,1,0:T(8,128)(2,1)S(1)} %collective-permute-done.6.a3), channel_id=1, source_target_pairs={{0,16},{1,17},{2,18},{3,19},{4,20},{5,21},{6,22},{7,23},{8,24},{9,... | collective-permute-start | bytes 1474568 | tf_op jit(solution)/shard_map/ppermute | solution.py:792
  68.3 2.0 collective-permute-start.9
  182.8 24.1 %all-to-all-start.1 = ((bf16[16,16,2560]{2,1,0:T(8,128)(2,1)}), bf16[16,16,2560]{2,1,0:T(8,128)(2,1)S(1)}, u32[]{:S(2)}, u32[]{:S(2)}) async-start(bf16[16,16,2560]{2,1,0:T(8,128)(2,1)} %bitcast.15), calls=%async_computation.1 | async-start | bytes 2621440 | tf_op jit(solution)/shard_map/all_to_all | solution.py:761
  188.3 112.5 %all-gather.5.cloned.1.call-start = ((), (), s32[]{:S(2)}) async-start(), calls=%async_computation.9 | async-start | bytes 3342336 | tf_op jit(solution)/shard_map/all_gather | solution.py:902
  233.1 109.2 %reduce-scatter.5.cloned.1.call-start = ((), (), s32[]{:S(2)}) async-start(), calls=%async_computation.10 | async-start | bytes 2949120 | tf_op jit(solution)/shard_map/reduce_scatter | solution.py:929
  269.6 42.4 %copy-start = (bf16[256,1280]{1,0:T(8,128)(2,1)S(1)}, bf16[256,1280]{1,0:T(8,128)(2,1)}, u32[]{:S(2)}) copy-start(bf16[256,1280]{1,0:T(8,128)(2,1)} %get-tuple-element.73.n0_h) | copy-start | bytes 1966084
  269.6 42.4 %copy-start.1 = (f32[5,1280]{1,0:T(8,128)S(1)}, f32[5,1280]{1,0:T(8,128)}, u32[]{:S(2)}) copy-start(f32[5,1280]{1,0:T(8,128)} %lg.13) | copy-start | bytes 76804
  269.6 42.4 %copy-start.3 = (bf16[256,128]{1,0:T(8,128)(2,1)S(1)}, bf16[256,128]{1,0:T(8,128)(2,1)}, u32[]{:S(2)}) copy-start(bf16[256,128]{1,0:T(8,128)(2,1)} %get-tuple-element.81.g1c) | copy-start | bytes 196612
  269.6 42.3 %copy-start.4 = (f32[32,128]{1,0:T(8,128)S(1)}, f32[32,128]{1,0:T(8,128)}, u32[]{:S(2)}) copy-start(f32[32,128]{1,0:T(8,128)} %get-tuple-element.80.lat_gain) | copy-start | bytes 49156
  269.6 40.8 %all-to-all-start.3 = ((bf16[16,640,128]{2,1,0:T(8,128)(2,1)}), bf16[16,640,128]{2,1,0:T(8,128)(2,1)S(1)}, u32[]{:S(2)}, u32[]{:S(2)}) async-start(bf16[16,640,128]{2,1,0:T(8,128)(2,1)} %get-tuple-element.77), calls=%async_computation.4 | async-start | bytes 5242880 | tf_op jit(solution)/shard_map/all_to_all | solution.py:761
  317.8 24.5 %all-to-all-start.4 = ((bf16[8,352,128]{2,1,0:T(8,128)(2,1)}), bf16[8,352,128]{2,1,0:T(8,128)(2,1)S(1)}, u32[]{:S(2)}, u32[]{:S(2)}) async-start(bf16[8,352,128]{2,1,0:T(8,128)(2,1)} %get-tuple-element.82), calls=%async_computation.5 | async-start | bytes 1441792 | tf_op jit(solution)/shard_map/all_to_all | solution.py:761
  (12 other events, 71.9 us)
Sparse Core Ops, SparseCore 0:
  11.7 139.3 all-gather.2
  183.0 37.0 reduce-scatter.2
  233.2 67.6 all-gather.4
  303.1 39.1 reduce-scatter.4

commit v6 on v5

--- a/solution.py
+++ b/solution.py
@@ -898,7 +898,7 @@
         name="key_value_back",
     )
     gin4 = exchange(kv, BLK)
-    nb, _ = lax.optimization_barrier((nb, gin4))
+    nb, _ = lax.optimization_barrier((nb, gc))
     nf = lax.all_gather(nb, BLK, axis=0, tiled=True)
     dw = lax.psum_scatter(dw.reshape(NI * 1920, 128), BATCH, scatter_dimension=0, tiled=True)
 
@@ -959,7 +959,6 @@
         [((NI, 352, 128), BF, "v"), ((48, 160), F32, "v"), ((80, 96), F32, "v")],
         [(r1, "v"), (nf, "h"), (n0, "h"), (lg, "v"), (lat_gain, "v"), (g1c, "v")],
         [pltpu.VMEM((NJ * N, DI), BF), pltpu.VMEM((R, D), BF), pltpu.VMEM((256, 2048), BF), DMA((2,))],
-        vmem=52,
         name="tail_one",
     )
     r2 = exchange(p2, BATCH)

time: 359 us -> 349 us (0.972)
  the two profiles are of different devices: /device:TPU:2 before, /device:TPU:1 now
where the time goes in v6:
time: 349 us; the launch traced here: 342 us
  waiting for transfers between devices  122 us (35%)
  Pallas kernels  104 us (30%)
  blocking collectives  48.1 us (14%)
  starting transfers between devices  44.3 us (13%)
  between operations  14.9 us (4%)
  local copies, waits for them, and re-layouts  7.6 us (2%)
    pallas_call x12, Pallas kernels, call(): pl.pallas_call(body, out_shape=[jax.ShapeDtypeStruct(s, t) for s, t, _ in...  104 us
    all_to_all x4, waiting for transfers between devices, exchange(): lax.all_to_all(flat, axes, split_axis=0, concat_axis=0, tiled=True)  64.2 us
    all_to_all x1, blocking collectives, exchange(): lax.all_to_all(flat, axes, split_axis=0, concat_axis=0, tiled=True)  24.2 us
    all_to_all x4, starting transfers between devices, exchange(): lax.all_to_all(flat, axes, split_axis=0, concat_axis=0, tiled=True)  23.9 us
    all_gather x1, blocking collectives, shards(): e = lax.all_gather(mine, BLK, axis=0, tiled=True)  23.9 us
    all_gather x1, waiting for transfers between devices, shards(): w = lax.all_gather(wsh, AXES, axis=0, tiled=True).reshape(NI, NJ, ROWS_I, D)  22.8 us
    ppermute x1, waiting for transfers between devices, shards(): lax.ppermute(t1[0:2], AXES, along(1, 1))  13.2 us
    ppermute x2, waiting for transfers between devices, shards(): t1, t3 = (lax.ppermute(s0, AXES, along(1, d)) for d in (1, 3))  11.7 us
  transfers between devices with their start and end apart: 20, of which 12 were waited for; matrix products, arithmetic and copies ran while one was open for 0% of the time, Pallas kernels for 20%

profile of v6, /device:TPU:1, one launch (start us, length us, event | category | flops | bytes accessed | tf_op | source)
XLA Modules:
  0.0 341.9 jit_solution(1593154553210026333)
XLA Ops:
  13.3 4.7 %collective-permute-start.2 = (bf16[192,640]{1,0:T(8,128)(2,1)}, bf16[192,640]{1,0:T(8,128)(2,1)S(1)}, u32[]{:S(2)}, u32[]{:S(2)}) collective-permute-start(bf16[192,640]{1,0:T(8,128)(2,1)} %pack_early.1), channel_id=1, source_target_pairs={{0,12},{1,13},{2,14},{3,15},{4,0},{5,1},{6,2},{7,3},{8,4},{9,5},{1... | collective-permute-start | bytes 737288 | tf_op jit(solution)/shard_map/ppermute | solution.py:788
  18.7 5.4 %collective-permute-done.2 = bf16[192,640]{1,0:T(8,128)(2,1)S(1)} collective-permute-done((bf16[192,640]{1,0:T(8,128)(2,1)}, bf16[192,640]{1,0:T(8,128)(2,1)S(1)}, u32[]{:S(2)}, u32[]{:S(2)}) %collective-permute-start.2) | collective-permute-done | bytes 245792 | tf_op jit(solution)/shard_map/ppermute | solution.py:788
  33.5 11.7 %collective-permute-done.3.a1 = bf16[4,192,640]{2,1,0:T(8,128)(2,1)S(1)} collective-permute-done((bf16[4,192,640]{2,1,0:T(8,128)(2,1)S(1)}, bf16[4,192,640]{2,1,0:T(8,128)(2,1)S(1)}, u32[]{:S(2)}, u32[]{:S(2)}) %collective-permute-start.3) | collective-permute-done | bytes 983072 | tf_op jit(solution)/shard_map/ppermute | solution.py:789
  48.7 13.2 %collective-permute-done.4.a2 = bf16[2,192,640]{2,1,0:T(8,128)(2,1)S(1)} collective-permute-done((bf16[2,192,640]{2,1,0:T(8,128)(2,1)S(1)}, bf16[2,192,640]{2,1,0:T(8,128)(2,1)S(1)}, u32[]{:S(2)}, u32[]{:S(2)}) %collective-permute-start.4) | collective-permute-done | bytes 491552 | tf_op jit(solution)/shard_map/ppermute | solution.py:790
  61.8 6.2 %collective-permute-start.9 = (bf16[2,192,640]{2,1,0:T(8,128)(2,1)S(1)}, bf16[2,192,640]{2,1,0:T(8,128)(2,1)S(1)}, u32[]{:S(2)}, u32[]{:S(2)}) collective-permute-start(bf16[2,192,640]{2,1,0:T(8,128)(2,1)S(1)} %collective-permute-done.4.a2), channel_id=1, source_target_pairs={{0,16},{1,17},{2,18},{3,19},{4,20},{5,21},{6,22},{7,23},{8,24},{9,... | collective-permute-start | bytes 1474568 | tf_op jit(solution)/shard_map/ppermute | solution.py:792
  71.7 10.1 %enc.1 = (bf16[16,192,1280]{2,1,0:T(8,128)(2,1)}, bf16[128,768]{1,0:T(8,128)(2,1)}, bf16[128,1280]{1,0:T(8,128)(2,1)}, bf16[128,1280]{1,0:T(8,128)(2,1)}, bf16[2...) custom-call(s32[6]{0:T(128)} %stack.38.sc, ...), custom_call_target="tpu_custom_call" | custom-call | flops 3000000000 | bytes 4194304 | tf_op jit(solution)/shard_map/enc/pallas_call | solution.py:113
  81.9 24.2 %all_to_all.36.rcv = bf16[16,16,1408]{2,1,0:T(8,128)(2,1)S(1)} all-to-all(bf16[16,16,1408]{2,1,0:T(8,128)(2,1)} %bitcast.26), channel_id=1, replica_groups=mesh['y'=4,'core'=2,'x'=4,'z'=4] {'x','z'}, dimensions={0} | all-to-all | bytes 1441792 | tf_op jit(solution)/shard_map/all_to_all | solution.py:761
  106.6 23.9 %all_gather.9.e_h = bf16[256,1408]{1,0:T(8,128)(2,1)} all-gather(bf16[16,1408]{1,0:T(8,128)(2,1)S(1)} %combine.1), channel_id=1, replica_groups=mesh['y'=4,'core'=2,'x'=4,'z'=4] {'x','z'}, dimensions={0}, use_global_device_ids=true | all-gather | bytes 765952 | tf_op jit(solution)/shard_map/all_gather | solution.py:813
  130.5 22.8 %all-gather.3.cloned.1.call-done = bf16[16384,1280]{1,0:T(8,128)(2,1)} async-done(((bf16[128,1280]{1,0:T(8,128)(2,1)}), bf16[16384,1280]{1,0:T(8,128)(2,1)}) %all-gather.3.cloned.1.call-update) | async-done | bytes 41943056 | tf_op jit(solution)/shard_map/all_gather | solution.py:786
  153.3 27.7 %forward.1 = (bf16[128,768]{1,0:T(8,128)(2,1)}, f32[128,768]{1,0:T(8,128)}, f32[1,768]{1,0:T(1,128)}, bf16[256,2560]{1,0:T(8,128)(2,1)}, bf16[128,1280]{1,0:T(8,...) custom-call(bf16[128,768]{1,0:T(8,128)(2,1)} %bitcast.33, ...), custom_call_target="tpu_custom_call" | custom-call | flops 15000000512 | bytes 4194304 | tf_op jit(solution)/shard_map/forward/pallas_call | solution.py:113
  181.1 4.0 %dec_weights.1 = bf16[8,1920,128]{2,1,0:T(8,128)(2,1)} custom-call(bf16[128,1280]{1,0:T(8,128)(2,1)} %get-tuple-element.70.mix, bf16[128,768]{1,0:T(8,128)(2,1)} %bitcast.35, bf16[128,768]{1,0:T(8,128)(2,1)} %get-tuple-element.71.nd, bf16[128,1280]{1,0:T(8,128)(2,1)} %get-tuple-element.72.gq), custom_call_target="tpu_custom_call" | custom-call | flops 4000000000 | bytes 4194304 | tf_op jit(solution)/shard_map/dec_weights/pallas_call | solution.py:113
  185.1 4.7 %all-to-all-start.1 = ((bf16[16,16,2560]{2,1,0:T(8,128)(2,1)}), bf16[16,16,2560]{2,1,0:T(8,128)(2,1)S(1)}, u32[]{:S(2)}, u32[]{:S(2)}) async-start(bf16[16,16,2560]{2,1,0:T(8,128)(2,1)} %bitcast.15), calls=%async_computation.1 | async-start | bytes 2621440 | tf_op jit(solution)/shard_map/all_to_all | solution.py:761
  189.8 8.1 %prepare.1 = (bf16[4,256,1280]{2,1,0:T(8,128)(2,1)}, f32[4,256,128]{2,1,0:T(8,128)}, f32[2,256,1280]{2,1,0:T(8,128)}, bf16[6,256,1280]{2,1,0:T(8,128)(2,1)}, bf16[8,256,256]{2,1,0:T(8,128)(2,1)}) custom-call(f32[5,1280]{1,0:T(8,128)} %lg.13, bf16[4,256,1280]{2,1,0:T(8,128)(2,1)} %get-tuple-element.56.z_h, bf16[2,256,1280]{2,1,0:T(8,128)(2,1)} %get-tuple-element.57.h_h, ...), custom_call_target="tpu_custom_call" | custom-call | flops 5000000000 | bytes 4194304 | tf_op jit(solution)/shard_map/prepare/pallas_call | solution.py:113
  198.0 11.0 %all-to-all-done.1.rcv = bf16[16,16,2560]{2,1,0:T(8,128)(2,1)S(1)} async-done(((bf16[16,16,2560]{2,1,0:T(8,128)(2,1)}), bf16[16,16,2560]{2,1,0:T(8,128)(2,1)S(1)}, u32[]{:S(2)}, u32[]{:S(2)}) %all-to-all-start.1) | async-done | bytes 1310752 | tf_op jit(solution)/shard_map/all_to_all | solution.py:761
  210.0 7.2 %key_value_back.1 = (bf16[16,192,128]{2,1,0:T(8,128)(2,1)}, f32[1,1280]{1,0:T(1,128)}) custom-call(s32[6]{0:T(128)} %stack.38.sc, bf16[16,16,2560]{2,1,0:T(8,128)(2,1)} %copy-done.6, f32[5,1280]{1,0:T(8,128)} %lg.13, bf16[4,256,1280]{2,1,0:T(8,128)(2,1)} %get-tuple-element.59.n_h, f32[4,256,128]{2,1,0:T(8,128)} %get-tuple-element.60.i_h, ...), custom_call_target="tpu_custom_call" | custom-call | flops 100000000 | bytes 4194304 | tf_op jit(solution)/shard_map/key_value_back/pallas_call | solution.py:113
  217.3 4.3 %all-to-all-start.2 = ((bf16[16,192,128]{2,1,0:T(8,128)(2,1)}), bf16[16,192,128]{2,1,0:T(8,128)(2,1)S(1)}, u32[]{:S(2)}, u32[]{:S(2)}) async-start(bf16[16,192,128]{2,1,0:T(8,128)(2,1)} %get-tuple-element.62), calls=%async_computation.2 | async-start | bytes 1572864 | tf_op jit(solution)/shard_map/all_to_all | solution.py:761
  222.5 11.0 %all-to-all-done.2.gin = bf16[16,192,128]{2,1,0:T(8,128)(2,1)S(1)} async-done(((bf16[16,192,128]{2,1,0:T(8,128)(2,1)}), bf16[16,192,128]{2,1,0:T(8,128)(2,1)S(1)}, u32[]{:S(2)}, u32[]{:S(2)}) %all-to-all-start.2) | async-done | bytes 786464 | tf_op jit(solution)/shard_map/all_to_all | solution.py:761
  234.5 26.2 %lat_backward.1 = (bf16[256,1280]{1,0:T(8,128)(2,1)}, bf16[1280,1024]{1,0:T(8,128)(2,1)}, bf16[256,128]{1,0:T(8,128)(2,1)}, f32[32,128]{1,0:T(8,128)}) custom-call(s32[6]{0:T(128)} %stack.38.sc, bf16[16,192,128]{2,1,0:T(8,128)(2,1)} %copy-done.8, f32[5,1280]{1,0:T(8,128)} %lg.13, bf16[8,16,128,1280]{3,2,1,0:T(8,128)(2,1)} %bitcast.23, ...), custom_call_target="tpu_custom_call" | custom-call | flops 80000000000 | bytes 4194304 | tf_op jit(solution)/shard_map/lat_backward/pallas_call | solution.py:113
  260.7 10.1 %enc_back.1 = (f32[128,768]{1,0:T(8,128)}, bf16[16,640,128]{2,1,0:T(8,128)(2,1)}) custom-call(s32[6]{0:T(128)} %stack.38.sc, bf16[128,768]{1,0:T(8,128)(2,1)} %bitcast.31, f32[2,768]{1,0:T(2,128)} %bg.5, f32[5,1280]{1,0:T(8,128)} %lg.13, f32[1,768]{1,0:T(1,128)} %get-tuple-element.54.gd, f32[1,1280]{1,0:T(1,128)} %get-tuple-element.61.gc, ...), custom_call_target="tpu_custom_call" | custom-call | flops 3000000000 | bytes 4194304 | tf_op jit(solution)/shard_map/enc_back/pallas_call | solution.py:113
  270.9 4.5 %all-to-all-start.3 = ((bf16[16,640,128]{2,1,0:T(8,128)(2,1)}), bf16[16,640,128]{2,1,0:T(8,128)(2,1)S(1)}, u32[]{:S(2)}, u32[]{:S(2)}) async-start(bf16[16,640,128]{2,1,0:T(8,128)(2,1)} %get-tuple-element.77), calls=%async_computation.4 | async-start | bytes 5242880 | tf_op jit(solution)/shard_map/all_to_all | solution.py:761
  275.4 30.5 %all-to-all-done.3.rcv = bf16[16,640,128]{2,1,0:T(8,128)(2,1)S(1)} async-done(((bf16[16,640,128]{2,1,0:T(8,128)(2,1)}), bf16[16,640,128]{2,1,0:T(8,128)(2,1)S(1)}, u32[]{:S(2)}, u32[]{:S(2)}) %all-to-all-start.3) | async-done | bytes 2621472 | tf_op jit(solution)/shard_map/all_to_all | solution.py:761
  305.9 3.9 %tail_one.1 = (bf16[8,352,128]{2,1,0:T(8,128)(2,1)S(1)}, f32[48,160]{1,0:T(8,128)}, f32[80,96]{1,0:T(8,128)S(1)}) custom-call(bf16[16,640,128]{2,1,0:T(8,128)(2,1)S(1)} %all-to-all-done.3.rcv, bf16[2048,768]{1,0:T(8,128)(2,1)} %all-gather.5.cloned.1.call-done.nf_h, bf16[256,1280]{1,0:T(8,128)(2,1)S(1)} %copy-done, f32[5,1280]{1,0:T(8,128)S(1)} %copy-done.2, ...), custom_call_target="tpu_custom_call" | custom-call | bytes 4194304 | tf_op jit(solution)/shard_map/tail_one/pallas_call | solution.py:113
  310.6 10.4 %all-to-all-start.4 = ((bf16[8,352,128]{2,1,0:T(8,128)(2,1)}), bf16[8,352,128]{2,1,0:T(8,128)(2,1)S(1)}, u32[]{:S(2)}, u32[]{:S(2)}) async-start(bf16[8,352,128]{2,1,0:T(8,128)(2,1)} %copy-done.1), calls=%async_computation.5 | async-start | bytes 1441792 | tf_op jit(solution)/shard_map/all_to_all | solution.py:761
  321.0 11.6 %all-to-all-done.4.rcv = bf16[8,352,128]{2,1,0:T(8,128)(2,1)S(1)} async-done(((bf16[8,352,128]{2,1,0:T(8,128)(2,1)}), bf16[8,352,128]{2,1,0:T(8,128)(2,1)S(1)}, u32[]{:S(2)}, u32[]{:S(2)}) %all-to-all-start.4) | async-done | bytes 720928 | tf_op jit(solution)/shard_map/all_to_all | solution.py:761
  (74 shorter events, 29.5 us)
Async XLA Ops:
  7.2 146.1 %all-gather.3.cloned.1.call-start = ((), (), s32[]{:S(2)}) async-start(), calls=%async_computation.7 | async-start | bytes 42270720 | tf_op jit(solution)/shard_map/all_gather | solution.py:786
  10.9 249.8 %reduce-scatter.3.cloned.1.call-start = ((), (), s32[]{:S(2)}) async-start(), calls=%async_computation.8 | async-start | bytes 4423680 | tf_op jit(solution)/shard_map/reduce_scatter | solution.py:903
  13.3 10.7 %collective-permute-start.2 = (bf16[192,640]{1,0:T(8,128)(2,1)}, bf16[192,640]{1,0:T(8,128)(2,1)S(1)}, u32[]{:S(2)}, u32[]{:S(2)}) collective-permute-start(bf16[192,640]{1,0:T(8,128)(2,1)} %pack_early.1), channel_id=1, source_target_pairs={{0,12},{1,13},{2,14},{3,15},{4,0},{5,1},{6,2},{7,3},{8,4},{9,5},{1... | collective-permute-start | bytes 737288 | tf_op jit(solution)/shard_map/ppermute | solution.py:788
  18.0 7.1 %collective-permute-start.1 = (bf16[192,640]{1,0:T(8,128)(2,1)}, bf16[192,640]{1,0:T(8,128)(2,1)S(1)}, u32[]{:S(2)}, u32[]{:S(2)}) collective-permute-start(bf16[192,640]{1,0:T(8,128)(2,1)} %pack_early.1), channel_id=1, source_target_pairs={{0,8},{1,9},{2,10},{3,11},{4,12},{5,13},{6,14},{7,15},{8,0},{9,1},... | collective-permute-start | bytes 737288 | tf_op jit(solution)/shard_map/ppermute | solution.py:788
  18.0 9.4 %collective-permute-start = (bf16[192,640]{1,0:T(8,128)(2,1)}, bf16[192,640]{1,0:T(8,128)(2,1)S(1)}, u32[]{:S(2)}, u32[]{:S(2)}) collective-permute-start(bf16[192,640]{1,0:T(8,128)(2,1)} %pack_early.1), channel_id=1, source_target_pairs={{0,4},{1,5},{2,6},{3,7},{4,8},{5,9},{6,10},{7,11},{8,12},{9,13},{1... | collective-permute-start | bytes 737288 | tf_op jit(solution)/shard_map/ppermute | solution.py:788
  28.5 43.2 %copy-start.7 = (bf16[4,192,640]{2,1,0:T(8,128)(2,1)}, bf16[4,192,640]{2,1,0:T(8,128)(2,1)S(1)}, u32[]{:S(2)}) copy-start(bf16[4,192,640]{2,1,0:T(8,128)(2,1)S(1)} %pad_maximum_fusion.a0) | copy-start | bytes 2949124
  28.5 16.7 %collective-permute-start.3 = (bf16[4,192,640]{2,1,0:T(8,128)(2,1)S(1)}, bf16[4,192,640]{2,1,0:T(8,128)(2,1)S(1)}, u32[]{:S(2)}, u32[]{:S(2)}) collective-permute-start(bf16[4,192,640]{2,1,0:T(8,128)(2,1)S(1)} %pad_maximum_fusion.a0), channel_id=1, source_target_pairs={{0,1},{1,2},{2,3},{3,0},{4,5},{5,6},{6,7},{7,4},{8,9},{9,10},{10,1... | collective-permute-start | bytes 2949128 | tf_op jit(solution)/shard_map/ppermute | solution.py:789
  29.5 18.4 %collective-permute-start.5 = (bf16[4,192,640]{2,1,0:T(8,128)(2,1)S(1)}, bf16[4,192,640]{2,1,0:T(8,128)(2,1)S(1)}, u32[]{:S(2)}, u32[]{:S(2)}) collective-permute-start(bf16[4,192,640]{2,1,0:T(8,128)(2,1)S(1)} %pad_maximum_fusion.a0), channel_id=1, source_target_pairs={{0,3},{1,0},{2,1},{3,2},{4,7},{5,4},{6,5},{7,6},{8,11},{9,8},{10,9... | collective-permute-start | bytes 2949128 | tf_op jit(solution)/shard_map/ppermute | solution.py:789
  31.2 36.9 %collective-permute-start.7 = (bf16[4,192,640]{2,1,0:T(8,128)(2,1)S(1)}, bf16[4,192,640]{2,1,0:T(8,128)(2,1)S(1)}, u32[]{:S(2)}, u32[]{:S(2)}) collective-permute-start(bf16[4,192,640]{2,1,0:T(8,128)(2,1)S(1)} %pad_maximum_fusion.a0), channel_id=1, source_target_pairs={{0,16},{1,17},{2,18},{3,19},{4,20},{5,21},{6,22},{7,23},{8,24},{9,... | collective-permute-start | bytes 2949128 | tf_op jit(solution)/shard_map/ppermute | solution.py:792
  45.3 16.6 %collective-permute-start.4 = (bf16[2,192,640]{2,1,0:T(8,128)(2,1)S(1)}, bf16[2,192,640]{2,1,0:T(8,128)(2,1)S(1)}, u32[]{:S(2)}, u32[]{:S(2)}) collective-permute-start(bf16[2,192,640]{2,1,0:T(8,128)(2,1)S(1)} %slice.8), channel_id=1, source_target_pairs={{0,1},{1,2},{2,3},{3,0},{4,5},{5,6},{6,7},{7,4},{8,9},{9,10},{10,1... | collective-permute-start | bytes 1474568 | tf_op jit(solution)/shard_map/ppermute | solution.py:790
  45.4 22.8 %collective-permute-start.8 = (bf16[4,192,640]{2,1,0:T(8,128)(2,1)S(1)}, bf16[4,192,640]{2,1,0:T(8,128)(2,1)S(1)}, u32[]{:S(2)}, u32[]{:S(2)}) collective-permute-start(bf16[4,192,640]{2,1,0:T(8,128)(2,1)S(1)} %collective-permute-done.3.a1), channel_id=1, source_target_pairs={{0,16},{1,17},{2,18},{3,19},{4,20},{5,21},{6,22},{7,23},{8,24},{9,... | collective-permute-start | bytes 2949128 | tf_op jit(solution)/shard_map/ppermute | solution.py:792
  47.9 20.2 %collective-permute-start.11 = (bf16[4,192,640]{2,1,0:T(8,128)(2,1)S(1)}, bf16[4,192,640]{2,1,0:T(8,128)(2,1)S(1)}, u32[]{:S(2)}, u32[]{:S(2)}) collective-permute-start(bf16[4,192,640]{2,1,0:T(8,128)(2,1)S(1)} %collective-permute-done.5.a4), channel_id=1, source_target_pairs={{0,16},{1,17},{2,18},{3,19},{4,20},{5,21},{6,22},{7,23},{8,24},{9,... | collective-permute-start | bytes 2949128 | tf_op jit(solution)/shard_map/ppermute | solution.py:792
  48.0 20.0 %collective-permute-start.6 = (bf16[2,192,640]{2,1,0:T(8,128)(2,1)S(1)}, bf16[2,192,640]{2,1,0:T(8,128)(2,1)S(1)}, u32[]{:S(2)}, u32[]{:S(2)}) collective-permute-start(bf16[2,192,640]{2,1,0:T(8,128)(2,1)S(1)} %slice.9), channel_id=1, source_target_pairs={{0,3},{1,0},{2,1},{3,2},{4,7},{5,4},{6,5},{7,6},{8,11},{9,8},{10,9... | collective-permute-start | bytes 1474568 | tf_op jit(solution)/shard_map/ppermute | solution.py:790
  61.8 7.7 %collective-permute-start.9 = (bf16[2,192,640]{2,1,0:T(8,128)(2,1)S(1)}, bf16[2,192,640]{2,1,0:T(8,128)(2,1)S(1)}, u32[]{:S(2)}, u32[]{:S(2)}) collective-permute-start(bf16[2,192,640]{2,1,0:T(8,128)(2,1)S(1)} %collective-permute-done.4.a2), channel_id=1, source_target_pairs={{0,16},{1,17},{2,18},{3,19},{4,20},{5,21},{6,22},{7,23},{8,24},{9,... | collective-permute-start | bytes 1474568 | tf_op jit(solution)/shard_map/ppermute | solution.py:792
  68.0 2.2 collective-permute-start.10
  185.1 23.9 %all-to-all-start.1 = ((bf16[16,16,2560]{2,1,0:T(8,128)(2,1)}), bf16[16,16,2560]{2,1,0:T(8,128)(2,1)S(1)}, u32[]{:S(2)}, u32[]{:S(2)}) async-start(bf16[16,16,2560]{2,1,0:T(8,128)(2,1)} %bitcast.15), calls=%async_computation.1 | async-start | bytes 2621440 | tf_op jit(solution)/shard_map/all_to_all | solution.py:761
  217.3 16.3 %all-to-all-start.2 = ((bf16[16,192,128]{2,1,0:T(8,128)(2,1)}), bf16[16,192,128]{2,1,0:T(8,128)(2,1)S(1)}, u32[]{:S(2)}, u32[]{:S(2)}) async-start(bf16[16,192,128]{2,1,0:T(8,128)(2,1)} %get-tuple-element.62), calls=%async_computation.2 | async-start | bytes 1572864 | tf_op jit(solution)/shard_map/all_to_all | solution.py:761
  221.6 53.8 %all-gather.5.cloned.1.call-start = ((), (), s32[]{:S(2)}) async-start(), calls=%async_computation.9 | async-start | bytes 3342336 | tf_op jit(solution)/shard_map/all_gather | solution.py:902
  222.3 98.7 %reduce-scatter.5.cloned.1.call-start = ((), (), s32[]{:S(2)}) async-start(), calls=%async_computation.10 | async-start | bytes 2949120 | tf_op jit(solution)/shard_map/reduce_scatter | solution.py:929
  270.8 35.1 %copy-start = (bf16[256,1280]{1,0:T(8,128)(2,1)S(1)}, bf16[256,1280]{1,0:T(8,128)(2,1)}, u32[]{:S(2)}) copy-start(bf16[256,1280]{1,0:T(8,128)(2,1)} %get-tuple-element.73.n0_h) | copy-start | bytes 1966084
  270.8 35.1 %copy-start.2 = (f32[5,1280]{1,0:T(8,128)S(1)}, f32[5,1280]{1,0:T(8,128)}, u32[]{:S(2)}) copy-start(f32[5,1280]{1,0:T(8,128)} %lg.13) | copy-start | bytes 76804
  270.8 35.1 %copy-start.4 = (bf16[256,128]{1,0:T(8,128)(2,1)S(1)}, bf16[256,128]{1,0:T(8,128)(2,1)}, u32[]{:S(2)}) copy-start(bf16[256,128]{1,0:T(8,128)(2,1)} %get-tuple-element.81.g1c) | copy-start | bytes 196612
  270.9 35.0 %all-to-all-start.3 = ((bf16[16,640,128]{2,1,0:T(8,128)(2,1)}), bf16[16,640,128]{2,1,0:T(8,128)(2,1)S(1)}, u32[]{:S(2)}, u32[]{:S(2)}) async-start(bf16[16,640,128]{2,1,0:T(8,128)(2,1)} %get-tuple-element.77), calls=%async_computation.4 | async-start | bytes 5242880 | tf_op jit(solution)/shard_map/all_to_all | solution.py:761
  310.6 22.0 %all-to-all-start.4 = ((bf16[8,352,128]{2,1,0:T(8,128)(2,1)}), bf16[8,352,128]{2,1,0:T(8,128)(2,1)S(1)}, u32[]{:S(2)}, u32[]{:S(2)}) async-start(bf16[8,352,128]{2,1,0:T(8,128)(2,1)} %copy-done.1), calls=%async_computation.5 | async-start | bytes 1441792 | tf_op jit(solution)/shard_map/all_to_all | solution.py:761
  (14 other events, 107.0 us)
Sparse Core Ops, SparseCore 0:
  11.7 141.5 all-gather.2
  185.2 33.5 reduce-scatter.2
  224.6 50.6 all-gather.4
  277.6 31.3 reduce-scatter.4
